TPU v7x, 128 devices: a whole 4x4x4 slice. The times are simulated.
128 devices in a mesh: row: 16 (over x_lo, y, core), col: 8 (over x_hi, z).
Axes of the slice: x: 4 (x_hi: 2, x_lo: 2; x = x_hi * 2 + x_lo), y: 4, z: 4, core: 2. Of those that a mesh axis runs over, the one named last changes fastest.
Arguments:
- alignment_tensor: bfloat16 [256, 1024, 256], P(None, ('row', 'col')), may hold values from -6 to 6
- amino_exists_flags: int32 [256, 1024], P(None, ('row', 'col')), may hold values 0 or 1
- chain_exists_flags: int32 [256], replicated, may hold values 0 or 1
- chosen_slab_number: int32 [1], replicated, may hold values from 0 to 15
- duo_tensor: bfloat16 [1024, 1024, 128], P('row', 'col'), may hold values from -6 to 6
- duo_offset_matrix: bfloat16 [128, 8], replicated, may hold values from -0.5 to 0.5
- asking_matrix: bfloat16 [256, 256], replicated
- lookup_matrix: bfloat16 [256, 256], replicated
- content_matrix: bfloat16 [256, 256], replicated, may hold values from -0.375 to 0.375
- sigmoid_matrix: bfloat16 [256, 256], replicated, may hold values from -0.375 to 0.375
- final_projection_matrix: bfloat16 [256, 256], replicated, may hold values from -0.375 to 0.375
- first_factor_matrix: bfloat16 [256, 32], replicated, may hold values from -0.375 to 0.375
- second_factor_matrix: bfloat16 [256, 32], replicated, may hold values from -0.375 to 0.375
- product_to_duo_matrix: bfloat16 [1024, 128], replicated, may hold values from -3 to 3
Outputs:
- alignment_reweighted: bfloat16 [256, 1024, 256], P(None, ('row', 'col'))
- product_average: bfloat16 [64, 1024, 128], P(None, ('row', 'col'))
All inputs are finite; a program needn't handle non-finite values. No bound on the sum of `amino_exists_flags` on one device may be relied on, other than what follows from the above.
Results may differ from a plain program's by a relative error of at most 0.017.
Values may be sent and summed in bfloat16 or wider, within the bound.
No kernel may reach another device: no remote copies, remote signals or barrier semaphores. Data moves between devices by JAX's collectives and lax.ppermute only.
A program may use at most 128 MiB of HBM per device.

v0:
```python
import jax
import jax.numpy as jnp
from jax import lax
from jax.sharding import PartitionSpec as P

ALIGN_FEATURES = 256
DUO_FEATURES = 128
SCORE_GROUPS = 8
GROUP_FEATURES = 32
PROJECTED_WIDTH = 32


def broadcast(block, axis, source):
    block = jnp.where(lax.axis_index(axis) == source, block, jnp.zeros_like(block))
    return lax.psum(block, axis)


def standardize_features(x):
    mean = jnp.mean(x, axis=-1, keepdims=True)
    centred = x - mean
    var = jnp.mean(centred * centred, axis=-1, keepdims=True)
    return centred * lax.rsqrt(var + 1e-05)


def attend(asking_vector, key, content_vector, bias, key_mask):
    count, heads, width, length = asking_vector.shape
    scale = 1.0 / width**0.5
    pairs = count * heads // 2
    flat_q = asking_vector.reshape(pairs, 2, width, length)
    flat_k = key.reshape(pairs, 2, width, length)
    flat_v = content_vector.reshape(pairs, 2, width, length)
    mask_items = jnp.broadcast_to(key_mask[:, None, :], (count, heads, length)).reshape(
        pairs, 2, length
    )
    item_heads = (jnp.arange(pairs * 2, dtype=jnp.int32) % heads).reshape(pairs, 2)

    def one_pair(items):
        q_two, k_two, v_two, m_two, h_two = items
        bias_two = jnp.take(bias, h_two, axis=0).astype(jnp.float32)
        score = (
            jnp.einsum("ndi,ndj->nij", q_two, k_two, preferred_element_type=jnp.float32) * scale
            + bias_two
        )
        score = jnp.where(m_two[:, None, :] > 0, score, -1000000000.0)
        probs = jax.nn.softmax(score, axis=-1).astype(jnp.bfloat16)
        out = jnp.einsum("nij,ndj->ndi", probs, v_two, preferred_element_type=jnp.float32)
        return out.astype(jnp.bfloat16)

    result = lax.map(one_pair, (flat_q, flat_k, flat_v, mask_items, item_heads))
    return result.reshape(count, heads, width, length)


def per_device(
    alignment_tensor,
    amino_exists_flags,
    chain_exists_flags,
    chosen_slab_number,
    duo_tensor,
    duo_offset_matrix,
    asking_matrix,
    lookup_matrix,
    content_matrix,
    sigmoid_matrix,
    final_projection_matrix,
    first_factor_matrix,
    second_factor_matrix,
    product_to_duo_matrix,
):
    chain_count_sum = alignment_tensor.shape[0]
    device_amino_count = alignment_tensor.shape[1]
    normed_pair = standardize_features(duo_tensor.astype(jnp.float32)).astype(jnp.bfloat16)
    tile = jnp.einsum(
        "ijc,ch->hij", normed_pair, duo_offset_matrix, preferred_element_type=jnp.float32
    ).astype(jnp.bfloat16)
    transferred_piece, moved_mask = (
        lax.all_to_all(alignment_tensor, ("row", "col"), split_axis=0, concat_axis=1, tiled=True),
        lax.all_to_all(
            amino_exists_flags.astype(jnp.bfloat16),
            ("row", "col"),
            split_axis=0,
            concat_axis=1,
            tiled=True,
        ),
    )
    wide = lax.all_gather(tile, "col", axis=2, tiled=True)
    full_bias = lax.all_gather(wide, "row", axis=1, tiled=True)
    standardized_alignment = standardize_features(transferred_piece.astype(jnp.float32)).astype(
        jnp.bfloat16
    )
    asking_vector = jnp.einsum(
        "src,chd->shdr",
        standardized_alignment,
        asking_matrix.reshape(ALIGN_FEATURES, SCORE_GROUPS, GROUP_FEATURES),
        preferred_element_type=jnp.float32,
    ).astype(jnp.bfloat16)
    key = jnp.einsum(
        "src,chd->shdr",
        standardized_alignment,
        lookup_matrix.reshape(ALIGN_FEATURES, SCORE_GROUPS, GROUP_FEATURES),
        preferred_element_type=jnp.float32,
    ).astype(jnp.bfloat16)
    content_vector = jnp.einsum(
        "src,chd->shdr",
        standardized_alignment,
        content_matrix.reshape(ALIGN_FEATURES, SCORE_GROUPS, GROUP_FEATURES),
        preferred_element_type=jnp.float32,
    ).astype(jnp.bfloat16)
    sigmoid_argument = jnp.einsum(
        "src,chd->shdr",
        standardized_alignment,
        sigmoid_matrix.reshape(ALIGN_FEATURES, SCORE_GROUPS, GROUP_FEATURES),
        preferred_element_type=jnp.float32,
    )
    probability_combined = attend(asking_vector, key, content_vector, full_bias, moved_mask)
    scaled_heads = (
        jax.nn.sigmoid(sigmoid_argument) * probability_combined.astype(jnp.float32)
    ).astype(jnp.bfloat16)
    duo_increment = jnp.einsum(
        "shdr,hdc->src",
        scaled_heads,
        final_projection_matrix.reshape(SCORE_GROUPS, GROUP_FEATURES, ALIGN_FEATURES),
        preferred_element_type=jnp.float32,
    )
    fresh_sequence = (transferred_piece.astype(jnp.float32) + duo_increment).astype(jnp.bfloat16)
    alignment_reweighted = lax.all_to_all(
        fresh_sequence, ("row", "col"), split_axis=1, concat_axis=0, tiled=True
    )
    standardized_newer = standardize_features(alignment_reweighted.astype(jnp.float32)).astype(
        jnp.bfloat16
    )
    retained_flags = chain_exists_flags.astype(jnp.float32)[:, None, None]
    first_factor = (
        jnp.einsum(
            "src,ca->sra",
            standardized_newer,
            first_factor_matrix,
            preferred_element_type=jnp.float32,
        )
        * retained_flags
    ).astype(jnp.bfloat16)
    second_factor = (
        jnp.einsum(
            "src,ca->sra",
            standardized_newer,
            second_factor_matrix,
            preferred_element_type=jnp.float32,
        )
        * retained_flags
    ).astype(jnp.bfloat16)
    row_block = lax.all_gather(first_factor, "col", axis=1, tiled=True)
    slab_left = broadcast(row_block, "row", chosen_slab_number[0])
    slab_rows = slab_left.shape[1]
    tensor_product = (
        jnp.einsum("dnw,dgr->ngwr", slab_left, second_factor, preferred_element_type=jnp.float32)
        / chain_count_sum
    )
    tensor_product = tensor_product.astype(jnp.bfloat16).reshape(
        slab_rows * device_amino_count, PROJECTED_WIDTH * PROJECTED_WIDTH
    )
    product_average = (
        jnp.dot(tensor_product, product_to_duo_matrix, preferred_element_type=jnp.float32)
        .reshape(slab_rows, device_amino_count, DUO_FEATURES)
        .astype(jnp.bfloat16)
    )
    return (alignment_reweighted, product_average)


def solution(mesh):
    placed = (
        P(None, ("row", "col"), None),
        P(None, ("row", "col")),
        P(),
        P(),
        P("row", "col", None),
        P(),
        P(),
        P(),
        P(),
        P(),
        P(),
        P(),
        P(),
        P(),
    )
    return jax.shard_map(
        per_device,
        mesh=mesh,
        in_specs=placed,
        out_specs=(P(None, ("row", "col"), None), P(None, ("row", "col"), None)),
        check_vma=False,
    )
```

profile of v0, /device:TPU:1, one launch (start us, length us, event | category | flops | bytes accessed | tf_op | source)
XLA Modules:
  0.0 797.6 jit_solution(5378378450601491090)
XLA Ops:
  12.0 3.5 fusion.56
  15.7 47.9 %all-gather.4.cloned.1.call-done = bf16[8,64,1024]{2,0,1:T(8,128)(2,1)} async-done(((bf16[8,64,128]{2,0,1:T(8,128)(2,1)}), bf16[8,64,1024]{2,0,1:T(8,128)(2,1)}) %all-gather.4.cloned.1.call-update) | async-done | bytes 1048592 | tf_op jit(solution)/shard_map/all_gather | solution.py:85
  63.8 16.4 %all_to_all.43 = bf16[128,2,8]{2,1,0:T(2,128)(2,1)S(1)} all-to-all(bf16[128,2,8]{2,1,0:T(2,128)(2,1)S(1)} %bitcast.180), channel_id=1, replica_groups=mesh['row'=16,'col'=8] {'row','col'}, dimensions={0} | all-to-all | bytes 8192 | tf_op jit(solution)/shard_map/all_to_all | solution.py:77
  80.2 4.6 all-to-all-start
  86.1 24.9 %all-to-all-done = bf16[256,8,256]{2,1,0:T(8,128)(2,1)S(1)} async-done(((bf16[256,8,256]{2,1,0:T(8,128)(2,1)}), bf16[256,8,256]{2,1,0:T(8,128)(2,1)S(1)}, u32[]{:S(2)}, u32[]{:S(2)}) %all-to-all-start) | async-done | bytes 1048608 | tf_op jit(solution)/shard_map/all_to_all | solution.py:76
  118.3 49.4 %all-gather.6.cloned.1.call-done = bf16[8,1024,1024]{2,0,1:T(8,128)(2,1)} async-done(((bf16[8,64,1024]{2,0,1:T(8,128)(2,1)}), bf16[8,1024,1024]{2,0,1:T(8,128)(2,1)}) %all-gather.6.cloned.1.call-update) | async-done | bytes 16777232 | tf_op jit(solution)/shard_map/all_gather | solution.py:86
  167.7 18.6 %copy.110 = bf16[8,1024,1024]{2,1,0:T(8,128)(2,1)} copy(bf16[8,1024,1024]{2,0,1:T(8,128)(2,1)} %all-gather.6.cloned.1.call-done) | data formatting | bytes 33554432 | tf_op jit(solution)/shard_map/while | solution.py:49
  187.0 352.9 %while.10 = (s32[]{:T(128)}, bf16[8,2,32,1024]{3,2,1,0:T(8,128)(2,1)}, bf16[8,2,32,1024]{3,2,1,0:T(8,128)(2,1)}, bf16[8,2,1024]{2,1,0:T(2,128)(2,1)}, bf16[8,2,3...) while((s32[]{:T(128)}, ...), condition=%wide.region_7.8_spmd, body=%wide.region_4.7_spmd.sunk | while | flops 450960384 | bytes 84706488 | solution.py:49
  187.0 11.7 %fusion.102 = (bf16[8,512,1024]{2,1,0:T(8,128)(2,1)}, bf16[8,512,1024]{2,1,0:T(8,128)(2,1)}) fusion(bf16[8,1024,1024]{2,1,0:T(8,128)(2,1)} %get-tuple-element.197), kind=kLoop, calls=%fused_computation.98.clone.1 | loop fusion | bytes 33554432 | tf_op jit(solution)/shard_map/while/body/eval_jaxpr/jit(_take)/gather | solution.py:39
  198.8 4.1 gather_fusion
  205.4 4.1 gather_fusion.1
  212.8 5.8 fusion.104
  218.6 5.6 fusion.105
  224.3 6.9 fusion.106
  231.2 11.6 %fusion.102 = (bf16[8,512,1024]{2,1,0:T(8,128)(2,1)}, bf16[8,512,1024]{2,1,0:T(8,128)(2,1)}) fusion(bf16[8,1024,1024]{2,1,0:T(8,128)(2,1)} %get-tuple-element.197), kind=kLoop, calls=%fused_computation.98.clone.1 | loop fusion | bytes 33554432 | tf_op jit(solution)/shard_map/while/body/eval_jaxpr/jit(_take)/gather | solution.py:39
  242.8 4.1 gather_fusion
  249.5 4.1 gather_fusion.1
  256.9 5.9 fusion.104
  262.7 5.6 fusion.105
  268.4 6.9 fusion.106
  275.3 11.6 %fusion.102 = (bf16[8,512,1024]{2,1,0:T(8,128)(2,1)}, bf16[8,512,1024]{2,1,0:T(8,128)(2,1)}) fusion(bf16[8,1024,1024]{2,1,0:T(8,128)(2,1)} %get-tuple-element.197), kind=kLoop, calls=%fused_computation.98.clone.1 | loop fusion | bytes 33554432 | tf_op jit(solution)/shard_map/while/body/eval_jaxpr/jit(_take)/gather | solution.py:39
  287.0 4.1 gather_fusion
  293.6 4.1 gather_fusion.1
  301.0 5.8 fusion.104
  306.8 5.6 fusion.105
  312.4 6.9 fusion.106
  319.4 11.6 %fusion.102 = (bf16[8,512,1024]{2,1,0:T(8,128)(2,1)}, bf16[8,512,1024]{2,1,0:T(8,128)(2,1)}) fusion(bf16[8,1024,1024]{2,1,0:T(8,128)(2,1)} %get-tuple-element.197), kind=kLoop, calls=%fused_computation.98.clone.1 | loop fusion | bytes 33554432 | tf_op jit(solution)/shard_map/while/body/eval_jaxpr/jit(_take)/gather | solution.py:39
  331.0 4.1 gather_fusion
  337.7 4.1 gather_fusion.1
  345.1 5.8 fusion.104
  350.9 5.6 fusion.105
  356.5 6.9 fusion.106
  363.5 11.6 %fusion.102 = (bf16[8,512,1024]{2,1,0:T(8,128)(2,1)}, bf16[8,512,1024]{2,1,0:T(8,128)(2,1)}) fusion(bf16[8,1024,1024]{2,1,0:T(8,128)(2,1)} %get-tuple-element.197), kind=kLoop, calls=%fused_computation.98.clone.1 | loop fusion | bytes 33554432 | tf_op jit(solution)/shard_map/while/body/eval_jaxpr/jit(_take)/gather | solution.py:39
  375.1 4.1 gather_fusion
  381.8 4.1 gather_fusion.1
  389.1 5.8 fusion.104
  395.0 5.6 fusion.105
  400.6 6.9 fusion.106
  407.6 11.6 %fusion.102 = (bf16[8,512,1024]{2,1,0:T(8,128)(2,1)}, bf16[8,512,1024]{2,1,0:T(8,128)(2,1)}) fusion(bf16[8,1024,1024]{2,1,0:T(8,128)(2,1)} %get-tuple-element.197), kind=kLoop, calls=%fused_computation.98.clone.1 | loop fusion | bytes 33554432 | tf_op jit(solution)/shard_map/while/body/eval_jaxpr/jit(_take)/gather | solution.py:39
  419.2 4.1 gather_fusion
  425.9 4.1 gather_fusion.1
  433.2 5.8 fusion.104
  439.1 5.6 fusion.105
  444.7 6.9 fusion.106
  451.7 11.6 %fusion.102 = (bf16[8,512,1024]{2,1,0:T(8,128)(2,1)}, bf16[8,512,1024]{2,1,0:T(8,128)(2,1)}) fusion(bf16[8,1024,1024]{2,1,0:T(8,128)(2,1)} %get-tuple-element.197), kind=kLoop, calls=%fused_computation.98.clone.1 | loop fusion | bytes 33554432 | tf_op jit(solution)/shard_map/while/body/eval_jaxpr/jit(_take)/gather | solution.py:39
  463.3 4.1 gather_fusion
  470.0 4.1 gather_fusion.1
  477.3 5.8 fusion.104
  483.2 5.6 fusion.105
  488.8 6.9 fusion.106
  495.8 11.6 %fusion.102 = (bf16[8,512,1024]{2,1,0:T(8,128)(2,1)}, bf16[8,512,1024]{2,1,0:T(8,128)(2,1)}) fusion(bf16[8,1024,1024]{2,1,0:T(8,128)(2,1)} %get-tuple-element.197), kind=kLoop, calls=%fused_computation.98.clone.1 | loop fusion | bytes 33554432 | tf_op jit(solution)/shard_map/while/body/eval_jaxpr/jit(_take)/gather | solution.py:39
  507.4 4.1 gather_fusion
  514.1 4.1 gather_fusion.1
  521.4 5.8 fusion.104
  527.3 5.6 fusion.105
  532.9 7.0 fusion.106
  539.9 2.7 fusion.47
  544.6 8.7 %all-to-all-start.2 = ((bf16[2,1024,256]{2,0,1:T(2,128)(2,1)}), bf16[2,1024,256]{2,0,1:T(2,128)(2,1)S(1)}, u32[]{:S(2)}, u32[]{:S(2)}) async-start(bf16[2,1024,256]{2,0,1:T(2,128)(2,1)} %copy.111), calls=%async_computation.2 | async-start | bytes 2097152 | tf_op jit(solution)/shard_map/all_to_all | solution.py:125
  553.4 17.6 %all-to-all-done.2 = bf16[2,1024,256]{2,0,1:T(2,128)(2,1)S(1)} async-done(((bf16[2,1024,256]{2,0,1:T(2,128)(2,1)}), bf16[2,1024,256]{2,0,1:T(2,128)(2,1)S(1)}, u32[]{:S(2)}, u32[]{:S(2)}) %all-to-all-start.2) | async-done | bytes 1048608 | tf_op jit(solution)/shard_map/all_to_all | solution.py:125
  573.1 3.0 fusion.43
  576.4 2.7 fusion.51
  579.9 70.2 %all-gather.8.cloned.1.call-done = bf16[256,64,32]{2,1,0:T(8,128)(2,1)} async-done(((bf16[256,8,32]{2,1,0:T(8,128)(2,1)}), bf16[256,64,32]{2,1,0:T(8,128)(2,1)}) %all-gather.8.cloned.1.call-update) | async-done | bytes 1048592 | tf_op jit(solution)/shard_map/all_gather | solution.py:150
  654.4 126.6 %all-reduce.2.cloned.1.call-done = bf16[256,64,32]{2,1,0:T(8,128)(2,1)} async-done(((bf16[256,64,32]{2,1,0:T(8,128)(2,1)}), bf16[256,64,32]{2,1,0:T(8,128)(2,1)}) %all-reduce.2.cloned.1.call-update) | async-done | bytes 1048592 | tf_op jit(solution)/shard_map/psum | solution.py:15
  780.9 6.1 copy.119
  (145 shorter events, 74.0 us)
Async XLA Ops:
  7.2 782.3 %copy-start = (bf16[1024,128]{1,0:T(8,128)(2,1)S(1)}, bf16[1024,128]{1,0:T(8,128)(2,1)}, u32[]{:S(2)}) copy-start(bf16[1024,128]{1,0:T(8,128)(2,1)} %param.29) | copy-start | bytes 786436
  7.2 2.4 copy-start.2
  7.2 4.8 copy-start.16
  7.2 56.4 %all-gather.4.cloned.1.call-start = ((), (), s32[]{:S(2)}) async-start(), calls=%async_computation.3 | async-start | bytes 1179648 | tf_op jit(solution)/shard_map/all_gather | solution.py:85
  12.0 51.6 %copy-start.13 = (s32[256,8]{0,1:T(8,128)S(1)}, s32[256,8]{0,1:T(8,128)}, u32[]{:S(2)}) copy-start(s32[256,8]{0,1:T(8,128)} %param.17) | copy-start | bytes 24580
  15.6 69.2 %copy-start.8 = (bf16[256,256]{1,0:T(8,128)(2,1)S(1)}, bf16[256,256]{1,0:T(8,128)(2,1)}, u32[]{:S(2)}) copy-start(bf16[256,256]{1,0:T(8,128)(2,1)} %param.22) | copy-start | bytes 393220
  15.6 69.3 %copy-start.9 = (bf16[256,256]{1,0:T(8,128)(2,1)S(1)}, bf16[256,256]{1,0:T(8,128)(2,1)}, u32[]{:S(2)}) copy-start(bf16[256,256]{1,0:T(8,128)(2,1)} %param.23) | copy-start | bytes 393220
  15.6 69.4 %copy-start.10 = (bf16[256,256]{1,0:T(8,128)(2,1)S(1)}, bf16[256,256]{1,0:T(8,128)(2,1)}, u32[]{:S(2)}) copy-start(bf16[256,256]{1,0:T(8,128)(2,1)} %param.24) | copy-start | bytes 393220
  15.6 69.5 %copy-start.11 = (bf16[256,256]{1,0:T(8,128)(2,1)S(1)}, bf16[256,256]{1,0:T(8,128)(2,1)}, u32[]{:S(2)}) copy-start(bf16[256,256]{1,0:T(8,128)(2,1)} %param.25) | copy-start | bytes 393220
  15.6 152.1 %all-gather.6.cloned.1.call-start = ((), (), s32[]{:S(2)}) async-start(), calls=%async_computation.4 | async-start | bytes 17825792 | tf_op jit(solution)/shard_map/all_gather | solution.py:86
  80.2 30.9 %all-to-all-start = ((bf16[256,8,256]{2,1,0:T(8,128)(2,1)}), bf16[256,8,256]{2,1,0:T(8,128)(2,1)S(1)}, u32[]{:S(2)}, u32[]{:S(2)}) async-start(bf16[256,8,256]{2,1,0:T(8,128)(2,1)} %param.16), calls=%async_computation | async-start | bytes 2097152 | tf_op jit(solution)/shard_map/all_to_all | solution.py:76
  111.0 5.3 copy-start.3
  111.7 4.6 copy-start.6
  112.4 4.0 copy-start.12
  187.0 352.9 %copy-start.4 = (bf16[256,8,256]{2,1,0:T(8,128)(2,1)S(1)}, bf16[256,8,256]{2,1,0:T(8,128)(2,1)}, u32[]{:S(2)}) copy-start(bf16[256,8,256]{2,1,0:T(8,128)(2,1)} %copy-done.3) | copy-start | bytes 3145732
  187.0 352.9 %copy-start.7 = (f32[2,128,8]{2,1,0:T(8,128)S(1)}, f32[2,128,8]{2,1,0:T(8,128)}, u32[]{:S(2)}) copy-start(f32[2,128,8]{2,1,0:T(8,128)} %copy-done.6) | copy-start | bytes 24580
  218.6 5.6 copy-start.1
  262.7 5.6 copy-start.1
  306.8 5.6 copy-start.1
  350.9 5.6 copy-start.1
  395.0 5.6 copy-start.1
  439.1 5.6 copy-start.1
  483.2 5.6 copy-start.1
  527.3 5.6 copy-start.1
  542.6 10.8 %copy-start.14 = (s32[256]{0:T(256)S(1)}, s32[256]{0:T(256)}, u32[]{:S(2)}) copy-start(s32[256]{0:T(256)} %param.18) | copy-start | bytes 3076
  544.6 26.4 %all-to-all-start.2 = ((bf16[2,1024,256]{2,0,1:T(2,128)(2,1)}), bf16[2,1024,256]{2,0,1:T(2,128)(2,1)S(1)}, u32[]{:S(2)}, u32[]{:S(2)}) async-start(bf16[2,1024,256]{2,0,1:T(2,128)(2,1)} %copy.111), calls=%async_computation.2 | async-start | bytes 2097152 | tf_op jit(solution)/shard_map/all_to_all | solution.py:125
  553.3 96.8 %all-gather.8.cloned.1.call-start = ((), (), s32[]{:S(2)}) async-start(), calls=%async_computation.5 | async-start | bytes 4718592 | tf_op jit(solution)/shard_map/all_gather | solution.py:150
  572.4 80.0 %copy-start.5 = (bf16[128,2,8,256]{3,2,1,0:T(8,128)(2,1)}, bf16[128,2,8,256]{3,2,1,0:T(8,128)(2,1)S(1)}, u32[]{:S(2)}) copy-start(bf16[128,2,8,256]{3,2,1,0:T(8,128)(2,1)S(1)} %copy.112) | copy-start | bytes 3145732
  579.2 201.7 %all-reduce.2.cloned.1.call-start = ((), (), s32[]{:S(2)}) async-start(), calls=%async_computation.6 | async-start | bytes 8388608 | tf_op jit(solution)/shard_map/psum | solution.py:15
  652.4 0.7 copy-start.15
Sparse Core Ops, SparseCore 0:
  15.7 47.8 all-gather.3
  65.3 102.3 all-gather.5
  579.3 70.7 all-gather.7
  652.5 128.3 all-reduce.1
where the time goes:
time: 799 us; the launch traced here: 798 us
  waiting for transfers between devices  337 us (42%)
  local copies, waits for them, and re-layouts  231 us (29%)
  matrix products  167 us (21%)
  other arithmetic  18.2 us (2%)
  blocking collectives  16.4 us (2%)
  between operations  14.8 us (2%)
  starting transfers between devices  13.4 us (2%)
    gather x40, local copies, waits for them, and re-layouts, one_pair(): bias_two = jnp.take(bias, h_two, axis=0).astype(jnp.float32)  199 us
    psum x1, waiting for transfers between devices, broadcast(): return lax.psum(block, axis)  127 us
    all_gather x1, waiting for transfers between devices, per_device(): row_block = lax.all_gather(first_factor, 'col', axis=1, tiled=True)  70.2 us
    dot_general x8, matrix products, one_pair(): jnp.einsum('nij,ndj->ndi', probs, v_two, preferred_element_type=jnp.float32)  55.5 us
    all_gather x1, waiting for transfers between devices, per_device(): full_bias = lax.all_gather(wide, 'row', axis=1, tiled=True)  49.4 us
    all_gather x1, waiting for transfers between devices, per_device(): wide = lax.all_gather(tile, 'col', axis=2, tiled=True)  47.9 us
    sub x8, matrix products, one_pair(): probs = jax.nn.softmax(score, axis=-1).astype(jnp.bfloat16)  46.7 us
    dot_general x8, matrix products, one_pair(): jnp.einsum('ndi,ndj->nij', q_two, k_two, preferred_element_type=jnp.float32)  45.1 us
  transfers between devices with their start and end apart: 6, of which 6 were waited for; matrix products, arithmetic and copies ran while one was open for 1% of the time, Pallas kernels for 0%

commit v1 on v0

v1 whole, which is shorter than its diff:
```python
import functools

import jax
import jax.numpy as jnp
from jax import lax
from jax.experimental import pallas as pl
from jax.experimental.pallas import tpu as pltpu
from jax.sharding import PartitionSpec as P

LOG2E = 1.4426950408889634
MASKED = -1e9 * LOG2E
BOTH = ("row", "col")
NT = (((1,), (1,)), ((), ()))
TN = (((0,), (0,)), ((), ()))


def dot(a, b, dims=None):
    if dims is None:
        return jnp.dot(a, b, preferred_element_type=jnp.float32)
    return lax.dot_general(a, b, dims, preferred_element_type=jnp.float32)


def params(mib=48):
    return pltpu.CompilerParams(vmem_limit_bytes=mib << 20)


def cost(flops, moved, exps=0):
    return pl.CostEstimate(flops=flops, bytes_accessed=moved, transcendentals=exps)


def standardize(x):
    mean = jnp.mean(x, axis=-1, keepdims=True)
    centred = x - mean
    var = jnp.mean(centred * centred, axis=-1, keepdims=True)
    return centred * lax.rsqrt(var + 1e-05)


def iota(shape, dim):
    return lax.broadcasted_iota(jnp.int32, shape, dim)


def spread_columns(w):
    row, col = iota((256, 1024), 0), iota((256, 1024), 1)
    pick = (row == (col // 128) * 32 + col % 32).astype(jnp.bfloat16)
    wide = dot(w, pick).astype(jnp.bfloat16)
    quarter = (col // 32) % 4
    return [jnp.where(quarter == si, wide, jnp.zeros_like(wide)) for si in range(4)]


def spread_rows(w):
    row, col = iota((1024, 256), 0), iota((1024, 256), 1)
    pick = (col == (row // 128) * 32 + row % 32).astype(jnp.bfloat16)
    tall = dot(pick, w).astype(jnp.bfloat16)
    quarter = (row // 32) % 4
    return [jnp.where(quarter == si, tall, jnp.zeros_like(tall)) for si in range(4)]


def factor_columns(w, residue):
    row, col = iota((32, 256), 0), iota((32, 256), 1)
    pick = jnp.where((row == col // 8) & (col % 8 == residue), 1.0, 0.0).astype(jnp.bfloat16)
    return dot(w, pick).astype(jnp.bfloat16)


def right_columns(w, residue):
    row, col = iota((32, 256), 0), iota((32, 256), 1)
    pick = jnp.where((row == col % 32) & (col // 32 == residue), 1.0, 0.0).astype(jnp.bfloat16)
    return dot(w, pick).astype(jnp.bfloat16)


def four_abreast(x):
    groups, width = x.shape[0], x.shape[3]
    return jnp.concatenate([x[:, si].reshape(groups * 8, width) for si in range(4)], axis=1)


def bias_kernel(duo_ref, w_ref, flags_ref, out_ref, rows_s):
    step = pl.program_id(0)

    @pl.when(step < 4)
    def _():
        x = duo_ref[...].reshape(16 * 128, 128).astype(jnp.float32)
        n = standardize(x).astype(jnp.bfloat16)
        heads = lax.dot_general(
            w_ref[...], n, (((0,), (1,)), ((), ())), preferred_element_type=jnp.float32
        )
        for i in range(16):
            rows_s[:, i, :] = heads[:, i * 128 : (i + 1) * 128] * LOG2E
        out_ref[...] = rows_s[...].astype(jnp.bfloat16)

    @pl.when(step == 4)
    def _():
        out_ref[...] = jnp.broadcast_to(flags_ref[...][None], (8, 16, 128))


def bias_tile(duo, w, flags):
    return pl.pallas_call(
        bias_kernel,
        grid=(5,),
        in_specs=[
            pl.BlockSpec((16, 128, 128), lambda i: (jnp.minimum(i, 3), 0, 0)),
            pl.BlockSpec((128, 8), lambda i: (0, 0)),
            pl.BlockSpec((16, 128), lambda i: (0, 0)),
        ],
        out_specs=pl.BlockSpec((8, 16, 128), lambda i: (0, i, 0)),
        out_shape=jax.ShapeDtypeStruct((8, 80, 128), jnp.bfloat16),
        scratch_shapes=[pltpu.VMEM((8, 16, 128), jnp.float32)],
        compiler_params=params(),
        cost_estimate=cost(20_000_000, 2_200_000),
        name="bias_tile",
    )(duo, w, flags)


def qkv_kernel(x_ref, wq_ref, wk_ref, wv_ref, out_ref, w_s):
    @pl.when(pl.program_id(0) == 0)
    def _():
        for t, w in enumerate((wq_ref, wk_ref, wv_ref)):
            for si, part in enumerate(spread_columns(w[...])):
                w_s[t, si * 256 : (si + 1) * 256, :] = part

    x = x_ref[...].reshape(16, 4, 8, 256).astype(jnp.float32)
    n = four_abreast(standardize(x)).astype(jnp.bfloat16)
    for t in range(3):
        y = dot(n, w_s[t])
        if t == 0:
            y = y * (LOG2E / 32**0.5)
        y = y.reshape(4, 4, 8, 1024)
        for h in range(8):
            for g in range(4):
                out_ref[h, t, g] = y[:, g, :, h * 128 : (h + 1) * 128].astype(jnp.bfloat16)


def qkv(x, wq, wk, wv):
    whole = pl.BlockSpec((256, 256), lambda i: (0, 0))
    return pl.pallas_call(
        qkv_kernel,
        grid=(4,),
        in_specs=[
            pl.BlockSpec((4, 4, 4, 8, 256), lambda i: (i, 0, 0, 0, 0)),
            whole,
            whole,
            whole,
        ],
        out_specs=pl.BlockSpec((8, 3, 4, 4, 8, 128), lambda i: (0, 0, 0, i, 0, 0)),
        out_shape=jax.ShapeDtypeStruct((8, 3, 4, 16, 8, 128), jnp.bfloat16),
        scratch_shapes=[pltpu.VMEM((3, 1024, 1024), jnp.bfloat16)],
        compiler_params=params(),
        cost_estimate=cost(3_500_000_000, 4_500_000),
        name="qkv",
    )(x, wq, wk, wv)


def natural(block):
    x = jnp.swapaxes(block.astype(jnp.float32), 0, 1)
    return x.reshape(x.shape[0] * 64, 128).astype(jnp.bfloat16)


def attention_kernel(
    block, blocks, slab_ref, q_ref, k_ref, v_ref, bias_ref, mask_ref, out_ref, q_s, k_s, v_s
):
    lane = iota((1, 128), 1) // 32
    q_s[...] = natural(q_ref[:, 0, 0])
    k_s[...] = natural(k_ref[:, 0, 0])
    v = natural(v_ref[:, 0, 0])
    for si in range(4):
        keep = lane == si
        v_s[si, :, :128] = jnp.where(keep, v, jnp.zeros_like(v))
        v_s[si, :, 128:] = jnp.broadcast_to(jnp.where(keep, 1.0, 0.0), (1024, 128)).astype(
            jnp.bfloat16
        )
    present = [mask_ref[0, si : si + 1, :] > 0 for si in range(4)]
    tiles = block // 64

    def step(at, carry):
        rows = pl.ds(pl.multiple_of(at * block, block), block)
        q = q_s[rows, :]
        bias = jnp.concatenate(
            [
                jnp.concatenate([bias_ref[at * tiles + t, c, :64, :] for c in range(8)], 1)
                for t in range(tiles)
            ],
            0,
        )
        total = jnp.zeros((block, 256), jnp.float32)
        for si in range(4):
            one = jnp.where(lane == si, q, jnp.zeros_like(q))
            score = dot(one, k_s[...], NT) + bias.astype(jnp.float32)
            score = jnp.where(present[si], score, MASKED)
            top = jnp.max(score, axis=1, keepdims=True)
            probs = jnp.exp2(score - top).astype(jnp.bfloat16)
            total = total + dot(probs, v_s[si])
        result = total[:, :128] / total[:, 128:]
        eighth = block // 8
        out_ref[pl.ds(pl.multiple_of(at * eighth, eighth), eighth), 0] = result.reshape(
            eighth, 8, 128
        ).astype(jnp.bfloat16)
        return carry

    lax.fori_loop(0, blocks, step, 0)


def attention(received, bias, mask, slab=None):
    if slab is None:
        block, count = 256, 16
        slab = jnp.zeros((1,), jnp.int32)
        first = lambda slab_ref: 0
        name = "attention"
    else:
        block, count = 64, 1
        first = lambda slab_ref: slab_ref[0]
        name = "slab_attention"
    part = lambda t: pl.BlockSpec((8, 1, 1, 16, 8, 128), lambda g, s: (0, t, g, 0, 0, 0))
    return pl.pallas_call(
        functools.partial(attention_kernel, block, count * 64 // block),
        grid_spec=pltpu.PrefetchScalarGridSpec(
            num_scalar_prefetch=1,
            grid=(4,),
            in_specs=[
                pl.BlockSpec((8, 1, 1, count, 8, 128), lambda g, s: (0, 0, g, first(s), 0, 0)),
                part(1),
                part(2),
                pl.BlockSpec((count, 8, 80, 128), lambda g, s: (first(s), 0, 0, 0)),
                pl.BlockSpec((1, 4, 1024), lambda g, s: (g, 0, 0)),
            ],
            out_specs=pl.BlockSpec((count * 8, 1, 8, 128), lambda g, s: (0, g, 0, 0)),
            scratch_shapes=[
                pltpu.VMEM((count * 64, 128), jnp.bfloat16),
                pltpu.VMEM((1024, 128), jnp.bfloat16),
                pltpu.VMEM((4, 1024, 256), jnp.bfloat16),
            ],
        ),
        out_shape=jax.ShapeDtypeStruct((count * 8, 4, 8, 128), jnp.bfloat16),
        compiler_params=params(),
        cost_estimate=cost(count * 2_000_000_000, 3_000_000 + count * 200_000, count << 20),
        name=name,
    )(slab, received, received, received, bias, mask)


def gated_update(x, weighted, w_gate, w_out):
    n = four_abreast(standardize(x)).astype(jnp.bfloat16)
    gate = jax.nn.sigmoid(dot(n, w_gate))
    gated = (gate * weighted).astype(jnp.bfloat16)
    update = dot(gated, w_out)
    fresh = x + jnp.stack(
        [update[:, si * 256 : (si + 1) * 256].reshape(-1, 8, 256) for si in range(4)], axis=1
    )
    return fresh.astype(jnp.bfloat16).astype(jnp.float32)


def fill_weights(gate_ref, out_ref, gate_s, out_s):
    for si, part in enumerate(spread_columns(gate_ref[...])):
        gate_s[si * 256 : (si + 1) * 256, :] = part
    for si, part in enumerate(spread_rows(out_ref[...])):
        out_s[:, si * 256 : (si + 1) * 256] = part


def left_kernel(
    slab_ref, x_ref, weighted_ref, flags_ref, gate_ref, out_w_ref, factor_ref, out_ref,
    gate_s, out_s, normed_s,
):
    fill_weights(gate_ref, out_w_ref, gate_s, out_s)
    x = x_ref[0].astype(jnp.float32)
    weighted = jnp.concatenate(
        [weighted_ref[h].astype(jnp.float32).reshape(32, 128) for h in range(8)], axis=1
    )
    fresh = gated_update(x, weighted, gate_s[...], out_s[...])
    normed_s[...] = standardize(fresh).reshape(16, 8, 256)
    left = jnp.zeros((16, 256), jnp.float32)
    for residue in range(8):
        part = normed_s[:, residue, :].astype(jnp.bfloat16)
        left = left + dot(part, factor_columns(factor_ref[...], residue))
    left = (left * flags_ref[...]).astype(jnp.bfloat16)
    out_ref[...] = jnp.broadcast_to(left[None], (128, 16, 256))


def left_factor(slab, x, weighted, flags, w_gate, w_out, w_first):
    whole = lambda *shape: pl.BlockSpec(shape, lambda i, s: (0,) * len(shape))
    return pl.pallas_call(
        left_kernel,
        grid_spec=pltpu.PrefetchScalarGridSpec(
            num_scalar_prefetch=1,
            grid=(1,),
            in_specs=[
                pl.BlockSpec((1, 4, 4, 8, 256), lambda i, s: (s[0], 0, 0, 0, 0)),
                whole(8, 4, 8, 128),
                whole(16, 1),
                whole(256, 256),
                whole(256, 256),
                whole(256, 32),
            ],
            out_specs=whole(128, 16, 256),
            scratch_shapes=[
                pltpu.VMEM((1024, 1024), jnp.bfloat16),
                pltpu.VMEM((1024, 1024), jnp.bfloat16),
                pltpu.VMEM((16, 8, 256), jnp.float32),
            ],
        ),
        out_shape=jax.ShapeDtypeStruct((128, 16, 256), jnp.bfloat16),
        compiler_params=params(),
        cost_estimate=cost(1_000_000_000, 1_500_000),
        name="left_factor",
    )(slab, x, weighted, flags, w_gate, w_out, w_first)


def final_kernel(
    x_ref, weighted_ref, flags_ref, left_ref, gate_ref, out_w_ref, factor_ref, product_ref,
    fresh_ref, pair_ref, gate_s, out_s, factor_s, normed_s, right_s, outer_s, pair_s,
):
    step = pl.program_id(0)

    @pl.when(step == 0)
    def _():
        fill_weights(gate_ref, out_w_ref, gate_s, out_s)
        for residue in range(8):
            factor_s[residue] = right_columns(factor_ref[...], residue)

    x = x_ref[...].reshape(16, 4, 8, 256).astype(jnp.float32)
    weighted = jnp.concatenate(
        [
            weighted_ref[:, h].astype(jnp.float32).reshape(128, 128)
            for h in range(8)
        ],
        axis=1,
    )
    fresh = gated_update(x, weighted, gate_s[...], out_s[...])
    fresh_ref[...] = fresh.reshape(64, 8, 256).astype(jnp.bfloat16)
    normed_s[...] = standardize(fresh).reshape(64, 8, 256)
    right = jnp.zeros((64, 256), jnp.float32)
    for residue in range(8):
        part = normed_s[:, residue, :].astype(jnp.bfloat16)
        right = right + dot(part, factor_s[residue])
    right_s[pl.ds(pl.multiple_of(step * 64, 64), 64), :] = (right * flags_ref[...]).astype(
        jnp.bfloat16
    )

    @pl.when(step == pl.num_programs(0) - 1)
    def _():
        right_all = right_s[...]
        for c in range(8):
            left = left_ref[:, c].reshape(256, 256)
            outer_s[:, c] = (dot(left, right_all, TN) * (1.0 / 256)).reshape(32, 8, 256)
        lane = iota((1, 128), 1) // 32
        for j in range(8):
            half, source = (j // 4) * 128, j % 4
            quads = []
            for quad in range(8):
                block = None
                for u in range(4):
                    part = outer_s[quad * 4 + u, :, :, half : half + 128].reshape(64, 128)
                    if u != source:
                        part = pltpu.roll(part, ((u - source) % 4) * 32, 1)
                    block = part if block is None else jnp.where(lane == u, part, block)
                quads.append(block.astype(jnp.bfloat16))
            pair_s[:, j, :] = dot(jnp.concatenate(quads, axis=1), product_ref[...])
        pair_ref[...] = pair_s[...].astype(jnp.bfloat16)


def finish(x, weighted, flags, left, w_gate, w_out, w_second, w_product):
    whole = lambda *shape: pl.BlockSpec(shape, lambda i: (0,) * len(shape))
    return pl.pallas_call(
        final_kernel,
        grid=(4,),
        in_specs=[
            pl.BlockSpec((64, 8, 256), lambda i: (i, 0, 0)),
            pl.BlockSpec((4, 8, 4, 8, 128), lambda i: (i, 0, 0, 0, 0)),
            pl.BlockSpec((64, 1), lambda i: (i, 0)),
            whole(16, 8, 16, 256),
            whole(256, 256),
            whole(256, 256),
            whole(256, 32),
            whole(1024, 128),
        ],
        out_specs=[pl.BlockSpec((64, 8, 256), lambda i: (i, 0, 0)), whole(64, 8, 128)],
        out_shape=[
            jax.ShapeDtypeStruct((256, 8, 256), jnp.bfloat16),
            jax.ShapeDtypeStruct((64, 8, 128), jnp.bfloat16),
        ],
        scratch_shapes=[
            pltpu.VMEM((1024, 1024), jnp.bfloat16),
            pltpu.VMEM((1024, 1024), jnp.bfloat16),
            pltpu.VMEM((8, 256, 256), jnp.bfloat16),
            pltpu.VMEM((64, 8, 256), jnp.float32),
            pltpu.VMEM((256, 256), jnp.bfloat16),
            pltpu.VMEM((32, 8, 8, 256), jnp.float32),
            pltpu.VMEM((64, 8, 128), jnp.float32),
        ],
        compiler_params=params(),
        cost_estimate=cost(3_000_000_000, 5_000_000),
        name="finish",
    )(x, weighted, flags, left, w_gate, w_out, w_second, w_product)


def exchange(x, axes):
    return lax.all_to_all(x, axes, split_axis=0, concat_axis=0, tiled=True)


def per_device(
    alignment_tensor,
    amino_exists_flags,
    chain_exists_flags,
    chosen_slab_number,
    duo_tensor,
    duo_offset_matrix,
    asking_matrix,
    lookup_matrix,
    content_matrix,
    sigmoid_matrix,
    final_projection_matrix,
    first_factor_matrix,
    second_factor_matrix,
    product_to_duo_matrix,
):
    row = lax.axis_index("row")
    slab = chosen_slab_number
    sequences = exchange(alignment_tensor, "row").reshape(16, 4, 4, 8, 256)
    flags = amino_exists_flags.astype(jnp.bfloat16).reshape(16, 128)
    tile = bias_tile(duo_tensor, duo_offset_matrix, flags)
    bias = lax.all_gather(exchange(tile, "col"), "row", axis=0, tiled=False)
    received = exchange(qkv(sequences, asking_matrix, lookup_matrix, content_matrix), "col")

    mask = lax.dynamic_index_in_dim(bias, 64 + row, axis=2, keepdims=False)
    mask = jnp.transpose(mask.reshape(16, 8, 16, 8), (2, 0, 1, 3))
    mask = mask.reshape(4, 4, 1024).astype(jnp.float32)

    chains = chain_exists_flags.astype(jnp.float32)[:, None]
    own_chains = lax.dynamic_slice_in_dim(chains, row * 16, 16, 0)
    slab_weighted = exchange(attention(received, bias, mask, slab), "col")
    left = left_factor(
        slab,
        sequences,
        slab_weighted,
        own_chains,
        sigmoid_matrix,
        final_projection_matrix,
        first_factor_matrix,
    )
    left = exchange(left, BOTH).reshape(16, 8, 16, 256)
    weighted = exchange(attention(received, bias, mask), BOTH).reshape(16, 8, 4, 8, 128)
    return tuple(
        finish(
            alignment_tensor,
            weighted,
            chains,
            left,
            sigmoid_matrix,
            final_projection_matrix,
            second_factor_matrix,
            product_to_duo_matrix,
        )
    )


def solution(mesh):
    placed = (
        P(None, BOTH, None),
        P(None, BOTH),
        P(),
        P(),
        P("row", "col", None),
    ) + (P(),) * 9
    return jax.shard_map(
        per_device,
        mesh=mesh,
        in_specs=placed,
        out_specs=(P(None, BOTH, None), P(None, BOTH, None)),
        check_vma=False,
    )
```

time: 799 us -> 229 us (0.29)
  waiting for transfers between devices: 337 us -> 61.2 us
  local copies, waits for them, and re-layouts: 231 us -> 18.2 us
  matrix products: 167 us -> 0 us
  Pallas kernels: 0 us -> 66 us
  blocking collectives: 16.4 us -> 42.1 us
  other arithmetic: 18.2 us -> 1.71 us
  starting transfers between devices: 13.4 us -> 23.7 us
    gather x40 -> x0, local copies, waits for them, and re-layouts: 199 us -> none  [one_pair(): bias_two = jnp.take(bias, h_two, axis=0).astype(jnp.float32)]
    all_gather x3 -> x1, waiting for transfers between devices: 168 us -> 2.62 us  [per_device(): bias = lax.all_gather(exchange(tile, 'col'), 'row', axis=0, tiled=False)]
    psum x1 -> x0, waiting for transfers between devices: 127 us -> none  [broadcast(): return lax.psum(block, axis)]
    dot_general x25 -> x0, matrix products: 120 us -> none  [the longest x8 55.5 us: one_pair(): jnp.einsum('nij,ndj->ndi', probs, v_two, preferred_element_type=jnp.float32)]
    pallas_call x0 -> x6, Pallas kernels: none -> 66 us  [the longest x2 44 us: attention(): pl.pallas_call(functools.partial(attention_kernel, block, count * 64 // b...]
    sub x8 -> x0, matrix products: 46.7 us -> none  [one_pair(): probs = jax.nn.softmax(score, axis=-1).astype(jnp.bfloat16)]
    all_to_all x1 -> x2, blocking collectives: 16.4 us -> 42.1 us  [exchange(): return lax.all_to_all(x, axes, split_axis=0, concat_axis=0, tiled=True)]
    while x17 -> x0, local copies, waits for them, and re-layouts: 18.7 us -> none  [the longest x1 18.6 us: attend(): result = lax.map(one_pair, (flat_q, flat_k, flat_v, mask_items, item_heads))]
  transfers between devices with their start and end apart: 6 -> 5, of which waited for: 6 -> 4; matrix products, arithmetic and copies ran while one was open for 1% -> 3% of each run, Pallas kernels for 0% -> 20%
where the time goes in v1:
time: 229 us; the launch traced here: 228 us
  Pallas kernels  66 us (29%)
  waiting for transfers between devices  61.2 us (27%)
  blocking collectives  42.1 us (18%)
  starting transfers between devices  23.7 us (10%)
  local copies, waits for them, and re-layouts  18.2 us (8%)
  between operations  14.9 us (7%)
    all_to_all x4, waiting for transfers between devices, exchange(): return lax.all_to_all(x, axes, split_axis=0, concat_axis=0, tiled=True)  58.6 us
    pallas_call x2, Pallas kernels, attention(): pl.pallas_call(functools.partial(attention_kernel, block, count * 64 // b...  44 us
    all_to_all x2, blocking collectives, exchange(): return lax.all_to_all(x, axes, split_axis=0, concat_axis=0, tiled=True)  42.1 us
    all_to_all x4, starting transfers between devices, exchange(): return lax.all_to_all(x, axes, split_axis=0, concat_axis=0, tiled=True)  23.6 us
    unnamed x43, local copies, waits for them, and re-layouts  12.5 us
    pallas_call x1, Pallas kernels, finish(): pl.pallas_call(final_kernel, grid=(4,), in_specs=[pl.BlockSpec((64, 8, 25...  10.3 us
    pallas_call x1, Pallas kernels, qkv(): pl.pallas_call(qkv_kernel, grid=(4,), in_specs=[pl.BlockSpec((4, 4, 4, 8,...  6.17 us
    convert_element_type x3, local copies, waits for them, and re-layouts, per_device(): mask = mask.reshape(4, 4, 1024).astype(jnp.float32)  5.15 us
  transfers between devices with their start and end apart: 5, of which 4 were waited for; matrix products, arithmetic and copies ran while one was open for 3% of the time, Pallas kernels for 20%

profile of v1, /device:TPU:1, one launch (start us, length us, event | category | flops | bytes accessed | tf_op | source)
XLA Modules:
  0.0 227.8 jit_solution(3437262908273198897)
XLA Ops:
  7.2 0.0 copy-start.11
  7.2 0.0 all-gather.3.cloned.1.call-start
  7.2 0.8 copy.39.w_ref
  8.0 0.7 convert_element_type.15
  8.8 0.1 copy.38
  8.9 0.1 reshape.25.flags_ref
  9.0 0.0 copy-start.4
  9.0 1.6 copy-done.4
  10.6 0.0 copy-start.12
  10.6 0.0 copy-start.13
  10.6 3.3 %bias_tile.1 = bf16[8,80,128]{2,1,0:T(8,128)(2,1)S(1)} custom-call(bf16[64,128,128]{2,1,0:T(8,128)(2,1)S(1)} %copy-done.4, bf16[128,8]{1,0:T(8,128)(2,1)S(1)} %copy.39.w_ref, bf16[16,128]{1,0:T(8,128)(2,1)S(1)} %reshape.25.flags_ref), custom_call_target="tpu_custom_call" | custom-call | flops 20000000 | bytes 2200000 | tf_op jit(solution)/shard_map/bias_tile/pallas_call | solution.py:95
  13.9 15.3 %all_to_all.30 = bf16[8,80,128]{2,1,0:T(8,128)(2,1)} all-to-all(bf16[8,80,128]{2,1,0:T(8,128)(2,1)S(1)} %bias_tile.1), channel_id=1, replica_groups=mesh['row'=16,'col'=8] {'col'}, dimensions={0} | all-to-all | bytes 327680 | tf_op jit(solution)/shard_map/all_to_all | solution.py:392
  29.2 0.0 all-gather.3.cloned.1.call-update
  29.3 0.0 copy-done.5
  29.3 26.8 %all_to_all.31 = bf16[256,8,256]{2,1,0:T(8,128)(2,1)S(1)} all-to-all(bf16[256,8,256]{2,1,0:T(8,128)(2,1)S(1)} %copy-done.5), channel_id=1, replica_groups=mesh['row'=16,'col'=8] {'row'}, dimensions={0} | all-to-all | bytes 2097152 | tf_op jit(solution)/shard_map/all_to_all | solution.py:392
  56.1 0.0 copy-done.11
  56.1 0.0 copy-done.12
  56.1 0.0 copy-done.13
  56.1 6.2 %qkv.1 = bf16[8,3,4,16,8,128]{5,4,3,2,1,0:T(8,128)(2,1)S(1)} custom-call(bf16[16,4,4,8,256]{4,3,2,1,0:T(8,128)(2,1)S(1)} %bitcast.15, bf16[256,256]{1,0:T(8,128)(2,1)S(1)} %copy-done.11, bf16[256,256]{1,0:T(8,128)(2,1)S(1)} %copy-done.12, bf16[256,256]{1,0:T(8,128)(2,1)S(1)} %copy-done.13), custom_call_target="tpu_custom_call" | custom-call | flops 3500000000 | bytes 4500000 | tf_op jit(solution)/shard_map/qkv/pallas_call | solution.py:133
  62.3 0.0 copy-start.1
  62.3 1.6 copy-done.1
  63.9 0.0 copy-start.7
  63.9 1.0 copy-done.7
  64.9 3.6 %all-to-all-start.1 = ((bf16[8,3,4,16,8,128]{5,4,3,2,1,0:T(8,128)(2,1)}), bf16[8,3,4,16,8,128]{5,4,3,2,1,0:T(8,128)(2,1)S(1)}, u32[]{:S(2)}, u32[]{:S(2)}) async-start(bf16[8,3,4,16,8,128]{5,4,3,2,1,0:T(8,128)(2,1)} %copy-done.1), calls=%async_computation.1 | async-start | bytes 6291456 | tf_op jit(solution)/shard_map/all_to_all | solution.py:392
  69.2 2.6 %all-gather.3.cloned.1.call-done = bf16[128,80,128]{2,1,0:T(8,128)(2,1)} async-done(((bf16[8,80,128]{2,1,0:T(8,128)(2,1)}), bf16[128,80,128]{2,1,0:T(8,128)(2,1)}) %all-gather.3.cloned.1.call-update) | async-done | bytes 2621456 | tf_op jit(solution)/shard_map/all_gather | solution.py:416
  71.8 1.0 dynamic-slice_convert_fusion
  72.8 1.0 copy.40
  73.8 2.4 %copy.41 = f32[16,16,8,8]{3,2,1,0:T(8,128)} copy(f32[16,16,8,8]{1,3,0,2:T(8,128)} %bitcast.19) | data formatting | bytes 131072 | tf_op jit(solution)/shard_map/convert_element_type | solution.py:421
  76.2 1.8 reshape.28.mask_ref
  78.0 27.9 %all-to-all-done.1.q_ref.k_ref.v_ref = bf16[8,3,4,16,8,128]{5,4,3,2,1,0:T(8,128)(2,1)S(1)} async-done(((bf16[8,3,4,16,8,128]{5,4,3,2,1,0:T(8,128)(2,1)}), bf16[8,3,4,16,8,128]{5,4,3,2,1,0:T(8,128)(2,1)S(1)}, u32[]{:S(2)}, u32[]{:S(2)}) %all-to-all-start.1) | async-done | bytes 3145760 | tf_op jit(solution)/shard_map/all_to_all | solution.py:392
  105.8 0.0 copy-start.2
  105.8 1.7 copy-done.2
  107.6 0.0 copy-start
  107.6 6.2 %slab_attention.1 = bf16[8,4,8,128]{3,2,1,0:T(8,128)(2,1)} custom-call(s32[1]{0:T(128)S(6)} %copy.46.slab_ref, bf16[8,3,4,16,8,128]{5,4,3,2,1,0:T(8,128)(2,1)S(1)} %all-to-all-done.1.q_ref.k_ref.v_ref, bf16[8,3,4,16,8,128]{5,4,3,2,1,0:T(8,128)(2,1)S(1)} %all-to-all-done.1.q_ref.k_ref.v_ref, ...), custom_call_target="tpu_custom_call" | custom-call | flops 2000000000 | bytes 3200000 | tf_op jit(solution)/shard_map/slab_attention/pallas_call | solution.py:211
  113.8 0.0 copy-done
  113.8 5.2 %all-to-all-start.4 = ((bf16[8,4,8,128]{3,2,1,0:T(8,128)(2,1)}), bf16[8,4,8,128]{3,2,1,0:T(8,128)(2,1)S(1)}, u32[]{:S(2)}, u32[]{:S(2)}) async-start(bf16[8,4,8,128]{3,2,1,0:T(8,128)(2,1)} %slab_attention.1), calls=%async_computation.4 | async-start | bytes 131072 | tf_op jit(solution)/shard_map/all_to_all | solution.py:392
  119.0 0.0 copy-start.3
  119.0 1.7 copy-done.3
  120.7 0.0 copy-start.19
  120.8 37.8 %attention.1 = bf16[128,4,8,128]{3,2,1,0:T(8,128)(2,1)} custom-call(s32[1]{0:T(128)} %constant.8.clone.1.slab_ref, bf16[8,3,4,16,8,128]{5,4,3,2,1,0:T(8,128)(2,1)} %copy-done, bf16[8,3,4,16,8,128]{5,4,3,2,1,0:T(8,128)(2,1)} %copy-done, bf16[8,3,4,16,8,128]{5,4,3,2,1,0:T(8,128)(2,1)} %copy-done, bf16[16,8,80,128]{3,2,1,0:T(8,128)(2,1)S(1)} %bitcast.14, ...), custom_call_target="tpu_custom_call" | custom-call | flops 32000000000 | bytes 6200000 | tf_op jit(solution)/shard_map/attention/pallas_call | solution.py:211
  158.6 0.0 all-to-all-done.4.weighted_ref
  158.6 9.2 %all-to-all-start.3 = ((bf16[128,4,8,128]{3,2,1,0:T(8,128)(2,1)}), bf16[128,4,8,128]{3,2,1,0:T(8,128)(2,1)S(1)}, u32[]{:S(2)}, u32[]{:S(2)}) async-start(bf16[128,4,8,128]{3,2,1,0:T(8,128)(2,1)} %attention.1), calls=%async_computation.3 | async-start | bytes 2097152 | tf_op jit(solution)/shard_map/all_to_all | solution.py:392
  167.7 0.0 copy-done.19
  167.8 0.1 dynamic-slice_bitcast_fusion
  167.8 0.1 copy.42.flags_ref
  167.9 0.0 copy-done.17
  167.9 0.1 copy.43.factor_ref
  168.0 0.0 copy-done.8
  168.0 0.0 copy-done.14
  168.1 0.0 copy-start.15
  168.1 0.9 copy-done.15
  169.0 2.2 left_factor.1
  171.1 0.0 copy-start.9
  171.1 1.0 copy-done.9
  172.1 13.3 %all-to-all-done.3 = bf16[128,4,8,128]{3,2,1,0:T(8,128)(2,1)S(1)} async-done(((bf16[128,4,8,128]{3,2,1,0:T(8,128)(2,1)}), bf16[128,4,8,128]{3,2,1,0:T(8,128)(2,1)S(1)}, u32[]{:S(2)}, u32[]{:S(2)}) %all-to-all-start.3) | async-done | bytes 1048608 | tf_op jit(solution)/shard_map/all_to_all | solution.py:392
  185.4 5.6 %all-to-all-start.5 = ((bf16[128,16,256]{2,1,0:T(8,128)(2,1)}), bf16[128,16,256]{2,1,0:T(8,128)(2,1)S(1)}, u32[]{:S(2)}, u32[]{:S(2)}) async-start(bf16[128,16,256]{2,1,0:T(8,128)(2,1)} %copy-done.9), calls=%async_computation.5 | async-start | bytes 2097152 | tf_op jit(solution)/shard_map/all_to_all | solution.py:392
  191.1 0.1 copy.44.flags_ref
  191.2 0.0 copy-done.18
  191.2 0.1 copy.45.factor_ref
  191.3 17.4 %all-to-all-done.5 = bf16[128,16,256]{2,1,0:T(8,128)(2,1)S(1)} async-done(((bf16[128,16,256]{2,1,0:T(8,128)(2,1)}), bf16[128,16,256]{2,1,0:T(8,128)(2,1)S(1)}, u32[]{:S(2)}, u32[]{:S(2)}) %all-to-all-start.5) | async-done | bytes 1048608 | tf_op jit(solution)/shard_map/all_to_all | solution.py:392
  208.8 0.0 copy-done.6
  208.8 0.9 copy-done.10
  209.7 0.9 copy-done.16
  210.6 10.3 %finish.1 = (bf16[256,8,256]{2,1,0:T(8,128)(2,1)}, bf16[64,8,128]{2,1,0:T(8,128)(2,1)}) custom-call(bf16[256,8,256]{2,1,0:T(8,128)(2,1)S(1)} %copy-done.6, bf16[16,8,4,8,128]{4,3,2,1,0:T(8,128)(2,1)S(1)} %bitcast.17, f32[256,1]{1,0:T(8,128)S(1)} %copy.44.flags_ref, bf16[16,8,16,256]{3,2,1,0:T(8,128)(2,1)S(1)} %bitcast.18, bf16[256,256]{1,0:T(8,128)(2,1)S(1)} %copy-done.14, ...), custom_call_target="tpu_custom_call" | custom-call | flops 3000000000 | bytes 5000000 | tf_op jit(solution)/shard_map/finish/pallas_call | solution.py:358
  (9 shorter events, 0.0 us)
Async XLA Ops:
  7.2 48.9 %copy-start.11 = (bf16[256,256]{1,0:T(8,128)(2,1)S(1)}, bf16[256,256]{1,0:T(8,128)(2,1)}, u32[]{:S(2)}) copy-start(bf16[256,256]{1,0:T(8,128)(2,1)} %wq_ref.1) | copy-start | bytes 393220
  7.2 64.6 %all-gather.3.cloned.1.call-start = ((), (), s32[]{:S(2)}) async-start(), calls=%async_computation.6 | async-start | bytes 2785280 | tf_op jit(solution)/shard_map/all_gather | solution.py:416
  9.0 1.6 copy-start.4
  10.6 18.7 %copy-start.5 = (bf16[256,8,256]{2,1,0:T(8,128)(2,1)S(1)}, bf16[256,8,256]{2,1,0:T(8,128)(2,1)}, u32[]{:S(2)}) copy-start(bf16[256,8,256]{2,1,0:T(8,128)(2,1)} %x_ref.1) | copy-start | bytes 3145732
  10.6 45.5 %copy-start.12 = (bf16[256,256]{1,0:T(8,128)(2,1)S(1)}, bf16[256,256]{1,0:T(8,128)(2,1)}, u32[]{:S(2)}) copy-start(bf16[256,256]{1,0:T(8,128)(2,1)} %wk_ref.1) | copy-start | bytes 393220
  10.6 45.5 %copy-start.13 = (bf16[256,256]{1,0:T(8,128)(2,1)S(1)}, bf16[256,256]{1,0:T(8,128)(2,1)}, u32[]{:S(2)}) copy-start(bf16[256,256]{1,0:T(8,128)(2,1)} %wv_ref.1) | copy-start | bytes 393220
  62.3 1.6 copy-start.1
  63.9 1.0 copy-start.7
  64.9 40.9 %all-to-all-start.1 = ((bf16[8,3,4,16,8,128]{5,4,3,2,1,0:T(8,128)(2,1)}), bf16[8,3,4,16,8,128]{5,4,3,2,1,0:T(8,128)(2,1)S(1)}, u32[]{:S(2)}, u32[]{:S(2)}) async-start(bf16[8,3,4,16,8,128]{5,4,3,2,1,0:T(8,128)(2,1)} %copy-done.1), calls=%async_computation.1 | async-start | bytes 6291456 | tf_op jit(solution)/shard_map/all_to_all | solution.py:392
  105.8 1.7 copy-start.2
  107.6 6.2 %copy-start = (bf16[8,3,4,16,8,128]{5,4,3,2,1,0:T(8,128)(2,1)}, bf16[8,3,4,16,8,128]{5,4,3,2,1,0:T(8,128)(2,1)S(1)}, u32[]{:S(2)}) copy-start(bf16[8,3,4,16,8,128]{5,4,3,2,1,0:T(8,128)(2,1)S(1)} %all-to-all-done.1.q_ref.k_ref.v_ref) | copy-start | bytes 9437188
  113.8 44.8 %all-to-all-start.4 = ((bf16[8,4,8,128]{3,2,1,0:T(8,128)(2,1)}), bf16[8,4,8,128]{3,2,1,0:T(8,128)(2,1)S(1)}, u32[]{:S(2)}, u32[]{:S(2)}) async-start(bf16[8,4,8,128]{3,2,1,0:T(8,128)(2,1)} %slab_attention.1), calls=%async_computation.4 | async-start | bytes 131072 | tf_op jit(solution)/shard_map/all_to_all | solution.py:392
  119.0 1.7 copy-start.3
  120.7 47.0 %copy-start.19 = (s32[256]{0:T(256)S(1)}, s32[256]{0:T(256)}, u32[]{:S(2)}) copy-start(s32[256]{0:T(256)} %param.16) | copy-start | bytes 3076
  120.7 47.2 %copy-start.17 = (bf16[256,32]{0,1:T(8,128)(2,1)S(1)}, bf16[256,32]{0,1:T(8,128)(2,1)}, u32[]{:S(2)}) copy-start(bf16[256,32]{0,1:T(8,128)(2,1)} %param.25) | copy-start | bytes 49156
  120.8 47.3 %copy-start.8 = (bf16[256,8,256]{2,1,0:T(8,128)(2,1)S(1)}, bf16[256,8,256]{2,1,0:T(8,128)(2,1)}, u32[]{:S(2)}) copy-start(bf16[256,8,256]{2,1,0:T(8,128)(2,1)} %copy-done.7) | copy-start | bytes 3145732
  120.8 47.3 %copy-start.14 = (bf16[256,256]{1,0:T(8,128)(2,1)S(1)}, bf16[256,256]{1,0:T(8,128)(2,1)}, u32[]{:S(2)}) copy-start(bf16[256,256]{1,0:T(8,128)(2,1)} %gate_ref.3) | copy-start | bytes 393220
  158.6 26.9 %all-to-all-start.3 = ((bf16[128,4,8,128]{3,2,1,0:T(8,128)(2,1)}), bf16[128,4,8,128]{3,2,1,0:T(8,128)(2,1)S(1)}, u32[]{:S(2)}, u32[]{:S(2)}) async-start(bf16[128,4,8,128]{3,2,1,0:T(8,128)(2,1)} %attention.1), calls=%async_computation.3 | async-start | bytes 2097152 | tf_op jit(solution)/shard_map/all_to_all | solution.py:392
  168.1 0.9 copy-start.15
  169.0 22.2 %copy-start.18 = (bf16[256,32]{0,1:T(8,128)(2,1)S(1)}, bf16[256,32]{0,1:T(8,128)(2,1)}, u32[]{:S(2)}) copy-start(bf16[256,32]{0,1:T(8,128)(2,1)} %param.26) | copy-start | bytes 49156
  169.0 39.8 %copy-start.6 = (bf16[256,8,256]{2,1,0:T(8,128)(2,1)S(1)}, bf16[256,8,256]{2,1,0:T(8,128)(2,1)}, u32[]{:S(2)}) copy-start(bf16[256,8,256]{2,1,0:T(8,128)(2,1)} %x_ref.1) | copy-start | bytes 3145732
  171.1 1.0 copy-start.9
  185.4 23.3 %all-to-all-start.5 = ((bf16[128,16,256]{2,1,0:T(8,128)(2,1)}), bf16[128,16,256]{2,1,0:T(8,128)(2,1)S(1)}, u32[]{:S(2)}, u32[]{:S(2)}) async-start(bf16[128,16,256]{2,1,0:T(8,128)(2,1)} %copy-done.9), calls=%async_computation.5 | async-start | bytes 2097152 | tf_op jit(solution)/shard_map/all_to_all | solution.py:392
  208.8 1.0 copy-start.10
  209.7 0.9 copy-start.16
Sparse Core Ops, SparseCore 0:
  29.4 42.3 all-gather.2

commit v2 on v1

v2 whole, which is shorter than its diff:
```python
import functools

import jax
import jax.numpy as jnp
from jax import lax
from jax.experimental import pallas as pl
from jax.experimental.pallas import tpu as pltpu
from jax.sharding import PartitionSpec as P

LOG2E = 1.4426950408889634
MASKED = -1e9 * LOG2E
ROW = ("xl", "y", "core")
COL = ("xh", "z")
BOTH = ROW + COL
BLOCK, UNROLL = 256, 4
NT = (((1,), (1,)), ((), ()))
TN = (((0,), (0,)), ((), ()))


def dot(a, b, dims=None):
    if dims is None:
        return jnp.dot(a, b, preferred_element_type=jnp.float32)
    return lax.dot_general(a, b, dims, preferred_element_type=jnp.float32)


def params(mib=60):
    return pltpu.CompilerParams(vmem_limit_bytes=mib << 20)


def cost(flops, moved, exps=0):
    return pl.CostEstimate(flops=flops, bytes_accessed=moved, transcendentals=exps)


def standardize(x):
    mean = jnp.mean(x, axis=-1, keepdims=True)
    centred = x - mean
    var = jnp.mean(centred * centred, axis=-1, keepdims=True)
    return centred * lax.rsqrt(var + 1e-05)


def iota(shape, dim):
    return lax.broadcasted_iota(jnp.int32, shape, dim)


def spread_columns(w):
    row, col = iota((256, 1024), 0), iota((256, 1024), 1)
    pick = (row == (col // 128) * 32 + col % 32).astype(jnp.bfloat16)
    wide = dot(w, pick).astype(jnp.bfloat16)
    quarter = (col // 32) % 4
    return [jnp.where(quarter == si, wide, jnp.zeros_like(wide)) for si in range(4)]


def spread_rows(w):
    row, col = iota((1024, 256), 0), iota((1024, 256), 1)
    pick = (col == (row // 128) * 32 + row % 32).astype(jnp.bfloat16)
    tall = dot(pick, w).astype(jnp.bfloat16)
    quarter = (row // 32) % 4
    return [jnp.where(quarter == si, tall, jnp.zeros_like(tall)) for si in range(4)]


def factor_columns(w, residue):
    row, col = iota((32, 256), 0), iota((32, 256), 1)
    pick = jnp.where((row == col // 8) & (col % 8 == residue), 1.0, 0.0).astype(jnp.bfloat16)
    return dot(w, pick).astype(jnp.bfloat16)


def right_columns(w, residue):
    row, col = iota((32, 256), 0), iota((32, 256), 1)
    pick = jnp.where((row == col % 32) & (col // 32 == residue), 1.0, 0.0).astype(jnp.bfloat16)
    return dot(w, pick).astype(jnp.bfloat16)


def four_abreast(x):
    groups, width = x.shape[0], x.shape[3]
    return jnp.concatenate([x[:, si].reshape(groups * 8, width) for si in range(4)], axis=1)


def bias_kernel(duo_ref, w_ref, flags_ref, out_ref, rows_s):
    step = pl.program_id(0)

    @pl.when(step < 4)
    def _():
        x = duo_ref[...].reshape(16 * 128, 128).astype(jnp.float32)
        n = standardize(x).astype(jnp.bfloat16)
        heads = lax.dot_general(
            w_ref[...], n, (((0,), (1,)), ((), ())), preferred_element_type=jnp.float32
        )
        for i in range(16):
            rows_s[:, i, :] = heads[:, i * 128 : (i + 1) * 128] * LOG2E
        out_ref[...] = jnp.broadcast_to(rows_s[...].astype(jnp.bfloat16)[None], (2, 8, 16, 128))

    @pl.when(step == 4)
    def _():
        out_ref[...] = jnp.broadcast_to(flags_ref[...][None, None], (2, 8, 16, 128))


def bias_tile(duo, w, flags):
    return pl.pallas_call(
        bias_kernel,
        grid=(5,),
        in_specs=[
            pl.BlockSpec((16, 128, 128), lambda i: (jnp.minimum(i, 3), 0, 0)),
            pl.BlockSpec((128, 8), lambda i: (0, 0)),
            pl.BlockSpec((16, 128), lambda i: (0, 0)),
        ],
        out_specs=pl.BlockSpec((2, 8, 16, 128), lambda i: (0, 0, i, 0)),
        out_shape=jax.ShapeDtypeStruct((2, 8, 80, 128), jnp.bfloat16),
        scratch_shapes=[pltpu.VMEM((8, 16, 128), jnp.float32)],
        compiler_params=params(),
        cost_estimate=cost(20_000_000, 2_200_000),
        name="bias_tile",
    )(duo, w, flags)


def qkv_kernel(x_ref, wq_ref, wk_ref, wv_ref, early_ref, late_ref, w_s):
    @pl.when(pl.program_id(0) == 0)
    def _():
        for t, w in enumerate((wq_ref, wk_ref, wv_ref)):
            for si, part in enumerate(spread_columns(w[...])):
                w_s[t, si * 256 : (si + 1) * 256, :] = part

    x = x_ref[...].reshape(16, 4, 8, 256).astype(jnp.float32)
    n = four_abreast(standardize(x)).astype(jnp.bfloat16)
    for t in range(3):
        y = dot(n, w_s[t])
        if t == 0:
            y = y * (LOG2E / 32**0.5)
        y = y.reshape(4, 4, 8, 1024)
        for h in range(8):
            for g in range(4):
                out_ref = early_ref if g < 2 else late_ref
                out_ref[h, t, g % 2] = y[:, g, :, h * 128 : (h + 1) * 128].astype(jnp.bfloat16)


def qkv(x, wq, wk, wv):
    whole = pl.BlockSpec((256, 256), lambda i: (0, 0))
    return pl.pallas_call(
        qkv_kernel,
        grid=(4,),
        in_specs=[
            pl.BlockSpec((4, 4, 4, 8, 256), lambda i: (i, 0, 0, 0, 0)),
            whole,
            whole,
            whole,
        ],
        out_specs=[pl.BlockSpec((8, 3, 2, 4, 8, 128), lambda i: (0, 0, 0, i, 0, 0))] * 2,
        out_shape=[jax.ShapeDtypeStruct((8, 3, 2, 16, 8, 128), jnp.bfloat16)] * 2,
        scratch_shapes=[pltpu.VMEM((3, 1024, 1024), jnp.bfloat16)],
        compiler_params=params(),
        cost_estimate=cost(3_500_000_000, 4_500_000),
        name="qkv",
    )(x, wq, wk, wv)


def natural(block):
    x = jnp.swapaxes(block.astype(jnp.float32), 0, 1)
    return x.reshape(x.shape[0] * 64, 128).astype(jnp.bfloat16)


def bias_tile_at(bias_ref, r, c):
    if bias_ref.shape[0] == 1:
        return bias_ref[0, 0, c, :64, :]
    return bias_ref[lax.rem(r, 8), lax.div(r, 8), c, :64, :]


def attend(block, blocks, q_ref, k_ref, v_ref, bias_ref, present, out_ref, q_s, k_s, v_s):
    lane = iota((1, 128), 1) // 32
    wide_lane = (iota((1, 256), 1) // 32) % 4
    q_s[...] = natural(q_ref[:, 0, 0])
    k_s[...] = natural(k_ref[:, 0, 0])
    v_s[:, :128] = natural(v_ref[:, 0, 0])

    @pl.when(pl.program_id(0) == 0)
    def _():
        v_s[:, 128:] = jnp.ones((1024, 128), jnp.bfloat16)

    tiles = block // 64

    def step(at, carry):
        rows = pl.ds(pl.multiple_of(at * block, block), block)
        q = q_s[rows, :]
        bias = jnp.concatenate(
            [
                jnp.concatenate([bias_tile_at(bias_ref, at * tiles + t, c) for c in range(8)], 1)
                for t in range(tiles)
            ],
            0,
        ).astype(jnp.float32)
        ones = [jnp.where(lane == si, q, jnp.zeros_like(q)) for si in range(4)]

        def probs(score, si):
            score = jnp.where(present[si : si + 1] > 0, score + bias, MASKED)
            top = jnp.max(score, axis=1, keepdims=True)
            return jnp.exp2(score - top).astype(jnp.bfloat16)

        if block > 64:
            parts = [dot(probs(dot(ones[si], k_s[...], NT), si), v_s[...]) for si in range(4)]
        else:
            scores = dot(jnp.concatenate(ones, 0), k_s[...], NT)
            parts = [probs(scores[si * block : (si + 1) * block], si) for si in range(4)]
            parts = dot(jnp.concatenate(parts, 0), v_s[...])
            parts = [parts[si * block : (si + 1) * block] for si in range(4)]
        total = parts[0]
        for si in range(1, 4):
            total = jnp.where(wide_lane == si, parts[si], total)
        result = total[:, :128] / total[:, 128:]
        eighth = block // 8
        out_ref[pl.ds(pl.multiple_of(at * eighth, eighth), eighth), 0, 0] = result.reshape(
            eighth, 8, 128
        ).astype(jnp.bfloat16)
        return carry

    lax.fori_loop(0, blocks, step, 0, unroll=min(UNROLL, blocks))


def first_kernel(
    at_ref, q_ref, k_ref, v_ref, bias_ref, flags_ref, out_ref, slab_ref, mask_ref, *scratch
):
    @pl.when(pl.program_id(0) == 0)
    def _():
        both = flags_ref[...].astype(jnp.float32)
        flags = jnp.where(at_ref[1] // 8 == 0, both[..., :8, :], both[..., 8:, :])
        flags = jnp.swapaxes(flags, 0, 1)
        own = iota((16, 128), 1) == (at_ref[1] % 8) * 16 + iota((16, 128), 0)
        mask = dot(own.astype(jnp.bfloat16), flags.reshape(1024, 128).astype(jnp.bfloat16), NT)
        for g in range(4):
            mask_ref[g] = mask[g * 4 : g * 4 + 4]

    present = mask_ref[pl.program_id(0)]
    attend(BLOCK, 1024 // BLOCK, q_ref, k_ref, v_ref, bias_ref, present, out_ref, *scratch)
    slab_ref[:, 0, 0] = out_ref[pl.ds(pl.multiple_of(at_ref[0] * 8, 8), 8), 0, 0]


def slab_kernel(at_ref, q_ref, k_ref, v_ref, bias_ref, mask_ref, _, out_ref, *scratch):
    attend(64, 1, q_ref, k_ref, v_ref, bias_ref, mask_ref[0], out_ref, *scratch)


def later_kernel(q_ref, k_ref, v_ref, bias_ref, mask_ref, *rest):
    attend(BLOCK, 1024 // BLOCK, q_ref, k_ref, v_ref, bias_ref, mask_ref[0], *rest[-4:])


def attention_scratch(rows):
    return [
        pltpu.VMEM((rows, 128), jnp.bfloat16),
        pltpu.VMEM((1024, 128), jnp.bfloat16),
        pltpu.VMEM((1024, 256), jnp.bfloat16),
    ]


RETURNED = jax.ShapeDtypeStruct((128, 2, 4, 8, 128), jnp.bfloat16)
SLAB_WEIGHTED = jax.ShapeDtypeStruct((8, 1, 4, 8, 128), jnp.bfloat16)


def first_attention(at, received, bias):
    part = lambda t: pl.BlockSpec((8, 1, 1, 16, 8, 128), lambda g, s: (0, t, g, 0, 0, 0))
    return pl.pallas_call(
        first_kernel,
        grid_spec=pltpu.PrefetchScalarGridSpec(
            num_scalar_prefetch=1,
            grid=(2,),
            in_specs=[
                part(0),
                part(1),
                part(2),
                pl.BlockSpec((8, 2, 8, 80, 128), lambda g, s: (0, 0, 0, 0, 0)),
                pl.BlockSpec((8, 2, 8, 16, 128), lambda g, s: (0, 0, 0, 4, 0)),
            ],
            out_specs=[
                pl.BlockSpec((128, 1, 1, 8, 128), lambda g, s: (0, 0, g, 0, 0)),
                pl.BlockSpec((8, 1, 1, 8, 128), lambda g, s: (0, 0, g, 0, 0)),
                pl.BlockSpec((4, 4, 1024), lambda g, s: (0, 0, 0)),
            ],
            scratch_shapes=attention_scratch(1024),
        ),
        out_shape=[RETURNED, SLAB_WEIGHTED, jax.ShapeDtypeStruct((4, 4, 1024), jnp.float32)],
        compiler_params=params(),
        cost_estimate=cost(16_000_000_000, 4_000_000, 2 << 22),
        name="first_attention",
    )(at, received, received, received, bias, bias)


def slab_attention(at, received, bias, mask, onto):
    part = lambda t: pl.BlockSpec((8, 1, 1, 16, 8, 128), lambda g, s: (0, t, g, 0, 0, 0))
    return pl.pallas_call(
        slab_kernel,
        grid_spec=pltpu.PrefetchScalarGridSpec(
            num_scalar_prefetch=1,
            grid=(2,),
            in_specs=[
                pl.BlockSpec((8, 1, 1, 1, 8, 128), lambda g, s: (0, 0, g, s[0], 0, 0)),
                part(1),
                part(2),
                pl.BlockSpec(
                    (1, 1, 8, 80, 128), lambda g, s: (lax.rem(s[0], 8), lax.div(s[0], 8), 0, 0, 0)
                ),
                pl.BlockSpec((1, 4, 1024), lambda g, s: (g + 2, 0, 0)),
                pl.BlockSpec(memory_space=pl.ANY),
            ],
            out_specs=pl.BlockSpec((8, 1, 1, 8, 128), lambda g, s: (0, 0, g + 2, 0, 0)),
            scratch_shapes=attention_scratch(64),
        ),
        out_shape=SLAB_WEIGHTED,
        input_output_aliases={6: 0},
        compiler_params=params(),
        cost_estimate=cost(1_000_000_000, 2_000_000, 1 << 19),
        name="slab_attention",
    )(at, received, received, received, bias, mask, onto)


def later_attention(received, bias, mask, onto):
    part = lambda t: pl.BlockSpec((8, 1, 1, 16, 8, 128), lambda g: (0, t, g, 0, 0, 0))
    return pl.pallas_call(
        later_kernel,
        grid=(2,),
        in_specs=[
            part(0),
            part(1),
            part(2),
            pl.BlockSpec((8, 2, 8, 80, 128), lambda g: (0, 0, 0, 0, 0)),
            pl.BlockSpec((1, 4, 1024), lambda g: (g + 2, 0, 0)),
            pl.BlockSpec(memory_space=pl.ANY),
        ],
        out_specs=pl.BlockSpec((128, 1, 1, 8, 128), lambda g: (0, 0, g + 2, 0, 0)),
        out_shape=RETURNED,
        scratch_shapes=attention_scratch(1024),
        input_output_aliases={5: 0},
        compiler_params=params(),
        cost_estimate=cost(16_000_000_000, 4_000_000, 2 << 22),
        name="later_attention",
    )(received, received, received, bias, mask, onto)


def gates(x, w):
    return jax.nn.sigmoid(dot(four_abreast(standardize(x)).astype(jnp.bfloat16), w))


def prepare_kernel(
    at_ref, x_ref, slab_ref, gate_ref, out_w_ref, gates_ref, slab_gates_ref, spread_ref, w_s
):
    @pl.when(pl.program_id(0) == 0)
    def _():
        for si, part in enumerate(spread_columns(gate_ref[...])):
            w_s[si * 256 : (si + 1) * 256, :] = part
        for si, part in enumerate(spread_rows(out_w_ref[...])):
            spread_ref[:, si * 256 : (si + 1) * 256] = part
        slab_gates_ref[...] = gates(slab_ref[0].astype(jnp.float32), w_s[...])

    x = x_ref[...].reshape(16, 4, 8, 256).astype(jnp.float32)
    gates_ref[...] = gates(x, w_s[...]).astype(jnp.bfloat16)


def prepare(at, x, sequences, w_gate, w_out):
    whole = lambda *shape: pl.BlockSpec(shape, lambda i, s: (0,) * len(shape))
    return pl.pallas_call(
        prepare_kernel,
        grid_spec=pltpu.PrefetchScalarGridSpec(
            num_scalar_prefetch=1,
            grid=(4,),
            in_specs=[
                pl.BlockSpec((64, 8, 256), lambda i, s: (i, 0, 0)),
                pl.BlockSpec((1, 4, 4, 8, 256), lambda i, s: (s[0], 0, 0, 0, 0)),
                whole(256, 256),
                whole(256, 256),
            ],
            out_specs=[
                pl.BlockSpec((128, 1024), lambda i, s: (i, 0)),
                whole(32, 1024),
                whole(1024, 1024),
            ],
            scratch_shapes=[pltpu.VMEM((1024, 1024), jnp.bfloat16)],
        ),
        out_shape=[
            jax.ShapeDtypeStruct((512, 1024), jnp.bfloat16),
            jax.ShapeDtypeStruct((32, 1024), jnp.float32),
            jax.ShapeDtypeStruct((1024, 1024), jnp.bfloat16),
        ],
        compiler_params=params(),
        cost_estimate=cost(1_500_000_000, 6_000_000),
        name="prepare",
    )(at, x, sequences, w_gate, w_out)


def gated_update(x, gate, weighted, w_out):
    gated = (gate * weighted).astype(jnp.bfloat16)
    update = dot(gated, w_out)
    fresh = x + jnp.stack(
        [update[:, si * 256 : (si + 1) * 256].reshape(-1, 8, 256) for si in range(4)], axis=1
    )
    return fresh.astype(jnp.bfloat16).astype(jnp.float32)


def left_kernel(
    at_ref, x_ref, weighted_ref, flags_ref, gate_ref, out_w_ref, factor_ref, _, out_ref, normed_s
):
    x = x_ref[0].astype(jnp.float32)
    weighted = jnp.concatenate(
        [weighted_ref[h, 0].astype(jnp.float32).reshape(32, 128) for h in range(8)], axis=1
    )
    fresh = gated_update(x, gate_ref[...], weighted, out_w_ref[...])
    normed_s[...] = standardize(fresh).reshape(16, 8, 256)
    left = jnp.zeros((16, 256), jnp.float32)
    for residue in range(8):
        part = normed_s[:, residue, :].astype(jnp.bfloat16)
        left = left + dot(part, factor_columns(factor_ref[...], residue))
    left = left * flags_ref[...]
    for half in range(2):
        part = left[:, half * 128 : (half + 1) * 128].reshape(1, 2, 8, 128).astype(jnp.bfloat16)
        out_ref[:, 0, 2 * half : 2 * half + 2] = jnp.broadcast_to(part, (128, 2, 8, 128))


def left_factor(at, x, weighted, flags, gate, w_out, w_first, onto):
    whole = lambda *shape: pl.BlockSpec(shape, lambda i, s: (0,) * len(shape))
    return pl.pallas_call(
        left_kernel,
        grid_spec=pltpu.PrefetchScalarGridSpec(
            num_scalar_prefetch=1,
            grid=(1,),
            in_specs=[
                pl.BlockSpec((1, 4, 4, 8, 256), lambda i, s: (s[0], 0, 0, 0, 0)),
                whole(8, 1, 4, 8, 128),
                whole(16, 1),
                whole(32, 1024),
                whole(1024, 1024),
                whole(256, 32),
                pl.BlockSpec(memory_space=pl.ANY),
            ],
            out_specs=pl.BlockSpec((128, 1, 4, 8, 128), lambda i, s: (0, 1, 0, 0, 0)),
            scratch_shapes=[pltpu.VMEM((16, 8, 256), jnp.float32)],
        ),
        out_shape=RETURNED,
        input_output_aliases={7: 0},
        compiler_params=params(),
        cost_estimate=cost(100_000_000, 3_500_000),
        name="left_factor",
    )(at, x, weighted, flags, gate, w_out, w_first, onto)


def final_kernel(
    x_ref, weighted_ref, flags_ref, left_ref, gate_ref, out_w_ref, factor_ref, product_ref,
    fresh_ref, pair_ref, factor_s, normed_s, right_s, outer_s, pair_s,
):
    step = pl.program_id(0)

    @pl.when(step == 0)
    def _():
        for residue in range(8):
            factor_s[residue] = right_columns(factor_ref[...], residue)

    x = x_ref[...].reshape(16, 4, 8, 256).astype(jnp.float32)
    weighted = jnp.concatenate(
        [
            weighted_ref[:, h, 0].astype(jnp.float32).reshape(128, 128)
            for h in range(8)
        ],
        axis=1,
    )
    fresh = gated_update(x, gate_ref[...].astype(jnp.float32), weighted, out_w_ref[...])
    fresh_ref[...] = fresh.reshape(64, 8, 256).astype(jnp.bfloat16)
    normed_s[...] = standardize(fresh).reshape(64, 8, 256)
    right = jnp.zeros((64, 256), jnp.float32)
    for residue in range(8):
        part = normed_s[:, residue, :].astype(jnp.bfloat16)
        right = right + dot(part, factor_s[residue])
    right_s[pl.ds(pl.multiple_of(step * 64, 64), 64), :] = (right * flags_ref[...]).astype(
        jnp.bfloat16
    )

    @pl.when(step == pl.num_programs(0) - 1)
    def _():
        right_all = right_s[...]
        for c in range(8):
            left = left_ref[:, c, 0].astype(jnp.float32)
            left = jnp.concatenate(
                [left[:, :2].reshape(256, 128), left[:, 2:].reshape(256, 128)], axis=1
            ).astype(jnp.bfloat16)
            outer_s[:, c] = (dot(left, right_all, TN) * (1.0 / 256)).reshape(32, 8, 256)
        lane = iota((1, 128), 1) // 32
        for j in range(8):
            half, source = (j // 4) * 128, j % 4
            quads = []
            for quad in range(8):
                block = None
                for u in range(4):
                    part = outer_s[quad * 4 + u, :, :, half : half + 128].reshape(64, 128)
                    if u != source:
                        part = pltpu.roll(part, ((u - source) % 4) * 32, 1)
                    block = part if block is None else jnp.where(lane == u, part, block)
                quads.append(block.astype(jnp.bfloat16))
            pair_s[:, j, :] = dot(jnp.concatenate(quads, axis=1), product_ref[...])
        pair_ref[...] = pair_s[...].astype(jnp.bfloat16)


def finish(x, returned, flags, gate, w_out, w_second, w_product):
    whole = lambda *shape: pl.BlockSpec(shape, lambda i: (0,) * len(shape))
    return pl.pallas_call(
        final_kernel,
        grid=(4,),
        in_specs=[
            pl.BlockSpec((64, 8, 256), lambda i: (i, 0, 0)),
            pl.BlockSpec((4, 8, 1, 4, 8, 128), lambda i: (i, 0, 0, 0, 0, 0)),
            pl.BlockSpec((64, 1), lambda i: (i, 0)),
            pl.BlockSpec((16, 8, 1, 4, 8, 128), lambda i: (0, 0, 1, 0, 0, 0)),
            pl.BlockSpec((128, 1024), lambda i: (i, 0)),
            whole(1024, 1024),
            whole(256, 32),
            whole(1024, 128),
        ],
        out_specs=[pl.BlockSpec((64, 8, 256), lambda i: (i, 0, 0)), whole(64, 8, 128)],
        out_shape=[
            jax.ShapeDtypeStruct((256, 8, 256), jnp.bfloat16),
            jax.ShapeDtypeStruct((64, 8, 128), jnp.bfloat16),
        ],
        scratch_shapes=[
            pltpu.VMEM((8, 256, 256), jnp.bfloat16),
            pltpu.VMEM((64, 8, 256), jnp.float32),
            pltpu.VMEM((256, 256), jnp.bfloat16),
            pltpu.VMEM((32, 8, 8, 256), jnp.float32),
            pltpu.VMEM((64, 8, 128), jnp.float32),
        ],
        compiler_params=params(),
        cost_estimate=cost(3_000_000_000, 5_000_000),
        name="finish",
    )(x, returned, flags, returned, gate, w_out, w_second, w_product)


def exchange(x, axes):
    return lax.all_to_all(x, axes, split_axis=0, concat_axis=0, tiled=True)


def per_device(
    alignment_tensor,
    amino_exists_flags,
    chain_exists_flags,
    chosen_slab_number,
    duo_tensor,
    duo_offset_matrix,
    asking_matrix,
    lookup_matrix,
    content_matrix,
    sigmoid_matrix,
    final_projection_matrix,
    first_factor_matrix,
    second_factor_matrix,
    product_to_duo_matrix,
):
    row = lax.axis_index(ROW)
    at = jnp.concatenate([chosen_slab_number, jnp.reshape(row, (1,)).astype(jnp.int32)])
    sequences = exchange(alignment_tensor, ROW).reshape(16, 4, 4, 8, 256)

    flags = jnp.transpose(amino_exists_flags.reshape(2, 128, 8), (0, 2, 1))
    flags = flags.reshape(16, 128).astype(jnp.bfloat16)
    tile = bias_tile(duo_tensor, duo_offset_matrix, flags)
    sequences, tile = lax.optimization_barrier((sequences, tile))
    tile = exchange(tile.reshape(16, 80, 128), ("xl",) + COL)
    early, late = qkv(sequences, asking_matrix, lookup_matrix, content_matrix)
    early, late, tile = lax.optimization_barrier((early, late, tile))
    bias = lax.all_gather(tile.reshape(2, 8, 80, 128), ("y", "core"), axis=0, tiled=False)
    early = exchange(early, COL)
    late, early = lax.optimization_barrier((late, early))
    late = exchange(late, COL)

    chains = chain_exists_flags.astype(jnp.float32)[:, None]
    own_chains = lax.dynamic_slice_in_dim(chains, row * 16, 16, 0)
    gate, slab_gate, w_out = prepare(
        at, alignment_tensor, sequences, sigmoid_matrix, final_projection_matrix
    )

    early, gate, slab_gate, w_out = lax.optimization_barrier((early, gate, slab_gate, w_out))
    returned, slab_weighted, mask = first_attention(at, early, bias)
    slab_weighted = slab_attention(at, late, bias, mask, slab_weighted)
    slab_weighted = exchange(slab_weighted, COL)
    returned = later_attention(late, bias, mask, returned)
    slab_weighted, returned = lax.optimization_barrier((slab_weighted, returned))
    returned = left_factor(
        at, sequences, slab_weighted, own_chains, slab_gate, w_out, first_factor_matrix, returned
    )
    returned = exchange(returned, BOTH)
    return tuple(
        finish(
            alignment_tensor,
            returned.reshape(16, 8, 2, 4, 8, 128),
            chains,
            gate,
            w_out,
            second_factor_matrix,
            product_to_duo_matrix,
        )
    )


def solution(mesh):
    mesh = jax.sharding.Mesh(mesh.devices.reshape(2, 4, 2, 2, 4), BOTH)
    placed = (
        P(None, BOTH, None),
        P(None, BOTH),
        P(),
        P(),
        P(ROW, COL, None),
    ) + (P(),) * 9
    return jax.shard_map(
        per_device,
        mesh=mesh,
        in_specs=placed,
        out_specs=(P(None, BOTH, None), P(None, BOTH, None)),
        check_vma=False,
    )
```

time: 229 us -> 188 us (0.82)
  blocking collectives: 42.1 us -> 0 us
  starting transfers between devices: 23.7 us -> 41.4 us
  local copies, waits for them, and re-layouts: 18.2 us -> 7.7 us
  waiting for transfers between devices: 61.2 us -> 50.7 us
  Pallas kernels: 66 us -> 71.3 us
    all_to_all x2 -> x0, blocking collectives: 42.1 us -> none  [exchange(): return lax.all_to_all(x, axes, split_axis=0, concat_axis=0, tiled=True)]
    all_to_all x4 -> x6, starting transfers between devices: 23.6 us -> 41.4 us  [exchange(): return lax.all_to_all(x, axes, split_axis=0, concat_axis=0, tiled=True)]
    all_to_all x4 -> x6, waiting for transfers between devices: 58.6 us -> 50.7 us  [exchange(): return lax.all_to_all(x, axes, split_axis=0, concat_axis=0, tiled=True)]
    unnamed x43 -> x25, local copies, waits for them, and re-layouts: 12.5 us -> 6.16 us
    convert_element_type x4 -> x0, local copies, waits for them, and re-layouts: 5.28 us -> none  [the longest x3 5.15 us: per_device(): mask = mask.reshape(4, 4, 1024).astype(jnp.float32)]
    pallas_call x1, Pallas kernels: 2.15 us -> 5.07 us  [left_factor(): pl.pallas_call(left_kernel, grid_spec=pltpu.PrefetchScalarGridSpec(num_sc...]
    all_gather x1, waiting for transfers between devices: 2.62 us -> 0.01 us  [per_device(): lax.all_gather(tile.reshape(2, 8, 80, 128), ('y', 'core'), axis=0, tiled=...]
    pallas_call x2 -> x4, Pallas kernels: 44 us -> 42.6 us  [the longest x1 16.2 us: first_attention(): pl.pallas_call(first_kernel, grid_spec=pltpu.PrefetchScalarGridSpec(num_s...]
  transfers between devices with their start and end apart: 5 -> 7, of which waited for: 4 -> 4; matrix products, arithmetic and copies ran while one was open for 3% -> 3% of each run, Pallas kernels for 20% -> 28%
where the time goes in v2:
time: 188 us; the launch traced here: 187 us
  Pallas kernels  71.3 us (38%)
  waiting for transfers between devices  50.7 us (27%)
  starting transfers between devices  41.4 us (22%)
  between operations  14.8 us (8%)
  local copies, waits for them, and re-layouts  7.7 us (4%)
    all_to_all x6, waiting for transfers between devices, exchange(): return lax.all_to_all(x, axes, split_axis=0, concat_axis=0, tiled=True)  50.7 us
    all_to_all x6, starting transfers between devices, exchange(): return lax.all_to_all(x, axes, split_axis=0, concat_axis=0, tiled=True)  41.4 us
    pallas_call x1, Pallas kernels, first_attention(): pl.pallas_call(first_kernel, grid_spec=pltpu.PrefetchScalarGridSpec(num_s...  16.2 us
    pallas_call x1, Pallas kernels, later_attention(): pl.pallas_call(later_kernel, grid=(2,), in_specs=[part(0), part(1), part(...  15.3 us
    pallas_call x1, Pallas kernels, finish(): pl.pallas_call(final_kernel, grid=(4,), in_specs=[pl.BlockSpec((64, 8, 25...  10.2 us
    pallas_call x1, Pallas kernels, qkv(): pl.pallas_call(qkv_kernel, grid=(4,), in_specs=[pl.BlockSpec((4, 4, 4, 8,...  8.12 us
    pallas_call x1, Pallas kernels, prepare(): pl.pallas_call(prepare_kernel, grid_spec=pltpu.PrefetchScalarGridSpec(num...  6.66 us
    unnamed x25, local copies, waits for them, and re-layouts  6.16 us
  transfers between devices with their start and end apart: 7, of which 4 were waited for; matrix products, arithmetic and copies ran while one was open for 3% of the time, Pallas kernels for 28%

profile of v2, /device:TPU:1, one launch (start us, length us, event | category | flops | bytes accessed | tf_op | source)
XLA Modules:
  0.0 187.1 jit_solution(13442431726464494888)
XLA Ops:
  7.2 0.0 copy-start.9
  7.2 0.0 copy-start.8
  7.2 7.1 %all-to-all-start = ((bf16[256,8,256]{2,1,0:T(8,128)(2,1)}), bf16[256,8,256]{2,1,0:T(8,128)(2,1)S(1)}, u32[]{:S(2)}, u32[]{:S(2)}) async-start(bf16[256,8,256]{2,1,0:T(8,128)(2,1)} %x_ref.3), calls=%async_computation | async-start | bytes 2097152 | tf_op jit(solution)/shard_map/all_to_all | solution.py:527
  14.2 0.0 copy-done.9
  14.2 0.7 copy.28.w_ref
  15.0 0.0 copy-done.8
  15.0 0.6 convert_bitcast_fusion.flags_ref
  15.6 5.3 %bias_tile.1 = bf16[2,8,80,128]{3,2,1,0:T(8,128)(2,1)} custom-call(bf16[64,128,128]{2,1,0:T(8,128)(2,1)} %duo_ref.1, bf16[128,8]{1,0:T(8,128)(2,1)} %copy.28.w_ref, bf16[16,128]{1,0:T(8,128)(2,1)} %convert_bitcast_fusion.flags_ref), custom_call_target="tpu_custom_call" | custom-call | flops 20000000 | bytes 2200000 | tf_op jit(solution)/shard_map/bias_tile/pallas_call | solution.py:98
  20.8 9.2 %all-to-all-done = bf16[256,8,256]{2,1,0:T(8,128)(2,1)S(1)} async-done(((bf16[256,8,256]{2,1,0:T(8,128)(2,1)}), bf16[256,8,256]{2,1,0:T(8,128)(2,1)S(1)}, u32[]{:S(2)}, u32[]{:S(2)}) %all-to-all-start) | async-done | bytes 1048608 | tf_op jit(solution)/shard_map/all_to_all | solution.py:527
  30.1 0.0 copy-start.1
  30.1 7.3 %all-to-all-start.1 = ((bf16[16,80,128]{2,1,0:T(8,128)(2,1)}), bf16[16,80,128]{2,1,0:T(8,128)(2,1)S(1)}, u32[]{:S(2)}, u32[]{:S(2)}) async-start(bf16[16,80,128]{2,1,0:T(8,128)(2,1)} %bitcast.19), calls=%async_computation.1 | async-start | bytes 655360 | tf_op jit(solution)/shard_map/all_to_all | solution.py:527
  37.4 0.0 all-gather.2.cloned.1.call-start
  37.4 0.0 copy-done.1
  37.4 8.1 %qkv.1 = (bf16[8,3,2,16,8,128]{5,4,3,2,1,0:T(8,128)(2,1)}, bf16[8,3,2,16,8,128]{5,4,3,2,1,0:T(8,128)(2,1)}) custom-call(bf16[16,4,4,8,256]{4,3,2,1,0:T(8,128)(2,1)} %bitcast.14, bf16[256,256]{1,0:T(8,128)(2,1)} %wq_ref.1, bf16[256,256]{1,0:T(8,128)(2,1)} %wk_ref.1, bf16[256,256]{1,0:T(8,128)(2,1)} %wv_ref.1), custom_call_target="tpu_custom_call" | custom-call | flops 3500000000 | bytes 4500000 | tf_op jit(solution)/shard_map/qkv/pallas_call | solution.py:137
  45.6 0.0 copy-start.10
  45.6 0.0 copy-start.6
  45.6 0.0 all-to-all-done.1
  45.6 0.0 copy-start.4
  45.6 0.7 copy-done.4
  46.3 0.0 all-gather.2.cloned.1.call-update
  46.4 6.6 %all-to-all-start.2 = ((bf16[8,3,2,16,8,128]{5,4,3,2,1,0:T(8,128)(2,1)}), bf16[8,3,2,16,8,128]{5,4,3,2,1,0:T(8,128)(2,1)S(1)}, u32[]{:S(2)}, u32[]{:S(2)}) async-start(bf16[8,3,2,16,8,128]{5,4,3,2,1,0:T(8,128)(2,1)} %get-tuple-element.28), calls=%async_computation.2 | async-start | bytes 3145728 | tf_op jit(solution)/shard_map/all_to_all | solution.py:527
  53.6 0.0 copy-done.10
  53.6 0.1 dynamic-slice_bitcast_fusion
  53.7 0.7 copy.29.flags_ref
  54.4 0.0 copy-done.6
  54.4 0.7 copy.30.factor_ref
  55.1 0.6 pad_add_fusion.at_ref
  55.7 6.7 %prepare.1 = (bf16[512,1024]{1,0:T(8,128)(2,1)}, f32[32,1024]{1,0:T(8,128)}, bf16[1024,1024]{1,0:T(8,128)(2,1)}) custom-call(s32[2]{0:T(128)} %pad_add_fusion.at_ref, bf16[256,8,256]{2,1,0:T(8,128)(2,1)} %x_ref.3, bf16[16,4,4,8,256]{4,3,2,1,0:T(8,128)(2,1)} %bitcast.15, bf16[256,256]{1,0:T(8,128)(2,1)} %gate_ref.1, bf16[256,256]{1,0:T(8,128)(2,1)} %out_w_ref.1), custom_call_target="tpu_custom_call" | custom-call | flops 1500000000 | bytes 6000000 | tf_op jit(solution)/shard_map/prepare/pallas_call | solution.py:354
  62.3 10.2 %all-to-all-done.2.q_ref.k_ref.v_ref = bf16[8,3,2,16,8,128]{5,4,3,2,1,0:T(8,128)(2,1)S(1)} async-done(((bf16[8,3,2,16,8,128]{5,4,3,2,1,0:T(8,128)(2,1)}), bf16[8,3,2,16,8,128]{5,4,3,2,1,0:T(8,128)(2,1)S(1)}, u32[]{:S(2)}, u32[]{:S(2)}) %all-to-all-start.2) | async-done | bytes 1572896 | tf_op jit(solution)/shard_map/all_to_all | solution.py:527
  72.5 0.0 copy-start.3
  72.5 6.2 %all-to-all-start.3 = ((bf16[8,3,2,16,8,128]{5,4,3,2,1,0:T(8,128)(2,1)}), bf16[8,3,2,16,8,128]{5,4,3,2,1,0:T(8,128)(2,1)S(1)}, u32[]{:S(2)}, u32[]{:S(2)}) async-start(bf16[8,3,2,16,8,128]{5,4,3,2,1,0:T(8,128)(2,1)} %get-tuple-element.29), calls=%async_computation.3 | async-start | bytes 3145728 | tf_op jit(solution)/shard_map/all_to_all | solution.py:527
  78.7 0.0 all-gather.2.cloned.1.call-done.bias_ref.flags_ref
  78.7 0.0 copy-done.3
  78.7 16.2 %first_attention.1 = (bf16[128,2,4,8,128]{4,3,2,1,0:T(8,128)(2,1)}, bf16[8,1,4,8,128]{4,3,2,1,0:T(8,128)(2,1)}, f32[4,4,1024]{2,1,0:T(4,128)}) custom-call(s32[2]{0:T(128)} %pad_add_fusion.at_ref, bf16[8,3,2,16,8,128]{5,4,3,2,1,0:T(8,128)(2,1)} %copy-done.3, bf16[8,3,2,16,8,128]{5,4,3,2,1,0:T(8,128)(2,1)} %copy-done.3, ...), custom_call_target="tpu_custom_call" | custom-call | flops 16000000000 | bytes 4000000 | tf_op jit(solution)/shard_map/first_attention/pallas_call | solution.py:256
  94.9 4.3 %all-to-all-done.3.q_ref.k_ref.v_ref = bf16[8,3,2,16,8,128]{5,4,3,2,1,0:T(8,128)(2,1)S(1)} async-done(((bf16[8,3,2,16,8,128]{5,4,3,2,1,0:T(8,128)(2,1)}), bf16[8,3,2,16,8,128]{5,4,3,2,1,0:T(8,128)(2,1)S(1)}, u32[]{:S(2)}, u32[]{:S(2)}) %all-to-all-start.3) | async-done | bytes 1572896 | tf_op jit(solution)/shard_map/all_to_all | solution.py:527
  99.2 0.0 copy-start
  99.2 1.2 copy-done
  100.5 4.4 %slab_attention.1 = bf16[8,1,4,8,128]{4,3,2,1,0:T(8,128)(2,1)} custom-call(s32[2]{0:T(128)} %pad_add_fusion.at_ref, bf16[8,3,2,16,8,128]{5,4,3,2,1,0:T(8,128)(2,1)} %copy-done, bf16[8,3,2,16,8,128]{5,4,3,2,1,0:T(8,128)(2,1)} %copy-done, bf16[8,3,2,16,8,128]{5,4,3,2,1,0:T(8,128)(2,1)} %copy-done, ...), custom_call_target="tpu_custom_call", output_to_operand_aliasing={{}: (6, {})} | custom-call | flops 1000000000 | bytes 2000000 | tf_op jit(solution)/shard_map/slab_attention/pallas_call | solution.py:284
  104.9 5.2 %all-to-all-start.4 = ((bf16[8,1,4,8,128]{4,3,2,1,0:T(8,128)(2,1)}), bf16[8,1,4,8,128]{4,3,2,1,0:T(8,128)(2,1)S(1)}, u32[]{:S(2)}, u32[]{:S(2)}) async-start(bf16[8,1,4,8,128]{4,3,2,1,0:T(8,128)(2,1)} %slab_attention.1), calls=%async_computation.4 | async-start | bytes 131072 | tf_op jit(solution)/shard_map/all_to_all | solution.py:527
  110.1 15.3 %later_attention.1._ = bf16[128,2,4,8,128]{4,3,2,1,0:T(8,128)(2,1)} custom-call(bf16[8,3,2,16,8,128]{5,4,3,2,1,0:T(8,128)(2,1)} %copy-done, bf16[8,3,2,16,8,128]{5,4,3,2,1,0:T(8,128)(2,1)} %copy-done, bf16[8,3,2,16,8,128]{5,4,3,2,1,0:T(8,128)(2,1)} %copy-done, ...), custom_call_target="tpu_custom_call", output_to_operand_aliasing={{}: (5, {})} | custom-call | flops 16000000000 | bytes 4000000 | tf_op jit(solution)/shard_map/later_attention/pallas_call | solution.py:312
  125.3 0.0 all-to-all-done.4.weighted_ref
  125.3 0.0 copy-start.5
  125.3 0.6 copy-done.5
  126.0 5.1 %left_factor.1 = bf16[128,2,4,8,128]{4,3,2,1,0:T(8,128)(2,1)} custom-call(s32[2]{0:T(128)} %pad_add_fusion.at_ref, bf16[16,4,4,8,256]{4,3,2,1,0:T(8,128)(2,1)} %bitcast.16, bf16[8,1,4,8,128]{4,3,2,1,0:T(8,128)(2,1)} %copy-done.5, f32[16,1]{1,0:T(8,128)} %copy.29.flags_ref, f32[32,1024]{1,0:T(8,128)} %get-tuple-element.40.gate_ref, ...), custom_call_target="tpu_custom_call", output_to_operand_aliasing={{}: (7, {})} | custom-call | flops 100000000 | bytes 3500000 | tf_op jit(solution)/shard_map/left_factor/pallas_call | solution.py:413
  131.0 0.0 copy-start.7
  131.0 9.1 %all-to-all-start.5 = ((bf16[128,2,4,8,128]{4,3,2,1,0:T(8,128)(2,1)}), bf16[128,2,4,8,128]{4,3,2,1,0:T(8,128)(2,1)S(1)}, u32[]{:S(2)}, u32[]{:S(2)}) async-start(bf16[128,2,4,8,128]{4,3,2,1,0:T(8,128)(2,1)} %left_factor.1), calls=%async_computation.5 | async-start | bytes 4194304 | tf_op jit(solution)/shard_map/all_to_all | solution.py:527
  140.2 0.8 copy.31.flags_ref
  141.0 0.0 copy-done.7
  141.0 0.7 copy.32.factor_ref
  141.7 27.0 %all-to-all-done.5 = bf16[128,2,4,8,128]{4,3,2,1,0:T(8,128)(2,1)S(1)} async-done(((bf16[128,2,4,8,128]{4,3,2,1,0:T(8,128)(2,1)}), bf16[128,2,4,8,128]{4,3,2,1,0:T(8,128)(2,1)S(1)}, u32[]{:S(2)}, u32[]{:S(2)}) %all-to-all-start.5) | async-done | bytes 2097184 | tf_op jit(solution)/shard_map/all_to_all | solution.py:527
  168.7 0.0 copy-start.2
  168.7 1.3 copy-done.2
  170.0 10.2 %finish.1 = (bf16[256,8,256]{2,1,0:T(8,128)(2,1)}, bf16[64,8,128]{2,1,0:T(8,128)(2,1)}) custom-call(bf16[256,8,256]{2,1,0:T(8,128)(2,1)} %x_ref.3, bf16[16,8,2,4,8,128]{5,4,3,2,1,0:T(8,128)(2,1)} %bitcast.17, f32[256,1]{1,0:T(8,128)} %copy.31.flags_ref, bf16[16,8,2,4,8,128]{5,4,3,2,1,0:T(8,128)(2,1)} %bitcast.18, ...), custom_call_target="tpu_custom_call" | custom-call | flops 3000000000 | bytes 5000000 | tf_op jit(solution)/shard_map/finish/pallas_call | solution.py:495
  (1 shorter events, 0.0 us)
Async XLA Ops:
  7.2 7.1 %copy-start.9 = (bf16[128,8]{0,1:T(8,128)(2,1)S(1)}, bf16[128,8]{0,1:T(8,128)(2,1)}, u32[]{:S(2)}) copy-start(bf16[128,8]{0,1:T(8,128)(2,1)} %param.19) | copy-start | bytes 6148
  7.2 7.8 %copy-start.8 = (s32[256,8]{0,1:T(8,128)S(1)}, s32[256,8]{0,1:T(8,128)}, u32[]{:S(2)}) copy-start(s32[256,8]{0,1:T(8,128)} %param.15) | copy-start | bytes 24580
  7.2 22.9 %all-to-all-start = ((bf16[256,8,256]{2,1,0:T(8,128)(2,1)}), bf16[256,8,256]{2,1,0:T(8,128)(2,1)S(1)}, u32[]{:S(2)}, u32[]{:S(2)}) async-start(bf16[256,8,256]{2,1,0:T(8,128)(2,1)} %x_ref.3), calls=%async_computation | async-start | bytes 2097152 | tf_op jit(solution)/shard_map/all_to_all | solution.py:527
  30.1 7.4 %copy-start.1 = (bf16[256,8,256]{2,1,0:T(8,128)(2,1)}, bf16[256,8,256]{2,1,0:T(8,128)(2,1)S(1)}, u32[]{:S(2)}) copy-start(bf16[256,8,256]{2,1,0:T(8,128)(2,1)S(1)} %all-to-all-done) | copy-start | bytes 3145732
  30.1 15.5 %all-to-all-start.1 = ((bf16[16,80,128]{2,1,0:T(8,128)(2,1)}), bf16[16,80,128]{2,1,0:T(8,128)(2,1)S(1)}, u32[]{:S(2)}, u32[]{:S(2)}) async-start(bf16[16,80,128]{2,1,0:T(8,128)(2,1)} %bitcast.19), calls=%async_computation.1 | async-start | bytes 655360 | tf_op jit(solution)/shard_map/all_to_all | solution.py:527
  37.4 41.3 %all-gather.2.cloned.1.call-start = ((), (), s32[]{:S(2)}) async-start(), calls=%async_computation.6 | async-start | bytes 2949120 | tf_op jit(solution)/shard_map/all_gather | solution.py:557
  45.6 8.0 %copy-start.10 = (s32[256]{0:T(256)S(1)}, s32[256]{0:T(256)}, u32[]{:S(2)}) copy-start(s32[256]{0:T(256)} %param.16) | copy-start | bytes 3076
  45.6 8.8 %copy-start.6 = (bf16[256,32]{0,1:T(8,128)(2,1)S(1)}, bf16[256,32]{0,1:T(8,128)(2,1)}, u32[]{:S(2)}) copy-start(bf16[256,32]{0,1:T(8,128)(2,1)} %param.25) | copy-start | bytes 49156
  45.6 0.7 copy-start.4
  46.4 26.1 %all-to-all-start.2 = ((bf16[8,3,2,16,8,128]{5,4,3,2,1,0:T(8,128)(2,1)}), bf16[8,3,2,16,8,128]{5,4,3,2,1,0:T(8,128)(2,1)S(1)}, u32[]{:S(2)}, u32[]{:S(2)}) async-start(bf16[8,3,2,16,8,128]{5,4,3,2,1,0:T(8,128)(2,1)} %get-tuple-element.28), calls=%async_computation.2 | async-start | bytes 3145728 | tf_op jit(solution)/shard_map/all_to_all | solution.py:527
  72.5 6.2 %copy-start.3 = (bf16[8,3,2,16,8,128]{5,4,3,2,1,0:T(8,128)(2,1)}, bf16[8,3,2,16,8,128]{5,4,3,2,1,0:T(8,128)(2,1)S(1)}, u32[]{:S(2)}) copy-start(bf16[8,3,2,16,8,128]{5,4,3,2,1,0:T(8,128)(2,1)S(1)} %all-to-all-done.2.q_ref.k_ref.v_ref) | copy-start | bytes 4718596
  72.5 26.7 %all-to-all-start.3 = ((bf16[8,3,2,16,8,128]{5,4,3,2,1,0:T(8,128)(2,1)}), bf16[8,3,2,16,8,128]{5,4,3,2,1,0:T(8,128)(2,1)S(1)}, u32[]{:S(2)}, u32[]{:S(2)}) async-start(bf16[8,3,2,16,8,128]{5,4,3,2,1,0:T(8,128)(2,1)} %get-tuple-element.29), calls=%async_computation.3 | async-start | bytes 3145728 | tf_op jit(solution)/shard_map/all_to_all | solution.py:527
  99.2 1.2 copy-start
  104.9 20.5 %all-to-all-start.4 = ((bf16[8,1,4,8,128]{4,3,2,1,0:T(8,128)(2,1)}), bf16[8,1,4,8,128]{4,3,2,1,0:T(8,128)(2,1)S(1)}, u32[]{:S(2)}, u32[]{:S(2)}) async-start(bf16[8,1,4,8,128]{4,3,2,1,0:T(8,128)(2,1)} %slab_attention.1), calls=%async_computation.4 | async-start | bytes 131072 | tf_op jit(solution)/shard_map/all_to_all | solution.py:527
  125.3 0.6 copy-start.5
  131.0 9.9 %copy-start.7 = (bf16[256,32]{0,1:T(8,128)(2,1)S(1)}, bf16[256,32]{0,1:T(8,128)(2,1)}, u32[]{:S(2)}) copy-start(bf16[256,32]{0,1:T(8,128)(2,1)} %param.26) | copy-start | bytes 49156
  131.0 37.6 %all-to-all-start.5 = ((bf16[128,2,4,8,128]{4,3,2,1,0:T(8,128)(2,1)}), bf16[128,2,4,8,128]{4,3,2,1,0:T(8,128)(2,1)S(1)}, u32[]{:S(2)}, u32[]{:S(2)}) async-start(bf16[128,2,4,8,128]{4,3,2,1,0:T(8,128)(2,1)} %left_factor.1), calls=%async_computation.5 | async-start | bytes 4194304 | tf_op jit(solution)/shard_map/all_to_all | solution.py:527
  168.7 1.3 copy-start.2
Sparse Core Ops, SparseCore 0:
  46.5 26.9 all-gather.1

commit v3 on v2

--- a/solution.py
+++ b/solution.py
@@ -13,6 +13,7 @@
 COL = ("xh", "z")
 BOTH = ROW + COL
 BLOCK, UNROLL = 256, 4
+QKV_STEPS, FINISH_STEPS = 2, 1
 NT = (((1,), (1,)), ((), ()))
 TN = (((0,), (0,)), ((), ()))
 
@@ -42,37 +43,45 @@
     return lax.broadcasted_iota(jnp.int32, shape, dim)
 
 
-def spread_columns(w):
-    row, col = iota((256, 1024), 0), iota((256, 1024), 1)
-    pick = (row == (col // 128) * 32 + col % 32).astype(jnp.bfloat16)
-    wide = dot(w, pick).astype(jnp.bfloat16)
-    quarter = (col // 32) % 4
-    return [jnp.where(quarter == si, wide, jnp.zeros_like(wide)) for si in range(4)]
-
-
-def spread_rows(w):
-    row, col = iota((1024, 256), 0), iota((1024, 256), 1)
-    pick = (col == (row // 128) * 32 + row % 32).astype(jnp.bfloat16)
-    tall = dot(pick, w).astype(jnp.bfloat16)
-    quarter = (row // 32) % 4
-    return [jnp.where(quarter == si, tall, jnp.zeros_like(tall)) for si in range(4)]
-
-
-def factor_columns(w, residue):
+def factor(normed, w, across):
     row, col = iota((32, 256), 0), iota((32, 256), 1)
-    pick = jnp.where((row == col // 8) & (col % 8 == residue), 1.0, 0.0).astype(jnp.bfloat16)
-    return dot(w, pick).astype(jnp.bfloat16)
-
-
-def right_columns(w, residue):
-    row, col = iota((32, 256), 0), iota((32, 256), 1)
-    pick = jnp.where((row == col % 32) & (col // 32 == residue), 1.0, 0.0).astype(jnp.bfloat16)
-    return dot(w, pick).astype(jnp.bfloat16)
-
-
-def four_abreast(x):
-    groups, width = x.shape[0], x.shape[3]
-    return jnp.concatenate([x[:, si].reshape(groups * 8, width) for si in range(4)], axis=1)
+    channel, residue = (col % 32, col // 32) if across == 32 else (col // 8, col % 8)
+    wide = dot(w, (row == channel).astype(jnp.bfloat16)).astype(jnp.bfloat16)
+    y = dot(normed, wide).reshape(-1, 8, 256)
+    own = iota((1, 8, 256), 1) == residue[:1].reshape(1, 1, 256)
+    return jnp.sum(jnp.where(own, y, 0.0), axis=1)
+
+
+def swap_quarters(blocks):
+    quarter = iota((1, 128), 1) // 32
+
+    def swap(a, b, shift, keep):
+        return (
+            jnp.where(keep, a, pltpu.roll(b, shift, 1)),
+            jnp.where(keep, pltpu.roll(a, 128 - shift, 1), b),
+        )
+
+    a, b, c, d = blocks
+    a, c = swap(a, c, 64, quarter < 2)
+    b, d = swap(b, d, 64, quarter < 2)
+    a, b = swap(a, b, 32, quarter % 2 == 0)
+    c, d = swap(c, d, 32, quarter % 2 == 0)
+    return a, b, c, d
+
+
+def by_sequence(heads):
+    first, second = swap_quarters(heads[:4]), swap_quarters(heads[4:])
+    whole = [jnp.concatenate(two, axis=1).reshape(-1, 8, 256) for two in zip(first, second)]
+    return jnp.stack(whole, axis=1).reshape(-1, 256)
+
+
+def by_head(y):
+    y = y.reshape(-1, 4, 8, 256)
+    heads = []
+    for half in range(2):
+        blocks = [y[:, si, :, half * 128 : (half + 1) * 128].reshape(-1, 128) for si in range(4)]
+        heads.extend(swap_quarters(blocks))
+    return heads
 
 
 def bias_kernel(duo_ref, w_ref, flags_ref, out_ref, rows_s):
@@ -112,42 +121,36 @@
     )(duo, w, flags)
 
 
-def qkv_kernel(x_ref, wq_ref, wk_ref, wv_ref, early_ref, late_ref, w_s):
-    @pl.when(pl.program_id(0) == 0)
-    def _():
-        for t, w in enumerate((wq_ref, wk_ref, wv_ref)):
-            for si, part in enumerate(spread_columns(w[...])):
-                w_s[t, si * 256 : (si + 1) * 256, :] = part
-
-    x = x_ref[...].reshape(16, 4, 8, 256).astype(jnp.float32)
-    n = four_abreast(standardize(x)).astype(jnp.bfloat16)
-    for t in range(3):
-        y = dot(n, w_s[t])
+def qkv_kernel(x_ref, wq_ref, wk_ref, wv_ref, early_ref, late_ref):
+    groups = 16 // QKV_STEPS
+    n = standardize(x_ref[...].reshape(groups * 128, 256).astype(jnp.float32))
+    n = n.astype(jnp.bfloat16)
+    for t, w in enumerate((wq_ref, wk_ref, wv_ref)):
+        y = dot(n, w[...])
         if t == 0:
             y = y * (LOG2E / 32**0.5)
-        y = y.reshape(4, 4, 8, 1024)
-        for h in range(8):
+        for h, part in enumerate(by_head(y)):
+            part = part.reshape(groups, 4, 8, 128).astype(jnp.bfloat16)
             for g in range(4):
                 out_ref = early_ref if g < 2 else late_ref
-                out_ref[h, t, g % 2] = y[:, g, :, h * 128 : (h + 1) * 128].astype(jnp.bfloat16)
+                out_ref[h, t, g % 2] = part[:, g]
 
 
 def qkv(x, wq, wk, wv):
     whole = pl.BlockSpec((256, 256), lambda i: (0, 0))
     return pl.pallas_call(
         qkv_kernel,
-        grid=(4,),
+        grid=(QKV_STEPS,),
         in_specs=[
-            pl.BlockSpec((4, 4, 4, 8, 256), lambda i: (i, 0, 0, 0, 0)),
+            pl.BlockSpec((16 // QKV_STEPS, 4, 4, 8, 256), lambda i: (i, 0, 0, 0, 0)),
             whole,
             whole,
             whole,
         ],
-        out_specs=[pl.BlockSpec((8, 3, 2, 4, 8, 128), lambda i: (0, 0, 0, i, 0, 0))] * 2,
+        out_specs=[pl.BlockSpec((8, 3, 2, 16 // QKV_STEPS, 8, 128), lambda i: (0, 0, 0, i, 0, 0))] * 2,
         out_shape=[jax.ShapeDtypeStruct((8, 3, 2, 16, 8, 128), jnp.bfloat16)] * 2,
-        scratch_shapes=[pltpu.VMEM((3, 1024, 1024), jnp.bfloat16)],
-        compiler_params=params(),
-        cost_estimate=cost(3_500_000_000, 4_500_000),
+        compiler_params=params(),
+        cost_estimate=cost(800_000_000, 4_500_000),
         name="qkv",
     )(x, wq, wk, wv)
 
@@ -214,7 +217,7 @@
 
 
 def first_kernel(
-    at_ref, q_ref, k_ref, v_ref, bias_ref, flags_ref, out_ref, slab_ref, mask_ref, *scratch
+    at_ref, q_ref, k_ref, v_ref, bias_ref, flags_ref, out_ref, slab_ref, slab_bias_ref, mask_ref, *scratch
 ):
     @pl.when(pl.program_id(0) == 0)
     def _():
@@ -225,6 +228,8 @@
         mask = dot(own.astype(jnp.bfloat16), flags.reshape(1024, 128).astype(jnp.bfloat16), NT)
         for g in range(4):
             mask_ref[g] = mask[g * 4 : g * 4 + 4]
+        slab = at_ref[0]
+        slab_bias_ref[0, 0] = bias_ref[lax.rem(slab, 8), lax.div(slab, 8), :, :64]
 
     present = mask_ref[pl.program_id(0)]
     attend(BLOCK, 1024 // BLOCK, q_ref, k_ref, v_ref, bias_ref, present, out_ref, *scratch)
@@ -268,11 +273,17 @@
             out_specs=[
                 pl.BlockSpec((128, 1, 1, 8, 128), lambda g, s: (0, 0, g, 0, 0)),
                 pl.BlockSpec((8, 1, 1, 8, 128), lambda g, s: (0, 0, g, 0, 0)),
+                pl.BlockSpec((1, 1, 8, 64, 128), lambda g, s: (0, 0, 0, 0, 0)),
                 pl.BlockSpec((4, 4, 1024), lambda g, s: (0, 0, 0)),
             ],
             scratch_shapes=attention_scratch(1024),
         ),
-        out_shape=[RETURNED, SLAB_WEIGHTED, jax.ShapeDtypeStruct((4, 4, 1024), jnp.float32)],
+        out_shape=[
+            RETURNED,
+            SLAB_WEIGHTED,
+            jax.ShapeDtypeStruct((1, 1, 8, 64, 128), jnp.bfloat16),
+            jax.ShapeDtypeStruct((4, 4, 1024), jnp.float32),
+        ],
         compiler_params=params(),
         cost_estimate=cost(16_000_000_000, 4_000_000, 2 << 22),
         name="first_attention",
@@ -290,9 +301,7 @@
                 pl.BlockSpec((8, 1, 1, 1, 8, 128), lambda g, s: (0, 0, g, s[0], 0, 0)),
                 part(1),
                 part(2),
-                pl.BlockSpec(
-                    (1, 1, 8, 80, 128), lambda g, s: (lax.rem(s[0], 8), lax.div(s[0], 8), 0, 0, 0)
-                ),
+                pl.BlockSpec((1, 1, 8, 64, 128), lambda g, s: (0, 0, 0, 0, 0)),
                 pl.BlockSpec((1, 4, 1024), lambda g, s: (g + 2, 0, 0)),
                 pl.BlockSpec(memory_space=pl.ANY),
             ],
@@ -331,77 +340,51 @@
 
 
 def gates(x, w):
-    return jax.nn.sigmoid(dot(four_abreast(standardize(x)).astype(jnp.bfloat16), w))
-
-
-def prepare_kernel(
-    at_ref, x_ref, slab_ref, gate_ref, out_w_ref, gates_ref, slab_gates_ref, spread_ref, w_s
-):
-    @pl.when(pl.program_id(0) == 0)
-    def _():
-        for si, part in enumerate(spread_columns(gate_ref[...])):
-            w_s[si * 256 : (si + 1) * 256, :] = part
-        for si, part in enumerate(spread_rows(out_w_ref[...])):
-            spread_ref[:, si * 256 : (si + 1) * 256] = part
-        slab_gates_ref[...] = gates(slab_ref[0].astype(jnp.float32), w_s[...])
-
-    x = x_ref[...].reshape(16, 4, 8, 256).astype(jnp.float32)
-    gates_ref[...] = gates(x, w_s[...]).astype(jnp.bfloat16)
-
-
-def prepare(at, x, sequences, w_gate, w_out):
+    return jax.nn.sigmoid(dot(standardize(x).astype(jnp.bfloat16), w))
+
+
+def prepare_kernel(at_ref, x_ref, slab_ref, gate_ref, gates_ref, slab_gates_ref):
+    x = x_ref[...].reshape(2048, 256).astype(jnp.float32)
+    gates_ref[...] = gates(x, gate_ref[...]).astype(jnp.bfloat16)
+    slab_gates_ref[...] = gates(slab_ref[0].reshape(128, 256).astype(jnp.float32), gate_ref[...])
+
+
+def prepare(at, x, sequences, w_gate):
     whole = lambda *shape: pl.BlockSpec(shape, lambda i, s: (0,) * len(shape))
     return pl.pallas_call(
         prepare_kernel,
         grid_spec=pltpu.PrefetchScalarGridSpec(
             num_scalar_prefetch=1,
-            grid=(4,),
+            grid=(1,),
             in_specs=[
-                pl.BlockSpec((64, 8, 256), lambda i, s: (i, 0, 0)),
+                whole(256, 8, 256),
                 pl.BlockSpec((1, 4, 4, 8, 256), lambda i, s: (s[0], 0, 0, 0, 0)),
                 whole(256, 256),
-                whole(256, 256),
             ],
-            out_specs=[
-                pl.BlockSpec((128, 1024), lambda i, s: (i, 0)),
-                whole(32, 1024),
-                whole(1024, 1024),
-            ],
-            scratch_shapes=[pltpu.VMEM((1024, 1024), jnp.bfloat16)],
+            out_specs=[whole(2048, 256), whole(128, 256)],
         ),
         out_shape=[
-            jax.ShapeDtypeStruct((512, 1024), jnp.bfloat16),
-            jax.ShapeDtypeStruct((32, 1024), jnp.float32),
-            jax.ShapeDtypeStruct((1024, 1024), jnp.bfloat16),
-        ],
-        compiler_params=params(),
-        cost_estimate=cost(1_500_000_000, 6_000_000),
+            jax.ShapeDtypeStruct((2048, 256), jnp.bfloat16),
+            jax.ShapeDtypeStruct((128, 256), jnp.float32),
+        ],
+        compiler_params=params(),
+        cost_estimate=cost(300_000_000, 3_000_000),
         name="prepare",
-    )(at, x, sequences, w_gate, w_out)
-
-
-def gated_update(x, gate, weighted, w_out):
-    gated = (gate * weighted).astype(jnp.bfloat16)
-    update = dot(gated, w_out)
-    fresh = x + jnp.stack(
-        [update[:, si * 256 : (si + 1) * 256].reshape(-1, 8, 256) for si in range(4)], axis=1
-    )
-    return fresh.astype(jnp.bfloat16).astype(jnp.float32)
+    )(at, x, sequences, w_gate)
+
+
+def gated_update(x, gate, heads, w_out):
+    gated = (gate * by_sequence(heads)).astype(jnp.bfloat16)
+    return (x + dot(gated, w_out)).astype(jnp.bfloat16).astype(jnp.float32)
 
 
 def left_kernel(
-    at_ref, x_ref, weighted_ref, flags_ref, gate_ref, out_w_ref, factor_ref, _, out_ref, normed_s
+    at_ref, x_ref, weighted_ref, flags_ref, gate_ref, out_w_ref, factor_ref, _, out_ref
 ):
-    x = x_ref[0].astype(jnp.float32)
-    weighted = jnp.concatenate(
-        [weighted_ref[h, 0].astype(jnp.float32).reshape(32, 128) for h in range(8)], axis=1
-    )
-    fresh = gated_update(x, gate_ref[...], weighted, out_w_ref[...])
-    normed_s[...] = standardize(fresh).reshape(16, 8, 256)
-    left = jnp.zeros((16, 256), jnp.float32)
-    for residue in range(8):
-        part = normed_s[:, residue, :].astype(jnp.bfloat16)
-        left = left + dot(part, factor_columns(factor_ref[...], residue))
+    x = x_ref[0].reshape(128, 256).astype(jnp.float32)
+    heads = [weighted_ref[h, 0].astype(jnp.float32).reshape(32, 128) for h in range(8)]
+    fresh = gated_update(x, gate_ref[...], heads, out_w_ref[...])
+    left = factor(standardize(fresh).astype(jnp.bfloat16), factor_ref[...], 1)
     left = left * flags_ref[...]
     for half in range(2):
         part = left[:, half * 128 : (half + 1) * 128].reshape(1, 2, 8, 128).astype(jnp.bfloat16)
@@ -419,13 +402,12 @@
                 pl.BlockSpec((1, 4, 4, 8, 256), lambda i, s: (s[0], 0, 0, 0, 0)),
                 whole(8, 1, 4, 8, 128),
                 whole(16, 1),
-                whole(32, 1024),
-                whole(1024, 1024),
+                whole(128, 256),
+                whole(256, 256),
                 whole(256, 32),
                 pl.BlockSpec(memory_space=pl.ANY),
             ],
             out_specs=pl.BlockSpec((128, 1, 4, 8, 128), lambda i, s: (0, 1, 0, 0, 0)),
-            scratch_shapes=[pltpu.VMEM((16, 8, 256), jnp.float32)],
         ),
         out_shape=RETURNED,
         input_output_aliases={7: 0},
@@ -437,31 +419,19 @@
 
 def final_kernel(
     x_ref, weighted_ref, flags_ref, left_ref, gate_ref, out_w_ref, factor_ref, product_ref,
-    fresh_ref, pair_ref, factor_s, normed_s, right_s, outer_s, pair_s,
+    fresh_ref, pair_ref, right_s, outer_s, pair_s,
 ):
     step = pl.program_id(0)
-
-    @pl.when(step == 0)
-    def _():
-        for residue in range(8):
-            factor_s[residue] = right_columns(factor_ref[...], residue)
-
-    x = x_ref[...].reshape(16, 4, 8, 256).astype(jnp.float32)
-    weighted = jnp.concatenate(
-        [
-            weighted_ref[:, h, 0].astype(jnp.float32).reshape(128, 128)
-            for h in range(8)
-        ],
-        axis=1,
-    )
-    fresh = gated_update(x, gate_ref[...].astype(jnp.float32), weighted, out_w_ref[...])
-    fresh_ref[...] = fresh.reshape(64, 8, 256).astype(jnp.bfloat16)
-    normed_s[...] = standardize(fresh).reshape(64, 8, 256)
-    right = jnp.zeros((64, 256), jnp.float32)
-    for residue in range(8):
-        part = normed_s[:, residue, :].astype(jnp.bfloat16)
-        right = right + dot(part, factor_s[residue])
-    right_s[pl.ds(pl.multiple_of(step * 64, 64), 64), :] = (right * flags_ref[...]).astype(
+    chains = 256 // FINISH_STEPS
+
+    x = x_ref[...].reshape(chains * 8, 256).astype(jnp.float32)
+    heads = [
+        weighted_ref[:, h, 0].astype(jnp.float32).reshape(chains * 2, 128) for h in range(8)
+    ]
+    fresh = gated_update(x, gate_ref[...].astype(jnp.float32), heads, out_w_ref[...])
+    fresh_ref[...] = fresh.reshape(chains, 8, 256).astype(jnp.bfloat16)
+    right = factor(standardize(fresh).astype(jnp.bfloat16), factor_ref[...], 32)
+    right_s[pl.ds(pl.multiple_of(step * chains, chains), chains), :] = (right * flags_ref[...]).astype(
         jnp.bfloat16
     )
 
@@ -494,30 +464,28 @@
     whole = lambda *shape: pl.BlockSpec(shape, lambda i: (0,) * len(shape))
     return pl.pallas_call(
         final_kernel,
-        grid=(4,),
+        grid=(FINISH_STEPS,),
         in_specs=[
-            pl.BlockSpec((64, 8, 256), lambda i: (i, 0, 0)),
-            pl.BlockSpec((4, 8, 1, 4, 8, 128), lambda i: (i, 0, 0, 0, 0, 0)),
-            pl.BlockSpec((64, 1), lambda i: (i, 0)),
+            pl.BlockSpec((256 // FINISH_STEPS, 8, 256), lambda i: (i, 0, 0)),
+            pl.BlockSpec((16 // FINISH_STEPS, 8, 1, 4, 8, 128), lambda i: (i, 0, 0, 0, 0, 0)),
+            pl.BlockSpec((256 // FINISH_STEPS, 1), lambda i: (i, 0)),
             pl.BlockSpec((16, 8, 1, 4, 8, 128), lambda i: (0, 0, 1, 0, 0, 0)),
-            pl.BlockSpec((128, 1024), lambda i: (i, 0)),
-            whole(1024, 1024),
+            pl.BlockSpec((2048 // FINISH_STEPS, 256), lambda i: (i, 0)),
+            whole(256, 256),
             whole(256, 32),
             whole(1024, 128),
         ],
-        out_specs=[pl.BlockSpec((64, 8, 256), lambda i: (i, 0, 0)), whole(64, 8, 128)],
+        out_specs=[pl.BlockSpec((256 // FINISH_STEPS, 8, 256), lambda i: (i, 0, 0)), whole(64, 8, 128)],
         out_shape=[
             jax.ShapeDtypeStruct((256, 8, 256), jnp.bfloat16),
             jax.ShapeDtypeStruct((64, 8, 128), jnp.bfloat16),
         ],
         scratch_shapes=[
-            pltpu.VMEM((8, 256, 256), jnp.bfloat16),
-            pltpu.VMEM((64, 8, 256), jnp.float32),
             pltpu.VMEM((256, 256), jnp.bfloat16),
             pltpu.VMEM((32, 8, 8, 256), jnp.float32),
             pltpu.VMEM((64, 8, 128), jnp.float32),
         ],
-        compiler_params=params(),
+        compiler_params=params(36),
         cost_estimate=cost(3_000_000_000, 5_000_000),
         name="finish",
     )(x, returned, flags, returned, gate, w_out, w_second, w_product)
@@ -561,18 +529,23 @@
 
     chains = chain_exists_flags.astype(jnp.float32)[:, None]
     own_chains = lax.dynamic_slice_in_dim(chains, row * 16, 16, 0)
-    gate, slab_gate, w_out = prepare(
-        at, alignment_tensor, sequences, sigmoid_matrix, final_projection_matrix
-    )
-
-    early, gate, slab_gate, w_out = lax.optimization_barrier((early, gate, slab_gate, w_out))
-    returned, slab_weighted, mask = first_attention(at, early, bias)
-    slab_weighted = slab_attention(at, late, bias, mask, slab_weighted)
+    gate, slab_gate = prepare(at, alignment_tensor, sequences, sigmoid_matrix)
+
+    early, gate, slab_gate = lax.optimization_barrier((early, gate, slab_gate))
+    returned, slab_weighted, slab_bias, mask = first_attention(at, early, bias)
+    slab_weighted = slab_attention(at, late, slab_bias, mask, slab_weighted)
     slab_weighted = exchange(slab_weighted, COL)
     returned = later_attention(late, bias, mask, returned)
     slab_weighted, returned = lax.optimization_barrier((slab_weighted, returned))
     returned = left_factor(
-        at, sequences, slab_weighted, own_chains, slab_gate, w_out, first_factor_matrix, returned
+        at,
+        sequences,
+        slab_weighted,
+        own_chains,
+        slab_gate,
+        final_projection_matrix,
+        first_factor_matrix,
+        returned,
     )
     returned = exchange(returned, BOTH)
     return tuple(
@@ -581,7 +554,7 @@
             returned.reshape(16, 8, 2, 4, 8, 128),
             chains,
             gate,
-            w_out,
+            final_projection_matrix,
             second_factor_matrix,
             product_to_duo_matrix,
         )

time: 188 us -> 179 us (0.952)
  Pallas kernels: 71.3 us -> 58.8 us
  waiting for transfers between devices: 50.7 us -> 56.8 us
  starting transfers between devices: 41.4 us -> 39.2 us
    pallas_call x2, Pallas kernels: 18.4 us -> 10.2 us  [the longest x1 5.55 us: qkv(): pl.pallas_call(qkv_kernel, grid=(QKV_STEPS,), in_specs=[pl.BlockSpec((16...]
    all_to_all x6, waiting for transfers between devices: 50.7 us -> 56.7 us  [exchange(): return lax.all_to_all(x, axes, split_axis=0, concat_axis=0, tiled=True)]
    pallas_call x1, Pallas kernels: 6.66 us -> 4.08 us  [prepare(): pl.pallas_call(prepare_kernel, grid_spec=pltpu.PrefetchScalarGridSpec(num...]
    all_to_all x6, starting transfers between devices: 41.4 us -> 39.1 us  [exchange(): return lax.all_to_all(x, axes, split_axis=0, concat_axis=0, tiled=True)]
    unnamed x25 -> x31, local copies, waits for them, and re-layouts: 6.16 us -> 6.33 us
  transfers between devices with their start and end apart: 7 -> 7, of which waited for: 4 -> 5; matrix products, arithmetic and copies ran while one was open for 3% -> 2% of each run, Pallas kernels for 28% -> 26%
where the time goes in v3:
time: 179 us; the launch traced here: 178 us
  Pallas kernels  58.8 us (33%)
  waiting for transfers between devices  56.8 us (32%)
  starting transfers between devices  39.2 us (22%)
  between operations  14.8 us (8%)
  local copies, waits for them, and re-layouts  7.22 us (4%)
    all_to_all x6, waiting for transfers between devices, exchange(): return lax.all_to_all(x, axes, split_axis=0, concat_axis=0, tiled=True)  56.7 us
    all_to_all x6, starting transfers between devices, exchange(): return lax.all_to_all(x, axes, split_axis=0, concat_axis=0, tiled=True)  39.1 us
    pallas_call x1, Pallas kernels, first_attention(): pl.pallas_call(first_kernel, grid_spec=pltpu.PrefetchScalarGridSpec(num_s...  16.2 us
    pallas_call x1, Pallas kernels, later_attention(): pl.pallas_call(later_kernel, grid=(2,), in_specs=[part(0), part(1), part(...  15.2 us
    unnamed x31, local copies, waits for them, and re-layouts  6.33 us
    pallas_call x1, Pallas kernels, qkv(): pl.pallas_call(qkv_kernel, grid=(QKV_STEPS,), in_specs=[pl.BlockSpec((16...  5.55 us
    pallas_call x1, Pallas kernels, bias_tile(): pl.pallas_call(bias_kernel, grid=(5,), in_specs=[pl.BlockSpec((16, 128, 1...  5.3 us
    pallas_call x1, Pallas kernels, finish(): pl.pallas_call(final_kernel, grid=(FINISH_STEPS,), in_specs=[pl.BlockSpec...  4.66 us
  transfers between devices with their start and end apart: 7, of which 5 were waited for; matrix products, arithmetic and copies ran while one was open for 2% of the time, Pallas kernels for 26%

profile of v3, /device:TPU:1, one launch (start us, length us, event | category | flops | bytes accessed | tf_op | source)
XLA Modules:
  0.0 178.0 jit_solution(12545554067566021637)
XLA Ops:
  7.2 0.0 copy-start.12
  7.2 0.0 copy-start.11
  7.2 7.1 %all-to-all-start = ((bf16[256,8,256]{2,1,0:T(8,128)(2,1)}), bf16[256,8,256]{2,1,0:T(8,128)(2,1)S(1)}, u32[]{:S(2)}, u32[]{:S(2)}) async-start(bf16[256,8,256]{2,1,0:T(8,128)(2,1)} %x_ref.3), calls=%async_computation | async-start | bytes 2097152 | tf_op jit(solution)/shard_map/all_to_all | solution.py:495
  14.2 0.0 copy-done.12
  14.2 0.7 copy.28.w_ref
  15.0 0.0 copy-done.11
  15.0 0.6 convert_bitcast_fusion.flags_ref
  15.6 5.3 %bias_tile.1 = bf16[2,8,80,128]{3,2,1,0:T(8,128)(2,1)} custom-call(bf16[64,128,128]{2,1,0:T(8,128)(2,1)} %duo_ref.1, bf16[128,8]{1,0:T(8,128)(2,1)} %copy.28.w_ref, bf16[16,128]{1,0:T(8,128)(2,1)} %convert_bitcast_fusion.flags_ref), custom_call_target="tpu_custom_call" | custom-call | flops 20000000 | bytes 2200000 | tf_op jit(solution)/shard_map/bias_tile/pallas_call | solution.py:107
  20.9 9.2 %all-to-all-done = bf16[256,8,256]{2,1,0:T(8,128)(2,1)S(1)} async-done(((bf16[256,8,256]{2,1,0:T(8,128)(2,1)}), bf16[256,8,256]{2,1,0:T(8,128)(2,1)S(1)}, u32[]{:S(2)}, u32[]{:S(2)}) %all-to-all-start) | async-done | bytes 1048608 | tf_op jit(solution)/shard_map/all_to_all | solution.py:495
  30.1 0.0 copy-start.5
  30.1 7.3 %all-to-all-start.1 = ((bf16[16,80,128]{2,1,0:T(8,128)(2,1)}), bf16[16,80,128]{2,1,0:T(8,128)(2,1)S(1)}, u32[]{:S(2)}, u32[]{:S(2)}) async-start(bf16[16,80,128]{2,1,0:T(8,128)(2,1)} %bitcast.19), calls=%async_computation.1 | async-start | bytes 655360 | tf_op jit(solution)/shard_map/all_to_all | solution.py:495
  37.4 0.0 all-gather.2.cloned.1.call-start
  37.4 0.0 copy-done.5
  37.4 5.5 %qkv.1 = (bf16[8,3,2,16,8,128]{5,4,3,2,1,0:T(8,128)(2,1)}, bf16[8,3,2,16,8,128]{5,4,3,2,1,0:T(8,128)(2,1)}) custom-call(bf16[16,4,4,8,256]{4,3,2,1,0:T(8,128)(2,1)} %bitcast.16, bf16[256,256]{1,0:T(8,128)(2,1)} %wq_ref.1, bf16[256,256]{1,0:T(8,128)(2,1)} %wk_ref.1, bf16[256,256]{1,0:T(8,128)(2,1)} %wv_ref.1), custom_call_target="tpu_custom_call" | custom-call | flops 800000000 | bytes 4500000 | tf_op jit(solution)/shard_map/qkv/pallas_call | solution.py:141
  43.0 0.0 copy-start.13
  43.0 0.0 copy-start.9
  43.0 2.3 %all-to-all-done.1 = bf16[16,80,128]{2,1,0:T(8,128)(2,1)S(1)} async-done(((bf16[16,80,128]{2,1,0:T(8,128)(2,1)}), bf16[16,80,128]{2,1,0:T(8,128)(2,1)S(1)}, u32[]{:S(2)}, u32[]{:S(2)}) %all-to-all-start.1) | async-done | bytes 327712 | tf_op jit(solution)/shard_map/all_to_all | solution.py:495
  45.3 0.0 copy-start.7
  45.3 0.7 copy-done.7
  46.0 0.0 all-gather.2.cloned.1.call-update
  46.0 4.3 %all-to-all-start.2 = ((bf16[8,3,2,16,8,128]{5,4,3,2,1,0:T(8,128)(2,1)}), bf16[8,3,2,16,8,128]{5,4,3,2,1,0:T(8,128)(2,1)S(1)}, u32[]{:S(2)}, u32[]{:S(2)}) async-start(bf16[8,3,2,16,8,128]{5,4,3,2,1,0:T(8,128)(2,1)} %get-tuple-element.27), calls=%async_computation.2 | async-start | bytes 3145728 | tf_op jit(solution)/shard_map/all_to_all | solution.py:495
  51.0 0.0 copy-done.13
  51.0 0.1 dynamic-slice_bitcast_fusion
  51.1 0.7 copy.29.flags_ref
  51.8 0.0 copy-done.9
  51.8 0.7 copy.30.factor_ref
  52.5 0.6 pad_add_fusion.at_ref
  53.1 4.1 %prepare.1 = (bf16[2048,256]{1,0:T(8,128)(2,1)}, f32[128,256]{1,0:T(8,128)}) custom-call(s32[2]{0:T(128)} %pad_add_fusion.at_ref, bf16[256,8,256]{2,1,0:T(8,128)(2,1)} %x_ref.3, bf16[16,4,4,8,256]{4,3,2,1,0:T(8,128)(2,1)} %bitcast.17, bf16[256,256]{1,0:T(8,128)(2,1)} %gate_ref.1), custom_call_target="tpu_custom_call" | custom-call | flops 300000000 | bytes 3000000 | tf_op jit(solution)/shard_map/prepare/pallas_call | solution.py:354
  57.2 12.7 %all-to-all-done.2.q_ref.k_ref.v_ref = bf16[8,3,2,16,8,128]{5,4,3,2,1,0:T(8,128)(2,1)S(1)} async-done(((bf16[8,3,2,16,8,128]{5,4,3,2,1,0:T(8,128)(2,1)}), bf16[8,3,2,16,8,128]{5,4,3,2,1,0:T(8,128)(2,1)S(1)}, u32[]{:S(2)}, u32[]{:S(2)}) %all-to-all-start.2) | async-done | bytes 1572896 | tf_op jit(solution)/shard_map/all_to_all | solution.py:495
  69.9 0.0 copy-start.6
  69.9 6.2 %all-to-all-start.3 = ((bf16[8,3,2,16,8,128]{5,4,3,2,1,0:T(8,128)(2,1)}), bf16[8,3,2,16,8,128]{5,4,3,2,1,0:T(8,128)(2,1)S(1)}, u32[]{:S(2)}, u32[]{:S(2)}) async-start(bf16[8,3,2,16,8,128]{5,4,3,2,1,0:T(8,128)(2,1)} %get-tuple-element.28), calls=%async_computation.3 | async-start | bytes 3145728 | tf_op jit(solution)/shard_map/all_to_all | solution.py:495
  76.1 0.0 all-gather.2.cloned.1.call-done.bias_ref.flags_ref
  76.1 0.0 copy-done.6
  76.1 16.2 %first_attention.1 = (bf16[128,2,4,8,128]{4,3,2,1,0:T(8,128)(2,1)}, bf16[8,1,4,8,128]{4,3,2,1,0:T(8,128)(2,1)}, bf16[1,1,8,64,128]{4,3,2,1,0:T(8,128)(2,1)}, f32[4,4,1024]{2,1,0:T(4,128)}) custom-call(s32[2]{0:T(128)} %pad_add_fusion.at_ref, bf16[8,3,2,16,8,128]{5,4,3,2,1,0:T(8,128)(2,1)} %copy-done.6, bf16[8,3,2,16,8,128]{5,4,3,2,1,0:T(8,128)(2,1)} %copy-done.6, ...), custom_call_target="tpu_custom_call" | custom-call | flops 16000000000 | bytes 4000000 | tf_op jit(solution)/shard_map/first_attention/pallas_call | solution.py:261
  92.3 4.3 %all-to-all-done.3.q_ref.k_ref.v_ref = bf16[8,3,2,16,8,128]{5,4,3,2,1,0:T(8,128)(2,1)S(1)} async-done(((bf16[8,3,2,16,8,128]{5,4,3,2,1,0:T(8,128)(2,1)}), bf16[8,3,2,16,8,128]{5,4,3,2,1,0:T(8,128)(2,1)S(1)}, u32[]{:S(2)}, u32[]{:S(2)}) %all-to-all-start.3) | async-done | bytes 1572896 | tf_op jit(solution)/shard_map/all_to_all | solution.py:495
  96.6 0.0 copy-start.4
  96.6 1.2 copy-done.4
  97.8 4.4 %slab_attention.1 = bf16[8,1,4,8,128]{4,3,2,1,0:T(8,128)(2,1)} custom-call(s32[2]{0:T(128)} %pad_add_fusion.at_ref, bf16[8,3,2,16,8,128]{5,4,3,2,1,0:T(8,128)(2,1)} %copy-done.4, bf16[8,3,2,16,8,128]{5,4,3,2,1,0:T(8,128)(2,1)} %copy-done.4, bf16[8,3,2,16,8,128]{5,4,3,2,1,0:T(8,128)(2,1)} %copy-done.4, ...), custom_call_target="tpu_custom_call", output_to_operand_aliasing={{}: (6, {})} | custom-call | flops 1000000000 | bytes 2000000 | tf_op jit(solution)/shard_map/slab_attention/pallas_call | solution.py:295
  102.2 5.2 %all-to-all-start.4 = ((bf16[8,1,4,8,128]{4,3,2,1,0:T(8,128)(2,1)}), bf16[8,1,4,8,128]{4,3,2,1,0:T(8,128)(2,1)S(1)}, u32[]{:S(2)}, u32[]{:S(2)}) async-start(bf16[8,1,4,8,128]{4,3,2,1,0:T(8,128)(2,1)} %slab_attention.1), calls=%async_computation.4 | async-start | bytes 131072 | tf_op jit(solution)/shard_map/all_to_all | solution.py:495
  107.4 15.2 %later_attention.1._ = bf16[128,2,4,8,128]{4,3,2,1,0:T(8,128)(2,1)} custom-call(bf16[8,3,2,16,8,128]{5,4,3,2,1,0:T(8,128)(2,1)} %copy-done.4, bf16[8,3,2,16,8,128]{5,4,3,2,1,0:T(8,128)(2,1)} %copy-done.4, bf16[8,3,2,16,8,128]{5,4,3,2,1,0:T(8,128)(2,1)} %copy-done.4, ...), custom_call_target="tpu_custom_call", output_to_operand_aliasing={{}: (5, {})} | custom-call | flops 16000000000 | bytes 4000000 | tf_op jit(solution)/shard_map/later_attention/pallas_call | solution.py:321
  122.7 0.0 all-to-all-done.4.weighted_ref
  122.7 0.0 copy-start.8
  122.7 0.6 copy-done.8
  123.3 3.4 %left_factor.1 = bf16[128,2,4,8,128]{4,3,2,1,0:T(8,128)(2,1)} custom-call(s32[2]{0:T(128)} %pad_add_fusion.at_ref, bf16[16,4,4,8,256]{4,3,2,1,0:T(8,128)(2,1)} %bitcast.18, bf16[8,1,4,8,128]{4,3,2,1,0:T(8,128)(2,1)} %copy-done.8, f32[16,1]{1,0:T(8,128)} %copy.29.flags_ref, f32[128,256]{1,0:T(8,128)} %get-tuple-element.39.gate_ref, ...), custom_call_target="tpu_custom_call", output_to_operand_aliasing={{}: (7, {})} | custom-call | flops 100000000 | bytes 3500000 | tf_op jit(solution)/shard_map/left_factor/pallas_call | solution.py:396
  126.7 0.0 copy-start.10
  126.7 0.0 copy-start
  126.7 0.0 copy-start.1
  126.7 9.1 %all-to-all-start.5 = ((bf16[128,2,4,8,128]{4,3,2,1,0:T(8,128)(2,1)}), bf16[128,2,4,8,128]{4,3,2,1,0:T(8,128)(2,1)S(1)}, u32[]{:S(2)}, u32[]{:S(2)}) async-start(bf16[128,2,4,8,128]{4,3,2,1,0:T(8,128)(2,1)} %left_factor.1), calls=%async_computation.5 | async-start | bytes 4194304 | tf_op jit(solution)/shard_map/all_to_all | solution.py:495
  135.8 0.1 copy.31.flags_ref
  136.0 0.0 copy-done.10
  136.0 0.1 copy.32.factor_ref
  136.1 28.2 %all-to-all-done.5 = bf16[128,2,4,8,128]{4,3,2,1,0:T(8,128)(2,1)S(1)} async-done(((bf16[128,2,4,8,128]{4,3,2,1,0:T(8,128)(2,1)}), bf16[128,2,4,8,128]{4,3,2,1,0:T(8,128)(2,1)S(1)}, u32[]{:S(2)}, u32[]{:S(2)}) %all-to-all-start.5) | async-done | bytes 2097184 | tf_op jit(solution)/shard_map/all_to_all | solution.py:495
  164.3 0.0 copy-done
  164.3 0.0 copy-done.1
  164.3 0.0 copy-start.2
  164.3 1.2 copy-done.2
  165.5 0.0 copy-start.3
  165.5 0.9 copy-done.3
  166.5 4.7 %finish.1 = (bf16[256,8,256]{2,1,0:T(8,128)(2,1)}, bf16[64,8,128]{2,1,0:T(8,128)(2,1)}) custom-call(bf16[256,8,256]{2,1,0:T(8,128)(2,1)S(1)} %copy-done, bf16[16,8,2,4,8,128]{5,4,3,2,1,0:T(8,128)(2,1)S(1)} %bitcast.14, f32[256,1]{1,0:T(8,128)S(1)} %copy.31.flags_ref, bf16[16,8,2,4,8,128]{5,4,3,2,1,0:T(8,128)(2,1)S(1)} %bitcast.15, ...), custom_call_target="tpu_custom_call" | custom-call | flops 3000000000 | bytes 5000000 | tf_op jit(solution)/shard_map/finish/pallas_call | solution.py:465
  (1 shorter events, 0.0 us)
Async XLA Ops:
  7.2 7.1 %copy-start.12 = (bf16[128,8]{0,1:T(8,128)(2,1)S(1)}, bf16[128,8]{0,1:T(8,128)(2,1)}, u32[]{:S(2)}) copy-start(bf16[128,8]{0,1:T(8,128)(2,1)} %param.19) | copy-start | bytes 6148
  7.2 7.8 %copy-start.11 = (s32[256,8]{0,1:T(8,128)S(1)}, s32[256,8]{0,1:T(8,128)}, u32[]{:S(2)}) copy-start(s32[256,8]{0,1:T(8,128)} %param.15) | copy-start | bytes 24580
  7.2 22.9 %all-to-all-start = ((bf16[256,8,256]{2,1,0:T(8,128)(2,1)}), bf16[256,8,256]{2,1,0:T(8,128)(2,1)S(1)}, u32[]{:S(2)}, u32[]{:S(2)}) async-start(bf16[256,8,256]{2,1,0:T(8,128)(2,1)} %x_ref.3), calls=%async_computation | async-start | bytes 2097152 | tf_op jit(solution)/shard_map/all_to_all | solution.py:495
  30.1 7.4 %copy-start.5 = (bf16[256,8,256]{2,1,0:T(8,128)(2,1)}, bf16[256,8,256]{2,1,0:T(8,128)(2,1)S(1)}, u32[]{:S(2)}) copy-start(bf16[256,8,256]{2,1,0:T(8,128)(2,1)S(1)} %all-to-all-done) | copy-start | bytes 3145732
  30.1 15.2 %all-to-all-start.1 = ((bf16[16,80,128]{2,1,0:T(8,128)(2,1)}), bf16[16,80,128]{2,1,0:T(8,128)(2,1)S(1)}, u32[]{:S(2)}, u32[]{:S(2)}) async-start(bf16[16,80,128]{2,1,0:T(8,128)(2,1)} %bitcast.19), calls=%async_computation.1 | async-start | bytes 655360 | tf_op jit(solution)/shard_map/all_to_all | solution.py:495
  37.4 38.7 %all-gather.2.cloned.1.call-start = ((), (), s32[]{:S(2)}) async-start(), calls=%async_computation.6 | async-start | bytes 2949120 | tf_op jit(solution)/shard_map/all_gather | solution.py:525
  43.0 8.0 %copy-start.13 = (s32[256]{0:T(256)S(1)}, s32[256]{0:T(256)}, u32[]{:S(2)}) copy-start(s32[256]{0:T(256)} %param.16) | copy-start | bytes 3076
  43.0 8.8 %copy-start.9 = (bf16[256,32]{0,1:T(8,128)(2,1)S(1)}, bf16[256,32]{0,1:T(8,128)(2,1)}, u32[]{:S(2)}) copy-start(bf16[256,32]{0,1:T(8,128)(2,1)} %param.25) | copy-start | bytes 49156
  45.3 0.7 copy-start.7
  46.0 23.9 %all-to-all-start.2 = ((bf16[8,3,2,16,8,128]{5,4,3,2,1,0:T(8,128)(2,1)}), bf16[8,3,2,16,8,128]{5,4,3,2,1,0:T(8,128)(2,1)S(1)}, u32[]{:S(2)}, u32[]{:S(2)}) async-start(bf16[8,3,2,16,8,128]{5,4,3,2,1,0:T(8,128)(2,1)} %get-tuple-element.27), calls=%async_computation.2 | async-start | bytes 3145728 | tf_op jit(solution)/shard_map/all_to_all | solution.py:495
  69.9 6.2 %copy-start.6 = (bf16[8,3,2,16,8,128]{5,4,3,2,1,0:T(8,128)(2,1)}, bf16[8,3,2,16,8,128]{5,4,3,2,1,0:T(8,128)(2,1)S(1)}, u32[]{:S(2)}) copy-start(bf16[8,3,2,16,8,128]{5,4,3,2,1,0:T(8,128)(2,1)S(1)} %all-to-all-done.2.q_ref.k_ref.v_ref) | copy-start | bytes 4718596
  69.9 26.7 %all-to-all-start.3 = ((bf16[8,3,2,16,8,128]{5,4,3,2,1,0:T(8,128)(2,1)}), bf16[8,3,2,16,8,128]{5,4,3,2,1,0:T(8,128)(2,1)S(1)}, u32[]{:S(2)}, u32[]{:S(2)}) async-start(bf16[8,3,2,16,8,128]{5,4,3,2,1,0:T(8,128)(2,1)} %get-tuple-element.28), calls=%async_computation.3 | async-start | bytes 3145728 | tf_op jit(solution)/shard_map/all_to_all | solution.py:495
  96.6 1.2 copy-start.4
  102.2 20.4 %all-to-all-start.4 = ((bf16[8,1,4,8,128]{4,3,2,1,0:T(8,128)(2,1)}), bf16[8,1,4,8,128]{4,3,2,1,0:T(8,128)(2,1)S(1)}, u32[]{:S(2)}, u32[]{:S(2)}) async-start(bf16[8,1,4,8,128]{4,3,2,1,0:T(8,128)(2,1)} %slab_attention.1), calls=%async_computation.4 | async-start | bytes 131072 | tf_op jit(solution)/shard_map/all_to_all | solution.py:495
  122.7 0.6 copy-start.8
  126.7 9.3 %copy-start.10 = (bf16[256,32]{0,1:T(8,128)(2,1)S(1)}, bf16[256,32]{0,1:T(8,128)(2,1)}, u32[]{:S(2)}) copy-start(bf16[256,32]{0,1:T(8,128)(2,1)} %param.26) | copy-start | bytes 49156
  126.7 37.6 %copy-start = (bf16[256,8,256]{2,1,0:T(8,128)(2,1)S(1)}, bf16[256,8,256]{2,1,0:T(8,128)(2,1)}, u32[]{:S(2)}) copy-start(bf16[256,8,256]{2,1,0:T(8,128)(2,1)} %x_ref.3) | copy-start | bytes 3145732
  126.7 37.6 %copy-start.1 = (bf16[256,256]{1,0:T(8,128)(2,1)S(1)}, bf16[256,256]{1,0:T(8,128)(2,1)}, u32[]{:S(2)}) copy-start(bf16[256,256]{1,0:T(8,128)(2,1)} %out_w_ref.3) | copy-start | bytes 393220
  126.7 37.6 %all-to-all-start.5 = ((bf16[128,2,4,8,128]{4,3,2,1,0:T(8,128)(2,1)}), bf16[128,2,4,8,128]{4,3,2,1,0:T(8,128)(2,1)S(1)}, u32[]{:S(2)}, u32[]{:S(2)}) async-start(bf16[128,2,4,8,128]{4,3,2,1,0:T(8,128)(2,1)} %left_factor.1), calls=%async_computation.5 | async-start | bytes 4194304 | tf_op jit(solution)/shard_map/all_to_all | solution.py:495
  164.3 1.2 copy-start.2
  165.5 0.9 copy-start.3
Sparse Core Ops, SparseCore 0:
  46.1 24.8 all-gather.1

commit v4 on v3

--- a/solution.py
+++ b/solution.py
@@ -13,7 +13,7 @@
 COL = ("xh", "z")
 BOTH = ROW + COL
 BLOCK, UNROLL = 256, 4
-QKV_STEPS, FINISH_STEPS = 2, 1
+QKV_STEPS = 2
 NT = (((1,), (1,)), ((), ()))
 TN = (((0,), (0,)), ((), ()))
 
@@ -166,12 +166,14 @@
     return bias_ref[lax.rem(r, 8), lax.div(r, 8), c, :64, :]
 
 
-def attend(block, blocks, q_ref, k_ref, v_ref, bias_ref, present, out_ref, q_s, k_s, v_s):
+def attend(
+    block, blocks, q_ref, k_ref, v_ref, bias_ref, present, out_ref, q_s, k_s, v_s, which=0
+):
     lane = iota((1, 128), 1) // 32
     wide_lane = (iota((1, 256), 1) // 32) % 4
-    q_s[...] = natural(q_ref[:, 0, 0])
-    k_s[...] = natural(k_ref[:, 0, 0])
-    v_s[:, :128] = natural(v_ref[:, 0, 0])
+    q_s[...] = natural(q_ref[:, 0, which])
+    k_s[...] = natural(k_ref[:, 0, which])
+    v_s[:, :128] = natural(v_ref[:, 0, which])
 
     @pl.when(pl.program_id(0) == 0)
     def _():
@@ -208,12 +210,15 @@
             total = jnp.where(wide_lane == si, parts[si], total)
         result = total[:, :128] / total[:, 128:]
         eighth = block // 8
-        out_ref[pl.ds(pl.multiple_of(at * eighth, eighth), eighth), 0, 0] = result.reshape(
+        out_ref[pl.ds(pl.multiple_of(at * eighth, eighth), eighth), 0, which] = result.reshape(
             eighth, 8, 128
         ).astype(jnp.bfloat16)
         return carry
 
-    lax.fori_loop(0, blocks, step, 0, unroll=min(UNROLL, blocks))
+    if blocks == 1:
+        step(0, 0)
+    else:
+        lax.fori_loop(0, blocks, step, 0, unroll=UNROLL)
 
 
 def first_kernel(
@@ -237,7 +242,9 @@
 
 
 def slab_kernel(at_ref, q_ref, k_ref, v_ref, bias_ref, mask_ref, _, out_ref, *scratch):
-    attend(64, 1, q_ref, k_ref, v_ref, bias_ref, mask_ref[0], out_ref, *scratch)
+    for which in range(2):
+        own = scratch[which * 3 : which * 3 + 3]
+        attend(64, 1, q_ref, k_ref, v_ref, bias_ref, mask_ref[which], out_ref, *own, which)
 
 
 def later_kernel(q_ref, k_ref, v_ref, bias_ref, mask_ref, *rest):
@@ -252,7 +259,7 @@
     ]
 
 
-RETURNED = jax.ShapeDtypeStruct((128, 2, 4, 8, 128), jnp.bfloat16)
+RETURNED = jax.ShapeDtypeStruct((128, 1, 6, 8, 128), jnp.bfloat16)
 SLAB_WEIGHTED = jax.ShapeDtypeStruct((8, 1, 4, 8, 128), jnp.bfloat16)
 
 
@@ -291,22 +298,22 @@
 
 
 def slab_attention(at, received, bias, mask, onto):
-    part = lambda t: pl.BlockSpec((8, 1, 1, 16, 8, 128), lambda g, s: (0, t, g, 0, 0, 0))
+    part = lambda t: pl.BlockSpec((8, 1, 2, 16, 8, 128), lambda g, s: (0, t, 0, 0, 0, 0))
     return pl.pallas_call(
         slab_kernel,
         grid_spec=pltpu.PrefetchScalarGridSpec(
             num_scalar_prefetch=1,
-            grid=(2,),
+            grid=(1,),
             in_specs=[
-                pl.BlockSpec((8, 1, 1, 1, 8, 128), lambda g, s: (0, 0, g, s[0], 0, 0)),
+                pl.BlockSpec((8, 1, 2, 1, 8, 128), lambda g, s: (0, 0, 0, s[0], 0, 0)),
                 part(1),
                 part(2),
                 pl.BlockSpec((1, 1, 8, 64, 128), lambda g, s: (0, 0, 0, 0, 0)),
-                pl.BlockSpec((1, 4, 1024), lambda g, s: (g + 2, 0, 0)),
+                pl.BlockSpec((2, 4, 1024), lambda g, s: (1, 0, 0)),
                 pl.BlockSpec(memory_space=pl.ANY),
             ],
-            out_specs=pl.BlockSpec((8, 1, 1, 8, 128), lambda g, s: (0, 0, g + 2, 0, 0)),
-            scratch_shapes=attention_scratch(64),
+            out_specs=pl.BlockSpec((8, 1, 2, 8, 128), lambda g, s: (0, 0, 1, 0, 0)),
+            scratch_shapes=attention_scratch(64) * 2,
         ),
         out_shape=SLAB_WEIGHTED,
         input_output_aliases={6: 0},
@@ -387,8 +394,9 @@
     left = factor(standardize(fresh).astype(jnp.bfloat16), factor_ref[...], 1)
     left = left * flags_ref[...]
     for half in range(2):
-        part = left[:, half * 128 : (half + 1) * 128].reshape(1, 2, 8, 128).astype(jnp.bfloat16)
-        out_ref[:, 0, 2 * half : 2 * half + 2] = jnp.broadcast_to(part, (128, 2, 8, 128))
+        part = left[:, half * 128 : (half + 1) * 128].reshape(1, 2, 1, 8, 128)
+        part = jnp.broadcast_to(part, (8, 2, 8, 8, 128)).reshape(128, 8, 128)
+        out_ref[:, 0, half] = part.astype(jnp.bfloat16)
 
 
 def left_factor(at, x, weighted, flags, gate, w_out, w_first, onto):
@@ -407,7 +415,7 @@
                 whole(256, 32),
                 pl.BlockSpec(memory_space=pl.ANY),
             ],
-            out_specs=pl.BlockSpec((128, 1, 4, 8, 128), lambda i, s: (0, 1, 0, 0, 0)),
+            out_specs=pl.BlockSpec((128, 1, 2, 8, 128), lambda i, s: (0, 0, 2, 0, 0)),
         ),
         out_shape=RETURNED,
         input_output_aliases={7: 0},
@@ -417,78 +425,95 @@
     )(at, x, weighted, flags, gate, w_out, w_first, onto)
 
 
-def final_kernel(
-    x_ref, weighted_ref, flags_ref, left_ref, gate_ref, out_w_ref, factor_ref, product_ref,
-    fresh_ref, pair_ref, right_s, outer_s, pair_s,
+def fresh_kernel(
+    x_ref, weighted_ref, flags_ref, gate_ref, out_w_ref, factor_ref, fresh_ref, right_ref
 ):
-    step = pl.program_id(0)
-    chains = 256 // FINISH_STEPS
-
-    x = x_ref[...].reshape(chains * 8, 256).astype(jnp.float32)
-    heads = [
-        weighted_ref[:, h, 0].astype(jnp.float32).reshape(chains * 2, 128) for h in range(8)
-    ]
+    x = x_ref[...].reshape(2048, 256).astype(jnp.float32)
+    heads = [weighted_ref[:, h, 0].astype(jnp.float32).reshape(512, 128) for h in range(8)]
     fresh = gated_update(x, gate_ref[...].astype(jnp.float32), heads, out_w_ref[...])
-    fresh_ref[...] = fresh.reshape(chains, 8, 256).astype(jnp.bfloat16)
+    fresh_ref[...] = fresh.reshape(256, 8, 256).astype(jnp.bfloat16)
     right = factor(standardize(fresh).astype(jnp.bfloat16), factor_ref[...], 32)
-    right_s[pl.ds(pl.multiple_of(step * chains, chains), chains), :] = (right * flags_ref[...]).astype(
-        jnp.bfloat16
-    )
-
-    @pl.when(step == pl.num_programs(0) - 1)
-    def _():
-        right_all = right_s[...]
-        for c in range(8):
-            left = left_ref[:, c, 0].astype(jnp.float32)
-            left = jnp.concatenate(
-                [left[:, :2].reshape(256, 128), left[:, 2:].reshape(256, 128)], axis=1
-            ).astype(jnp.bfloat16)
-            outer_s[:, c] = (dot(left, right_all, TN) * (1.0 / 256)).reshape(32, 8, 256)
-        lane = iota((1, 128), 1) // 32
-        for j in range(8):
-            half, source = (j // 4) * 128, j % 4
-            quads = []
-            for quad in range(8):
-                block = None
-                for u in range(4):
-                    part = outer_s[quad * 4 + u, :, :, half : half + 128].reshape(64, 128)
-                    if u != source:
-                        part = pltpu.roll(part, ((u - source) % 4) * 32, 1)
-                    block = part if block is None else jnp.where(lane == u, part, block)
-                quads.append(block.astype(jnp.bfloat16))
-            pair_s[:, j, :] = dot(jnp.concatenate(quads, axis=1), product_ref[...])
-        pair_ref[...] = pair_s[...].astype(jnp.bfloat16)
-
-
-def finish(x, returned, flags, gate, w_out, w_second, w_product):
+    right_ref[...] = (right * flags_ref[...]).astype(jnp.bfloat16)
+
+
+def renew(x, returned, flags, gate, w_out, w_second):
     whole = lambda *shape: pl.BlockSpec(shape, lambda i: (0,) * len(shape))
     return pl.pallas_call(
-        final_kernel,
-        grid=(FINISH_STEPS,),
+        fresh_kernel,
+        grid=(1,),
         in_specs=[
-            pl.BlockSpec((256 // FINISH_STEPS, 8, 256), lambda i: (i, 0, 0)),
-            pl.BlockSpec((16 // FINISH_STEPS, 8, 1, 4, 8, 128), lambda i: (i, 0, 0, 0, 0, 0)),
-            pl.BlockSpec((256 // FINISH_STEPS, 1), lambda i: (i, 0)),
-            pl.BlockSpec((16, 8, 1, 4, 8, 128), lambda i: (0, 0, 1, 0, 0, 0)),
-            pl.BlockSpec((2048 // FINISH_STEPS, 256), lambda i: (i, 0)),
+            whole(256, 8, 256),
+            pl.BlockSpec((16, 8, 1, 4, 8, 128), lambda i: (0, 0, 0, 0, 0, 0)),
+            whole(256, 1),
+            whole(2048, 256),
             whole(256, 256),
             whole(256, 32),
-            whole(1024, 128),
         ],
-        out_specs=[pl.BlockSpec((256 // FINISH_STEPS, 8, 256), lambda i: (i, 0, 0)), whole(64, 8, 128)],
+        out_specs=[whole(256, 8, 256), whole(256, 256)],
         out_shape=[
             jax.ShapeDtypeStruct((256, 8, 256), jnp.bfloat16),
-            jax.ShapeDtypeStruct((64, 8, 128), jnp.bfloat16),
-        ],
-        scratch_shapes=[
-            pltpu.VMEM((256, 256), jnp.bfloat16),
-            pltpu.VMEM((32, 8, 8, 256), jnp.float32),
-            pltpu.VMEM((64, 8, 128), jnp.float32),
+            jax.ShapeDtypeStruct((256, 256), jnp.bfloat16),
         ],
         compiler_params=params(36),
-        cost_estimate=cost(3_000_000_000, 5_000_000),
-        name="finish",
-    )(x, returned, flags, returned, gate, w_out, w_second, w_product)
+        cost_estimate=cost(1_500_000_000, 5_000_000),
+        name="renew",
+    )(x, returned, flags, gate, w_out, w_second)
+
+
+def pair_kernel(at_ref, mine_ref, other_ref, right_ref, product_ref, pair_ref, outer_s, pair_s):
+    own_first = lax.rem(at_ref[1], 2) == 0
+    mine, other = mine_ref[...].astype(jnp.float32), other_ref[...].astype(jnp.float32)
+    halves = (jnp.where(own_first, mine, other), jnp.where(own_first, other, mine))
+    right = right_ref[...].astype(jnp.float32).reshape(16, 2, 8, 256)
+    right = jnp.concatenate([right[:, half].reshape(128, 256) for half in range(2)], axis=0)
+    right = right.astype(jnp.bfloat16)
+    for c in range(8):
+        left = jnp.concatenate(
+            [
+                jnp.concatenate([part[:, c, q].reshape(128, 128) for q in range(2)], axis=1)
+                for part in halves
+            ],
+            axis=0,
+        ).astype(jnp.bfloat16)
+        outer_s[:, c] = (dot(left, right, TN) * (1.0 / 256)).reshape(32, 8, 256)
+    for half in range(2):
+        quads = [[] for _ in range(4)]
+        for quad in range(8):
+            parts = [
+                outer_s[quad * 4 + u, :, :, half * 128 : (half + 1) * 128].reshape(64, 128)
+                for u in range(4)
+            ]
+            for j, part in enumerate(swap_quarters(parts)):
+                quads[j].append(part.astype(jnp.bfloat16))
+        for j in range(4):
+            pair_s[:, half * 4 + j, :] = dot(jnp.concatenate(quads[j], axis=1), product_ref[...])
+    pair_ref[...] = pair_s[...].astype(jnp.bfloat16)
+
+
+def pair_mean(at, mine, other, right, w_product):
+    whole = lambda *shape: pl.BlockSpec(shape, lambda i, s: (0,) * len(shape))
+    return pl.pallas_call(
+        pair_kernel,
+        grid_spec=pltpu.PrefetchScalarGridSpec(
+            num_scalar_prefetch=1,
+            grid=(1,),
+            in_specs=[
+                whole(16, 8, 2, 8, 128),
+                whole(16, 8, 2, 8, 128),
+                whole(256, 256),
+                whole(1024, 128),
+            ],
+            out_specs=whole(64, 8, 128),
+            scratch_shapes=[
+                pltpu.VMEM((32, 8, 8, 256), jnp.float32),
+                pltpu.VMEM((64, 8, 128), jnp.float32),
+            ],
+        ),
+        out_shape=jax.ShapeDtypeStruct((64, 8, 128), jnp.bfloat16),
+        compiler_params=params(36),
+        cost_estimate=cost(500_000_000, 2_000_000),
+        name="pair_mean",
+    )(at, mine, other, right, w_product)
 
 
 def exchange(x, axes):
@@ -547,18 +572,18 @@
         first_factor_matrix,
         returned,
     )
-    returned = exchange(returned, BOTH)
-    return tuple(
-        finish(
-            alignment_tensor,
-            returned.reshape(16, 8, 2, 4, 8, 128),
-            chains,
-            gate,
-            final_projection_matrix,
-            second_factor_matrix,
-            product_to_duo_matrix,
-        )
+    returned = exchange(returned, BOTH).reshape(16, 8, 6, 8, 128)
+    mine = returned[:, :, 4:]
+    other = lax.ppermute(mine, "core", [(0, 1), (1, 0)])
+    fresh, right = renew(
+        alignment_tensor,
+        returned.reshape(16, 8, 1, 6, 8, 128),
+        chains,
+        gate,
+        final_projection_matrix,
+        second_factor_matrix,
     )
+    return fresh, pair_mean(at, mine, other, right, product_to_duo_matrix)
 
 
 def solution(mesh):

time: 179 us -> 177 us (0.989)
  blocking collectives: 0 us -> 32.3 us
  waiting for transfers between devices: 56.8 us -> 28.4 us
  starting transfers between devices: 39.2 us -> 31.8 us
  Pallas kernels: 58.8 us -> 61.2 us
    all_to_all x0 -> x1, blocking collectives: none -> 32.3 us  [exchange(): return lax.all_to_all(x, axes, split_axis=0, concat_axis=0, tiled=True)]
    all_to_all x6 -> x5, waiting for transfers between devices: 56.7 us -> 28.4 us  [exchange(): return lax.all_to_all(x, axes, split_axis=0, concat_axis=0, tiled=True)]
    all_to_all x6 -> x5, starting transfers between devices: 39.1 us -> 30 us  [exchange(): return lax.all_to_all(x, axes, split_axis=0, concat_axis=0, tiled=True)]
    pallas_call x1 -> x2, Pallas kernels: 4.66 us -> 7.69 us  [the longest x1 4.18 us: pair_mean(): pl.pallas_call(pair_kernel, grid_spec=pltpu.PrefetchScalarGridSpec(num_sc...]
    unnamed x31 -> x33, local copies, waits for them, and re-layouts: 6.33 us -> 5.38 us
  transfers between devices with their start and end apart: 7 -> 7, of which waited for: 5 -> 4; matrix products, arithmetic and copies ran while one was open for 2% -> 2% of each run, Pallas kernels for 26% -> 28%
where the time goes in v4:
time: 177 us; the launch traced here: 176 us
  Pallas kernels  61.2 us (35%)
  blocking collectives  32.3 us (18%)
  starting transfers between devices  31.8 us (18%)
  waiting for transfers between devices  28.4 us (16%)
  between operations  14.8 us (8%)
  local copies, waits for them, and re-layouts  6.3 us (4%)
    all_to_all x1, blocking collectives, exchange(): return lax.all_to_all(x, axes, split_axis=0, concat_axis=0, tiled=True)  32.3 us
    all_to_all x5, starting transfers between devices, exchange(): return lax.all_to_all(x, axes, split_axis=0, concat_axis=0, tiled=True)  30 us
    all_to_all x5, waiting for transfers between devices, exchange(): return lax.all_to_all(x, axes, split_axis=0, concat_axis=0, tiled=True)  28.4 us
    pallas_call x1, Pallas kernels, first_attention(): pl.pallas_call(first_kernel, grid_spec=pltpu.PrefetchScalarGridSpec(num_s...  16.3 us
    pallas_call x1, Pallas kernels, later_attention(): pl.pallas_call(later_kernel, grid=(2,), in_specs=[part(0), part(1), part(...  15.3 us
    pallas_call x1, Pallas kernels, qkv(): pl.pallas_call(qkv_kernel, grid=(QKV_STEPS,), in_specs=[pl.BlockSpec((16...  5.58 us
    unnamed x33, local copies, waits for them, and re-layouts  5.38 us
    pallas_call x1, Pallas kernels, bias_tile(): pl.pallas_call(bias_kernel, grid=(5,), in_specs=[pl.BlockSpec((16, 128, 1...  5.31 us
  transfers between devices with their start and end apart: 7, of which 4 were waited for; matrix products, arithmetic and copies ran while one was open for 2% of the time, Pallas kernels for 28%

profile of v4, /device:TPU:1, one launch (start us, length us, event | category | flops | bytes accessed | tf_op | source)
XLA Modules:
  0.0 176.1 jit_solution(16739749546469138586)
XLA Ops:
  7.2 0.0 copy-start.13
  7.2 0.0 copy-start.12
  7.2 7.1 %all-to-all-start = ((bf16[256,8,256]{2,1,0:T(8,128)(2,1)}), bf16[256,8,256]{2,1,0:T(8,128)(2,1)S(1)}, u32[]{:S(2)}, u32[]{:S(2)}) async-start(bf16[256,8,256]{2,1,0:T(8,128)(2,1)} %x_ref.3), calls=%async_computation | async-start | bytes 2097152 | tf_op jit(solution)/shard_map/all_to_all | solution.py:520
  14.2 0.0 copy-done.13
  14.2 0.7 copy.28.w_ref
  15.0 0.0 copy-done.12
  15.0 0.6 convert_bitcast_fusion.flags_ref
  15.6 5.3 %bias_tile.1 = bf16[2,8,80,128]{3,2,1,0:T(8,128)(2,1)} custom-call(bf16[64,128,128]{2,1,0:T(8,128)(2,1)} %duo_ref.1, bf16[128,8]{1,0:T(8,128)(2,1)} %copy.28.w_ref, bf16[16,128]{1,0:T(8,128)(2,1)} %convert_bitcast_fusion.flags_ref), custom_call_target="tpu_custom_call" | custom-call | flops 20000000 | bytes 2200000 | tf_op jit(solution)/shard_map/bias_tile/pallas_call | solution.py:107
  20.9 9.2 %all-to-all-done = bf16[256,8,256]{2,1,0:T(8,128)(2,1)S(1)} async-done(((bf16[256,8,256]{2,1,0:T(8,128)(2,1)}), bf16[256,8,256]{2,1,0:T(8,128)(2,1)S(1)}, u32[]{:S(2)}, u32[]{:S(2)}) %all-to-all-start) | async-done | bytes 1048608 | tf_op jit(solution)/shard_map/all_to_all | solution.py:520
  30.1 0.0 copy-start.6
  30.1 7.3 %all-to-all-start.1 = ((bf16[16,80,128]{2,1,0:T(8,128)(2,1)}), bf16[16,80,128]{2,1,0:T(8,128)(2,1)S(1)}, u32[]{:S(2)}, u32[]{:S(2)}) async-start(bf16[16,80,128]{2,1,0:T(8,128)(2,1)} %bitcast.20), calls=%async_computation.1 | async-start | bytes 655360 | tf_op jit(solution)/shard_map/all_to_all | solution.py:520
  37.4 0.0 all-gather.2.cloned.1.call-start
  37.4 0.0 copy-done.6
  37.4 5.6 %qkv.1 = (bf16[8,3,2,16,8,128]{5,4,3,2,1,0:T(8,128)(2,1)}, bf16[8,3,2,16,8,128]{5,4,3,2,1,0:T(8,128)(2,1)}) custom-call(bf16[16,4,4,8,256]{4,3,2,1,0:T(8,128)(2,1)} %bitcast.17, bf16[256,256]{1,0:T(8,128)(2,1)} %wq_ref.1, bf16[256,256]{1,0:T(8,128)(2,1)} %wk_ref.1, bf16[256,256]{1,0:T(8,128)(2,1)} %wv_ref.1), custom_call_target="tpu_custom_call" | custom-call | flops 800000000 | bytes 4500000 | tf_op jit(solution)/shard_map/qkv/pallas_call | solution.py:141
  43.0 2.2 %all-to-all-done.1 = bf16[16,80,128]{2,1,0:T(8,128)(2,1)S(1)} async-done(((bf16[16,80,128]{2,1,0:T(8,128)(2,1)}), bf16[16,80,128]{2,1,0:T(8,128)(2,1)S(1)}, u32[]{:S(2)}, u32[]{:S(2)}) %all-to-all-start.1) | async-done | bytes 327712 | tf_op jit(solution)/shard_map/all_to_all | solution.py:520
  45.3 0.0 copy-start.8
  45.3 0.8 copy-done.8
  46.0 0.0 all-gather.2.cloned.1.call-update
  46.1 0.0 copy-start.14
  46.1 0.0 copy-start.10
  46.1 4.3 %all-to-all-start.2 = ((bf16[8,3,2,16,8,128]{5,4,3,2,1,0:T(8,128)(2,1)}), bf16[8,3,2,16,8,128]{5,4,3,2,1,0:T(8,128)(2,1)S(1)}, u32[]{:S(2)}, u32[]{:S(2)}) async-start(bf16[8,3,2,16,8,128]{5,4,3,2,1,0:T(8,128)(2,1)} %get-tuple-element.29), calls=%async_computation.2 | async-start | bytes 3145728 | tf_op jit(solution)/shard_map/all_to_all | solution.py:520
  51.1 0.0 copy-done.14
  51.1 0.1 dynamic-slice_bitcast_fusion
  51.2 0.7 copy.29.flags_ref
  51.9 0.0 copy-done.10
  51.9 0.7 copy.30.factor_ref
  52.6 0.7 pad_add_fusion.at_ref
  53.2 4.0 %prepare.1 = (bf16[2048,256]{1,0:T(8,128)(2,1)}, f32[128,256]{1,0:T(8,128)}) custom-call(s32[2]{0:T(128)} %pad_add_fusion.at_ref, bf16[256,8,256]{2,1,0:T(8,128)(2,1)} %x_ref.3, bf16[16,4,4,8,256]{4,3,2,1,0:T(8,128)(2,1)} %bitcast.18, bf16[256,256]{1,0:T(8,128)(2,1)} %gate_ref.1), custom_call_target="tpu_custom_call" | custom-call | flops 300000000 | bytes 3000000 | tf_op jit(solution)/shard_map/prepare/pallas_call | solution.py:361
  57.3 12.7 %all-to-all-done.2.q_ref.k_ref.v_ref = bf16[8,3,2,16,8,128]{5,4,3,2,1,0:T(8,128)(2,1)S(1)} async-done(((bf16[8,3,2,16,8,128]{5,4,3,2,1,0:T(8,128)(2,1)}), bf16[8,3,2,16,8,128]{5,4,3,2,1,0:T(8,128)(2,1)S(1)}, u32[]{:S(2)}, u32[]{:S(2)}) %all-to-all-start.2) | async-done | bytes 1572896 | tf_op jit(solution)/shard_map/all_to_all | solution.py:520
  70.0 0.0 copy-start.7
  70.0 6.2 %all-to-all-start.3 = ((bf16[8,3,2,16,8,128]{5,4,3,2,1,0:T(8,128)(2,1)}), bf16[8,3,2,16,8,128]{5,4,3,2,1,0:T(8,128)(2,1)S(1)}, u32[]{:S(2)}, u32[]{:S(2)}) async-start(bf16[8,3,2,16,8,128]{5,4,3,2,1,0:T(8,128)(2,1)} %get-tuple-element.30), calls=%async_computation.3 | async-start | bytes 3145728 | tf_op jit(solution)/shard_map/all_to_all | solution.py:520
  76.2 0.0 copy-done.7
  76.2 0.0 all-gather.2.cloned.1.call-done.bias_ref.flags_ref
  76.2 16.3 %first_attention.1 = (bf16[128,1,6,8,128]{4,3,2,1,0:T(8,128)(2,1)}, bf16[8,1,4,8,128]{4,3,2,1,0:T(8,128)(2,1)}, bf16[1,1,8,64,128]{4,3,2,1,0:T(8,128)(2,1)}, f32[4,4,1024]{2,1,0:T(4,128)}) custom-call(s32[2]{0:T(128)} %pad_add_fusion.at_ref, bf16[8,3,2,16,8,128]{5,4,3,2,1,0:T(8,128)(2,1)} %copy-done.7, bf16[8,3,2,16,8,128]{5,4,3,2,1,0:T(8,128)(2,1)} %copy-done.7, ...), custom_call_target="tpu_custom_call" | custom-call | flops 16000000000 | bytes 4000000 | tf_op jit(solution)/shard_map/first_attention/pallas_call | solution.py:268
  92.4 4.3 %all-to-all-done.3.q_ref.k_ref.v_ref = bf16[8,3,2,16,8,128]{5,4,3,2,1,0:T(8,128)(2,1)S(1)} async-done(((bf16[8,3,2,16,8,128]{5,4,3,2,1,0:T(8,128)(2,1)}), bf16[8,3,2,16,8,128]{5,4,3,2,1,0:T(8,128)(2,1)S(1)}, u32[]{:S(2)}, u32[]{:S(2)}) %all-to-all-start.3) | async-done | bytes 1572896 | tf_op jit(solution)/shard_map/all_to_all | solution.py:520
  96.7 0.0 copy-start.5
  96.7 1.2 copy-done.5
  97.9 3.8 %slab_attention.1 = bf16[8,1,4,8,128]{4,3,2,1,0:T(8,128)(2,1)} custom-call(s32[2]{0:T(128)} %pad_add_fusion.at_ref, bf16[8,3,2,16,8,128]{5,4,3,2,1,0:T(8,128)(2,1)} %copy-done.5, bf16[8,3,2,16,8,128]{5,4,3,2,1,0:T(8,128)(2,1)} %copy-done.5, bf16[8,3,2,16,8,128]{5,4,3,2,1,0:T(8,128)(2,1)} %copy-done.5, ...), custom_call_target="tpu_custom_call", output_to_operand_aliasing={{}: (6, {})} | custom-call | flops 1000000000 | bytes 2000000 | tf_op jit(solution)/shard_map/slab_attention/pallas_call | solution.py:302
  101.7 5.2 %all-to-all-start.4 = ((bf16[8,1,4,8,128]{4,3,2,1,0:T(8,128)(2,1)}), bf16[8,1,4,8,128]{4,3,2,1,0:T(8,128)(2,1)S(1)}, u32[]{:S(2)}, u32[]{:S(2)}) async-start(bf16[8,1,4,8,128]{4,3,2,1,0:T(8,128)(2,1)} %slab_attention.1), calls=%async_computation.4 | async-start | bytes 131072 | tf_op jit(solution)/shard_map/all_to_all | solution.py:520
  106.9 15.3 %later_attention.1._ = bf16[128,1,6,8,128]{4,3,2,1,0:T(8,128)(2,1)} custom-call(bf16[8,3,2,16,8,128]{5,4,3,2,1,0:T(8,128)(2,1)} %copy-done.5, bf16[8,3,2,16,8,128]{5,4,3,2,1,0:T(8,128)(2,1)} %copy-done.5, bf16[8,3,2,16,8,128]{5,4,3,2,1,0:T(8,128)(2,1)} %copy-done.5, ...), custom_call_target="tpu_custom_call", output_to_operand_aliasing={{}: (5, {})} | custom-call | flops 16000000000 | bytes 4000000 | tf_op jit(solution)/shard_map/later_attention/pallas_call | solution.py:328
  122.1 0.0 all-to-all-done.4.weighted_ref
  122.1 0.0 copy-start.9
  122.1 0.6 copy-done.9
  122.8 3.2 %left_factor.1 = bf16[128,1,6,8,128]{4,3,2,1,0:T(8,128)(2,1)} custom-call(s32[2]{0:T(128)} %pad_add_fusion.at_ref, bf16[16,4,4,8,256]{4,3,2,1,0:T(8,128)(2,1)} %bitcast.19, bf16[8,1,4,8,128]{4,3,2,1,0:T(8,128)(2,1)} %copy-done.9, f32[16,1]{1,0:T(8,128)} %copy.29.flags_ref, f32[128,256]{1,0:T(8,128)} %get-tuple-element.41.gate_ref, ...), custom_call_target="tpu_custom_call", output_to_operand_aliasing={{}: (7, {})} | custom-call | flops 100000000 | bytes 3500000 | tf_op jit(solution)/shard_map/left_factor/pallas_call | solution.py:404
  126.0 0.0 copy-start.11
  126.0 0.0 copy-start
  126.0 0.0 copy-start.1
  126.0 32.3 %all_to_all.30 = bf16[128,1,6,8,128]{4,3,2,1,0:T(8,128)(2,1)S(1)} all-to-all(bf16[128,1,6,8,128]{4,3,2,1,0:T(8,128)(2,1)} %left_factor.1), channel_id=1, replica_groups=mesh['xl'=2,'y'=4,'core'=2,'xh'=2,'z'=4] {'xl','y','core','xh','z'}, dimensions={0} | all-to-all | bytes 3145728 | tf_op jit(solution)/shard_map/all_to_all | solution.py:520
  158.3 1.7 collective-permute-start
  160.0 0.1 copy.31.flags_ref
  160.2 0.0 copy-done.11
  160.2 0.1 copy.32.factor_ref
  160.3 0.0 copy-done
  160.3 0.0 copy-done.1
  160.3 0.0 copy-start.3
  160.3 1.2 copy-done.3
  161.6 0.0 copy-start.2
  161.6 0.0 copy-start.4
  161.6 3.5 %renew.1 = (bf16[256,8,256]{2,1,0:T(8,128)(2,1)}, bf16[256,256]{1,0:T(8,128)(2,1)S(1)}) custom-call(bf16[256,8,256]{2,1,0:T(8,128)(2,1)S(1)} %copy-done, bf16[16,8,1,6,8,128]{5,4,3,2,1,0:T(8,128)(2,1)S(1)} %bitcast.16, f32[256,1]{1,0:T(8,128)S(1)} %copy.31.flags_ref, bf16[2048,256]{1,0:T(8,128)(2,1)S(1)} %copy-done.3, bf16[256,256]{1,0:T(8,128)(2,1)S(1)} %copy-done.1, ...), custom_call_target="tpu_custom_call" | custom-call | flops 1500000000 | bytes 5000000 | tf_op jit(solution)/shard_map/renew/pallas_call | solution.py:441
  165.1 0.0 collective-permute-done.other_ref
  165.1 0.0 copy-done.2
  165.1 0.0 copy-done.4
  165.1 4.2 %pair_mean.1 = bf16[64,8,128]{2,1,0:T(8,128)(2,1)} custom-call(s32[2]{0:T(128)S(1)} %copy-done.2, bf16[16,8,2,8,128]{4,3,2,1,0:T(8,128)(2,1)S(1)} %slice.4.mine_ref, bf16[16,8,2,8,128]{4,3,2,1,0:T(8,128)(2,1)} %collective-permute-done.other_ref, bf16[256,256]{1,0:T(8,128)(2,1)S(1)} %get-tuple-element.45.right_ref, bf16[1024,128]{1,0:T(8,128)(2,1)S(1)} %copy-done.4), custom_call_target="tpu_custom_call" | custom-call | flops 500000000 | bytes 2000000 | tf_op jit(solution)/shard_map/pair_mean/pallas_call | solution.py:495
  (2 shorter events, 0.0 us)
Async XLA Ops:
  7.2 7.1 %copy-start.13 = (bf16[128,8]{0,1:T(8,128)(2,1)S(1)}, bf16[128,8]{0,1:T(8,128)(2,1)}, u32[]{:S(2)}) copy-start(bf16[128,8]{0,1:T(8,128)(2,1)} %param.19) | copy-start | bytes 6148
  7.2 7.8 %copy-start.12 = (s32[256,8]{0,1:T(8,128)S(1)}, s32[256,8]{0,1:T(8,128)}, u32[]{:S(2)}) copy-start(s32[256,8]{0,1:T(8,128)} %param.15) | copy-start | bytes 24580
  7.2 22.9 %all-to-all-start = ((bf16[256,8,256]{2,1,0:T(8,128)(2,1)}), bf16[256,8,256]{2,1,0:T(8,128)(2,1)S(1)}, u32[]{:S(2)}, u32[]{:S(2)}) async-start(bf16[256,8,256]{2,1,0:T(8,128)(2,1)} %x_ref.3), calls=%async_computation | async-start | bytes 2097152 | tf_op jit(solution)/shard_map/all_to_all | solution.py:520
  30.1 7.4 %copy-start.6 = (bf16[256,8,256]{2,1,0:T(8,128)(2,1)}, bf16[256,8,256]{2,1,0:T(8,128)(2,1)S(1)}, u32[]{:S(2)}) copy-start(bf16[256,8,256]{2,1,0:T(8,128)(2,1)S(1)} %all-to-all-done) | copy-start | bytes 3145732
  30.1 15.2 %all-to-all-start.1 = ((bf16[16,80,128]{2,1,0:T(8,128)(2,1)}), bf16[16,80,128]{2,1,0:T(8,128)(2,1)S(1)}, u32[]{:S(2)}, u32[]{:S(2)}) async-start(bf16[16,80,128]{2,1,0:T(8,128)(2,1)} %bitcast.20), calls=%async_computation.1 | async-start | bytes 655360 | tf_op jit(solution)/shard_map/all_to_all | solution.py:520
  37.4 38.8 %all-gather.2.cloned.1.call-start = ((), (), s32[]{:S(2)}) async-start(), calls=%async_computation.6 | async-start | bytes 2949120 | tf_op jit(solution)/shard_map/all_gather | solution.py:550
  45.3 0.8 copy-start.8
  46.1 5.0 %copy-start.14 = (s32[256]{0:T(256)S(1)}, s32[256]{0:T(256)}, u32[]{:S(2)}) copy-start(s32[256]{0:T(256)} %param.16) | copy-start | bytes 3076
  46.1 5.8 %copy-start.10 = (bf16[256,32]{0,1:T(8,128)(2,1)S(1)}, bf16[256,32]{0,1:T(8,128)(2,1)}, u32[]{:S(2)}) copy-start(bf16[256,32]{0,1:T(8,128)(2,1)} %param.25) | copy-start | bytes 49156
  46.1 23.9 %all-to-all-start.2 = ((bf16[8,3,2,16,8,128]{5,4,3,2,1,0:T(8,128)(2,1)}), bf16[8,3,2,16,8,128]{5,4,3,2,1,0:T(8,128)(2,1)S(1)}, u32[]{:S(2)}, u32[]{:S(2)}) async-start(bf16[8,3,2,16,8,128]{5,4,3,2,1,0:T(8,128)(2,1)} %get-tuple-element.29), calls=%async_computation.2 | async-start | bytes 3145728 | tf_op jit(solution)/shard_map/all_to_all | solution.py:520
  70.0 6.2 %copy-start.7 = (bf16[8,3,2,16,8,128]{5,4,3,2,1,0:T(8,128)(2,1)}, bf16[8,3,2,16,8,128]{5,4,3,2,1,0:T(8,128)(2,1)S(1)}, u32[]{:S(2)}) copy-start(bf16[8,3,2,16,8,128]{5,4,3,2,1,0:T(8,128)(2,1)S(1)} %all-to-all-done.2.q_ref.k_ref.v_ref) | copy-start | bytes 4718596
  70.0 26.7 %all-to-all-start.3 = ((bf16[8,3,2,16,8,128]{5,4,3,2,1,0:T(8,128)(2,1)}), bf16[8,3,2,16,8,128]{5,4,3,2,1,0:T(8,128)(2,1)S(1)}, u32[]{:S(2)}, u32[]{:S(2)}) async-start(bf16[8,3,2,16,8,128]{5,4,3,2,1,0:T(8,128)(2,1)} %get-tuple-element.30), calls=%async_computation.3 | async-start | bytes 3145728 | tf_op jit(solution)/shard_map/all_to_all | solution.py:520
  96.7 1.2 copy-start.5
  101.7 20.4 %all-to-all-start.4 = ((bf16[8,1,4,8,128]{4,3,2,1,0:T(8,128)(2,1)}), bf16[8,1,4,8,128]{4,3,2,1,0:T(8,128)(2,1)S(1)}, u32[]{:S(2)}, u32[]{:S(2)}) async-start(bf16[8,1,4,8,128]{4,3,2,1,0:T(8,128)(2,1)} %slab_attention.1), calls=%async_computation.4 | async-start | bytes 131072 | tf_op jit(solution)/shard_map/all_to_all | solution.py:520
  122.1 0.6 copy-start.9
  126.0 34.2 %copy-start.11 = (bf16[256,32]{0,1:T(8,128)(2,1)S(1)}, bf16[256,32]{0,1:T(8,128)(2,1)}, u32[]{:S(2)}) copy-start(bf16[256,32]{0,1:T(8,128)(2,1)} %param.26) | copy-start | bytes 49156
  126.0 34.3 %copy-start = (bf16[256,8,256]{2,1,0:T(8,128)(2,1)S(1)}, bf16[256,8,256]{2,1,0:T(8,128)(2,1)}, u32[]{:S(2)}) copy-start(bf16[256,8,256]{2,1,0:T(8,128)(2,1)} %x_ref.3) | copy-start | bytes 3145732
  126.0 34.3 %copy-start.1 = (bf16[256,256]{1,0:T(8,128)(2,1)S(1)}, bf16[256,256]{1,0:T(8,128)(2,1)}, u32[]{:S(2)}) copy-start(bf16[256,256]{1,0:T(8,128)(2,1)} %out_w_ref.3) | copy-start | bytes 393220
  158.3 6.7 %collective-permute-start = (bf16[16,8,2,8,128]{4,3,2,1,0:T(8,128)(2,1)S(1)}, bf16[16,8,2,8,128]{4,3,2,1,0:T(8,128)(2,1)}, u32[]{:S(2)}, u32[]{:S(2)}) collective-permute-start(bf16[16,8,2,8,128]{4,3,2,1,0:T(8,128)(2,1)S(1)} %slice.4.mine_ref), channel_id=1, source_target_pairs={{0,8},{8,0},{1,9},{9,1},{2,10},{10,2},{3,11},{11,3},{4,12},{12,4},... | collective-permute-start | bytes 1572872 | tf_op jit(solution)/shard_map/ppermute | solution.py:577
  160.3 1.2 copy-start.3
  161.6 3.5 %copy-start.2 = (s32[2]{0:T(128)S(1)}, s32[2]{0:T(128)}, u32[]{:S(2)}) copy-start(s32[2]{0:T(128)} %pad_add_fusion.at_ref) | copy-start | bytes 28
  161.6 3.5 %copy-start.4 = (bf16[1024,128]{1,0:T(8,128)(2,1)S(1)}, bf16[1024,128]{1,0:T(8,128)(2,1)}, u32[]{:S(2)}) copy-start(bf16[1024,128]{1,0:T(8,128)(2,1)} %product_ref.1) | copy-start | bytes 786436
Sparse Core Ops, SparseCore 0:
  46.2 24.8 all-gather.1

commit v5 on v4

--- a/solution.py
+++ b/solution.py
@@ -352,7 +352,8 @@
 
 def prepare_kernel(at_ref, x_ref, slab_ref, gate_ref, gates_ref, slab_gates_ref):
     x = x_ref[...].reshape(2048, 256).astype(jnp.float32)
-    gates_ref[...] = gates(x, gate_ref[...]).astype(jnp.bfloat16)
+    gates_ref[0] = gates(x, gate_ref[...]).astype(jnp.bfloat16)
+    gates_ref[1] = x_ref[...].reshape(2048, 256)
     slab_gates_ref[...] = gates(slab_ref[0].reshape(128, 256).astype(jnp.float32), gate_ref[...])
 
 
@@ -368,10 +369,10 @@
                 pl.BlockSpec((1, 4, 4, 8, 256), lambda i, s: (s[0], 0, 0, 0, 0)),
                 whole(256, 256),
             ],
-            out_specs=[whole(2048, 256), whole(128, 256)],
+            out_specs=[whole(2, 2048, 256), whole(128, 256)],
         ),
         out_shape=[
-            jax.ShapeDtypeStruct((2048, 256), jnp.bfloat16),
+            jax.ShapeDtypeStruct((2, 2048, 256), jnp.bfloat16),
             jax.ShapeDtypeStruct((128, 256), jnp.float32),
         ],
         compiler_params=params(),
@@ -425,27 +426,24 @@
     )(at, x, weighted, flags, gate, w_out, w_first, onto)
 
 
-def fresh_kernel(
-    x_ref, weighted_ref, flags_ref, gate_ref, out_w_ref, factor_ref, fresh_ref, right_ref
-):
-    x = x_ref[...].reshape(2048, 256).astype(jnp.float32)
+def fresh_kernel(own_ref, weighted_ref, flags_ref, out_w_ref, factor_ref, fresh_ref, right_ref):
+    x = own_ref[1].astype(jnp.float32)
     heads = [weighted_ref[:, h, 0].astype(jnp.float32).reshape(512, 128) for h in range(8)]
-    fresh = gated_update(x, gate_ref[...].astype(jnp.float32), heads, out_w_ref[...])
+    fresh = gated_update(x, own_ref[0].astype(jnp.float32), heads, out_w_ref[...])
     fresh_ref[...] = fresh.reshape(256, 8, 256).astype(jnp.bfloat16)
     right = factor(standardize(fresh).astype(jnp.bfloat16), factor_ref[...], 32)
     right_ref[...] = (right * flags_ref[...]).astype(jnp.bfloat16)
 
 
-def renew(x, returned, flags, gate, w_out, w_second):
+def renew(own, returned, flags, w_out, w_second):
     whole = lambda *shape: pl.BlockSpec(shape, lambda i: (0,) * len(shape))
     return pl.pallas_call(
         fresh_kernel,
         grid=(1,),
         in_specs=[
-            whole(256, 8, 256),
+            whole(2, 2048, 256),
             pl.BlockSpec((16, 8, 1, 4, 8, 128), lambda i: (0, 0, 0, 0, 0, 0)),
             whole(256, 1),
-            whole(2048, 256),
             whole(256, 256),
             whole(256, 32),
         ],
@@ -457,7 +455,7 @@
         compiler_params=params(36),
         cost_estimate=cost(1_500_000_000, 5_000_000),
         name="renew",
-    )(x, returned, flags, gate, w_out, w_second)
+    )(own, returned, flags, w_out, w_second)
 
 
 def pair_kernel(at_ref, mine_ref, other_ref, right_ref, product_ref, pair_ref, outer_s, pair_s):
@@ -554,9 +552,9 @@
 
     chains = chain_exists_flags.astype(jnp.float32)[:, None]
     own_chains = lax.dynamic_slice_in_dim(chains, row * 16, 16, 0)
-    gate, slab_gate = prepare(at, alignment_tensor, sequences, sigmoid_matrix)
-
-    early, gate, slab_gate = lax.optimization_barrier((early, gate, slab_gate))
+    own, slab_gate = prepare(at, alignment_tensor, sequences, sigmoid_matrix)
+
+    early, own, slab_gate = lax.optimization_barrier((early, own, slab_gate))
     returned, slab_weighted, slab_bias, mask = first_attention(at, early, bias)
     slab_weighted = slab_attention(at, late, slab_bias, mask, slab_weighted)
     slab_weighted = exchange(slab_weighted, COL)
@@ -576,10 +574,9 @@
     mine = returned[:, :, 4:]
     other = lax.ppermute(mine, "core", [(0, 1), (1, 0)])
     fresh, right = renew(
-        alignment_tensor,
+        own,
         returned.reshape(16, 8, 1, 6, 8, 128),
         chains,
-        gate,
         final_projection_matrix,
         second_factor_matrix,
     )

time: 177 us -> 177 us (level)
    unnamed x33 -> x31, local copies, waits for them, and re-layouts: 5.38 us -> 6.98 us
where the time goes in v5:
time: 177 us
  Pallas kernels  60.4 us (34%)
  blocking collectives  32.3 us (18%)
  starting transfers between devices  31.8 us (18%)
  waiting for transfers between devices  28.3 us (16%)
  between operations  14.8 us (8%)
  local copies, waits for them, and re-layouts  7.9 us (4%)
    all_to_all x1, blocking collectives, exchange(): return lax.all_to_all(x, axes, split_axis=0, concat_axis=0, tiled=True)  32.3 us
    all_to_all x5, starting transfers between devices, exchange(): return lax.all_to_all(x, axes, split_axis=0, concat_axis=0, tiled=True)  30 us
    all_to_all x5, waiting for transfers between devices, exchange(): return lax.all_to_all(x, axes, split_axis=0, concat_axis=0, tiled=True)  28.2 us
    pallas_call x1, Pallas kernels, first_attention(): pl.pallas_call(first_kernel, grid_spec=pltpu.PrefetchScalarGridSpec(num_s...  16.3 us
    pallas_call x1, Pallas kernels, later_attention(): pl.pallas_call(later_kernel, grid=(2,), in_specs=[part(0), part(1), part(...  15.3 us
    unnamed x31, local copies, waits for them, and re-layouts  6.98 us
    pallas_call x1, Pallas kernels, qkv(): pl.pallas_call(qkv_kernel, grid=(QKV_STEPS,), in_specs=[pl.BlockSpec((16...  5.54 us
    pallas_call x1, Pallas kernels, bias_tile(): pl.pallas_call(bias_kernel, grid=(5,), in_specs=[pl.BlockSpec((16, 128, 1...  5.29 us
  transfers between devices with their start and end apart: 7, of which 4 were waited for; matrix products, arithmetic and copies ran while one was open for 2% of the time, Pallas kernels for 28%

profile of v5, /device:TPU:1, one launch (start us, length us, event | category | flops | bytes accessed | tf_op | source)
XLA Modules:
  0.0 176.6 jit_solution(4886259953466249620)
XLA Ops:
  7.2 0.0 copy-start.12
  7.2 0.0 copy-start.11
  7.2 7.1 %all-to-all-start = ((bf16[256,8,256]{2,1,0:T(8,128)(2,1)}), bf16[256,8,256]{2,1,0:T(8,128)(2,1)S(1)}, u32[]{:S(2)}, u32[]{:S(2)}) async-start(bf16[256,8,256]{2,1,0:T(8,128)(2,1)} %x_ref.1), calls=%async_computation | async-start | bytes 2097152 | tf_op jit(solution)/shard_map/all_to_all | solution.py:518
  14.2 0.0 copy-done.12
  14.2 0.7 copy.28.w_ref
  15.0 0.0 copy-done.11
  15.0 0.6 convert_bitcast_fusion.flags_ref
  15.6 5.3 %bias_tile.1 = bf16[2,8,80,128]{3,2,1,0:T(8,128)(2,1)} custom-call(bf16[64,128,128]{2,1,0:T(8,128)(2,1)} %duo_ref.1, bf16[128,8]{1,0:T(8,128)(2,1)} %copy.28.w_ref, bf16[16,128]{1,0:T(8,128)(2,1)} %convert_bitcast_fusion.flags_ref), custom_call_target="tpu_custom_call" | custom-call | flops 20000000 | bytes 2200000 | tf_op jit(solution)/shard_map/bias_tile/pallas_call | solution.py:107
  20.9 9.2 %all-to-all-done = bf16[256,8,256]{2,1,0:T(8,128)(2,1)S(1)} async-done(((bf16[256,8,256]{2,1,0:T(8,128)(2,1)}), bf16[256,8,256]{2,1,0:T(8,128)(2,1)S(1)}, u32[]{:S(2)}, u32[]{:S(2)}) %all-to-all-start) | async-done | bytes 1048608 | tf_op jit(solution)/shard_map/all_to_all | solution.py:518
  30.1 0.0 copy-start.5
  30.1 7.3 %all-to-all-start.1 = ((bf16[16,80,128]{2,1,0:T(8,128)(2,1)}), bf16[16,80,128]{2,1,0:T(8,128)(2,1)S(1)}, u32[]{:S(2)}, u32[]{:S(2)}) async-start(bf16[16,80,128]{2,1,0:T(8,128)(2,1)} %bitcast.20), calls=%async_computation.1 | async-start | bytes 655360 | tf_op jit(solution)/shard_map/all_to_all | solution.py:518
  37.4 0.0 all-gather.2.cloned.1.call-start
  37.4 0.0 copy-done.5
  37.4 5.5 %qkv.1 = (bf16[8,3,2,16,8,128]{5,4,3,2,1,0:T(8,128)(2,1)}, bf16[8,3,2,16,8,128]{5,4,3,2,1,0:T(8,128)(2,1)}) custom-call(bf16[16,4,4,8,256]{4,3,2,1,0:T(8,128)(2,1)} %bitcast.17, bf16[256,256]{1,0:T(8,128)(2,1)} %wq_ref.1, bf16[256,256]{1,0:T(8,128)(2,1)} %wk_ref.1, bf16[256,256]{1,0:T(8,128)(2,1)} %wv_ref.1), custom_call_target="tpu_custom_call" | custom-call | flops 800000000 | bytes 4500000 | tf_op jit(solution)/shard_map/qkv/pallas_call | solution.py:141
  43.0 2.3 %all-to-all-done.1 = bf16[16,80,128]{2,1,0:T(8,128)(2,1)S(1)} async-done(((bf16[16,80,128]{2,1,0:T(8,128)(2,1)}), bf16[16,80,128]{2,1,0:T(8,128)(2,1)S(1)}, u32[]{:S(2)}, u32[]{:S(2)}) %all-to-all-start.1) | async-done | bytes 327712 | tf_op jit(solution)/shard_map/all_to_all | solution.py:518
  45.3 0.0 copy-start.7
  45.3 0.7 copy-done.7
  46.0 0.0 all-gather.2.cloned.1.call-update
  46.0 0.0 copy-start.13
  46.0 0.0 copy-start.9
  46.0 4.3 %all-to-all-start.2 = ((bf16[8,3,2,16,8,128]{5,4,3,2,1,0:T(8,128)(2,1)}), bf16[8,3,2,16,8,128]{5,4,3,2,1,0:T(8,128)(2,1)S(1)}, u32[]{:S(2)}, u32[]{:S(2)}) async-start(bf16[8,3,2,16,8,128]{5,4,3,2,1,0:T(8,128)(2,1)} %get-tuple-element.29), calls=%async_computation.2 | async-start | bytes 3145728 | tf_op jit(solution)/shard_map/all_to_all | solution.py:518
  51.0 0.0 copy-done.13
  51.0 0.1 dynamic-slice_bitcast_fusion
  51.1 0.7 copy.29.flags_ref
  51.8 0.0 copy-done.9
  51.8 0.7 copy.30.factor_ref
  52.5 0.6 pad_add_fusion.at_ref
  53.1 4.4 %prepare.1 = (bf16[2,2048,256]{2,1,0:T(8,128)(2,1)}, f32[128,256]{1,0:T(8,128)}) custom-call(s32[2]{0:T(128)} %pad_add_fusion.at_ref, bf16[256,8,256]{2,1,0:T(8,128)(2,1)} %x_ref.1, bf16[16,4,4,8,256]{4,3,2,1,0:T(8,128)(2,1)} %bitcast.18, bf16[256,256]{1,0:T(8,128)(2,1)} %gate_ref.1), custom_call_target="tpu_custom_call" | custom-call | flops 300000000 | bytes 3000000 | tf_op jit(solution)/shard_map/prepare/pallas_call | solution.py:362
  57.4 12.5 %all-to-all-done.2.q_ref.k_ref.v_ref = bf16[8,3,2,16,8,128]{5,4,3,2,1,0:T(8,128)(2,1)S(1)} async-done(((bf16[8,3,2,16,8,128]{5,4,3,2,1,0:T(8,128)(2,1)}), bf16[8,3,2,16,8,128]{5,4,3,2,1,0:T(8,128)(2,1)S(1)}, u32[]{:S(2)}, u32[]{:S(2)}) %all-to-all-start.2) | async-done | bytes 1572896 | tf_op jit(solution)/shard_map/all_to_all | solution.py:518
  69.9 0.0 copy-start.6
  69.9 1.2 copy-done.6
  71.1 6.2 %all-to-all-start.3 = ((bf16[8,3,2,16,8,128]{5,4,3,2,1,0:T(8,128)(2,1)}), bf16[8,3,2,16,8,128]{5,4,3,2,1,0:T(8,128)(2,1)S(1)}, u32[]{:S(2)}, u32[]{:S(2)}) async-start(bf16[8,3,2,16,8,128]{5,4,3,2,1,0:T(8,128)(2,1)} %get-tuple-element.34), calls=%async_computation.3 | async-start | bytes 3145728 | tf_op jit(solution)/shard_map/all_to_all | solution.py:518
  77.3 0.0 all-gather.2.cloned.1.call-done.bias_ref.flags_ref
  77.3 16.3 %first_attention.1 = (bf16[128,1,6,8,128]{4,3,2,1,0:T(8,128)(2,1)}, bf16[8,1,4,8,128]{4,3,2,1,0:T(8,128)(2,1)}, bf16[1,1,8,64,128]{4,3,2,1,0:T(8,128)(2,1)}, f32[4,4,1024]{2,1,0:T(4,128)}) custom-call(s32[2]{0:T(128)} %pad_add_fusion.at_ref, bf16[8,3,2,16,8,128]{5,4,3,2,1,0:T(8,128)(2,1)} %copy-done.6, bf16[8,3,2,16,8,128]{5,4,3,2,1,0:T(8,128)(2,1)} %copy-done.6, ...), custom_call_target="tpu_custom_call" | custom-call | flops 16000000000 | bytes 4000000 | tf_op jit(solution)/shard_map/first_attention/pallas_call | solution.py:268
  93.6 4.3 %all-to-all-done.3.q_ref.k_ref.v_ref = bf16[8,3,2,16,8,128]{5,4,3,2,1,0:T(8,128)(2,1)S(1)} async-done(((bf16[8,3,2,16,8,128]{5,4,3,2,1,0:T(8,128)(2,1)}), bf16[8,3,2,16,8,128]{5,4,3,2,1,0:T(8,128)(2,1)S(1)}, u32[]{:S(2)}, u32[]{:S(2)}) %all-to-all-start.3) | async-done | bytes 1572896 | tf_op jit(solution)/shard_map/all_to_all | solution.py:518
  97.9 0.0 copy-start.4
  97.9 1.2 copy-done.4
  99.1 3.8 %slab_attention.1 = bf16[8,1,4,8,128]{4,3,2,1,0:T(8,128)(2,1)} custom-call(s32[2]{0:T(128)} %pad_add_fusion.at_ref, bf16[8,3,2,16,8,128]{5,4,3,2,1,0:T(8,128)(2,1)} %copy-done.4, bf16[8,3,2,16,8,128]{5,4,3,2,1,0:T(8,128)(2,1)} %copy-done.4, bf16[8,3,2,16,8,128]{5,4,3,2,1,0:T(8,128)(2,1)} %copy-done.4, ...), custom_call_target="tpu_custom_call", output_to_operand_aliasing={{}: (6, {})} | custom-call | flops 1000000000 | bytes 2000000 | tf_op jit(solution)/shard_map/slab_attention/pallas_call | solution.py:302
  102.9 5.2 %all-to-all-start.4 = ((bf16[8,1,4,8,128]{4,3,2,1,0:T(8,128)(2,1)}), bf16[8,1,4,8,128]{4,3,2,1,0:T(8,128)(2,1)S(1)}, u32[]{:S(2)}, u32[]{:S(2)}) async-start(bf16[8,1,4,8,128]{4,3,2,1,0:T(8,128)(2,1)} %slab_attention.1), calls=%async_computation.4 | async-start | bytes 131072 | tf_op jit(solution)/shard_map/all_to_all | solution.py:518
  108.1 15.3 %later_attention.1._ = bf16[128,1,6,8,128]{4,3,2,1,0:T(8,128)(2,1)} custom-call(bf16[8,3,2,16,8,128]{5,4,3,2,1,0:T(8,128)(2,1)} %copy-done.4, bf16[8,3,2,16,8,128]{5,4,3,2,1,0:T(8,128)(2,1)} %copy-done.4, bf16[8,3,2,16,8,128]{5,4,3,2,1,0:T(8,128)(2,1)} %copy-done.4, ...), custom_call_target="tpu_custom_call", output_to_operand_aliasing={{}: (5, {})} | custom-call | flops 16000000000 | bytes 4000000 | tf_op jit(solution)/shard_map/later_attention/pallas_call | solution.py:328
  123.3 0.0 all-to-all-done.4.weighted_ref
  123.3 0.0 copy-start.8
  123.3 0.6 copy-done.8
  124.0 3.2 %left_factor.1 = bf16[128,1,6,8,128]{4,3,2,1,0:T(8,128)(2,1)} custom-call(s32[2]{0:T(128)} %pad_add_fusion.at_ref, bf16[16,4,4,8,256]{4,3,2,1,0:T(8,128)(2,1)} %bitcast.19, bf16[8,1,4,8,128]{4,3,2,1,0:T(8,128)(2,1)} %copy-done.8, f32[16,1]{1,0:T(8,128)} %copy.29.flags_ref, f32[128,256]{1,0:T(8,128)} %get-tuple-element.42.gate_ref, ...), custom_call_target="tpu_custom_call", output_to_operand_aliasing={{}: (7, {})} | custom-call | flops 100000000 | bytes 3500000 | tf_op jit(solution)/shard_map/left_factor/pallas_call | solution.py:405
  127.2 0.0 copy-start.10
  127.2 0.0 copy-start
  127.2 32.3 %all_to_all.30 = bf16[128,1,6,8,128]{4,3,2,1,0:T(8,128)(2,1)S(1)} all-to-all(bf16[128,1,6,8,128]{4,3,2,1,0:T(8,128)(2,1)} %left_factor.1), channel_id=1, replica_groups=mesh['xl'=2,'y'=4,'core'=2,'xh'=2,'z'=4] {'xl','y','core','xh','z'}, dimensions={0} | all-to-all | bytes 3145728 | tf_op jit(solution)/shard_map/all_to_all | solution.py:518
  159.5 1.7 collective-permute-start
  161.2 0.1 copy.31.flags_ref
  161.3 0.0 copy-done.10
  161.3 0.1 copy.32.factor_ref
  161.4 0.0 copy-done
  161.5 0.0 copy-start.2
  161.5 1.6 copy-done.2
  163.1 0.0 copy-start.1
  163.1 0.0 copy-start.3
  163.1 3.5 %renew.1 = (bf16[256,8,256]{2,1,0:T(8,128)(2,1)}, bf16[256,256]{1,0:T(8,128)(2,1)S(1)}) custom-call(bf16[2,2048,256]{2,1,0:T(8,128)(2,1)S(1)} %copy-done.2, bf16[16,8,1,6,8,128]{5,4,3,2,1,0:T(8,128)(2,1)S(1)} %bitcast.16, f32[256,1]{1,0:T(8,128)S(1)} %copy.31.flags_ref, bf16[256,256]{1,0:T(8,128)(2,1)S(1)} %copy-done, bf16[256,32]{1,0:T(8,128)(2,1)S(1)} %copy.32.factor_ref), custom_call_target="tpu_custom_call" | custom-call | flops 1500000000 | bytes 5000000 | tf_op jit(solution)/shard_map/renew/pallas_call | solution.py:440
  166.6 0.0 collective-permute-done.other_ref
  166.6 0.0 copy-done.1
  166.6 0.0 copy-done.3
  166.6 3.1 %pair_mean.1 = bf16[64,8,128]{2,1,0:T(8,128)(2,1)} custom-call(s32[2]{0:T(128)S(1)} %copy-done.1, bf16[16,8,2,8,128]{4,3,2,1,0:T(8,128)(2,1)S(1)} %slice.4.mine_ref, bf16[16,8,2,8,128]{4,3,2,1,0:T(8,128)(2,1)S(1)} %collective-permute-done.other_ref, bf16[256,256]{1,0:T(8,128)(2,1)S(1)} %get-tuple-element.45.right_ref, bf16[1024,128]{1,0:T(8,128)(2,1)S(1)} %copy-done.3), custom_call_target="tpu_custom_call" | custom-call | flops 500000000 | bytes 2000000 | tf_op jit(solution)/shard_map/pair_mean/pallas_call | solution.py:493
  (2 shorter events, 0.0 us)
Async XLA Ops:
  7.2 7.1 %copy-start.12 = (bf16[128,8]{0,1:T(8,128)(2,1)S(1)}, bf16[128,8]{0,1:T(8,128)(2,1)}, u32[]{:S(2)}) copy-start(bf16[128,8]{0,1:T(8,128)(2,1)} %param.19) | copy-start | bytes 6148
  7.2 7.8 %copy-start.11 = (s32[256,8]{0,1:T(8,128)S(1)}, s32[256,8]{0,1:T(8,128)}, u32[]{:S(2)}) copy-start(s32[256,8]{0,1:T(8,128)} %param.15) | copy-start | bytes 24580
  7.2 22.9 %all-to-all-start = ((bf16[256,8,256]{2,1,0:T(8,128)(2,1)}), bf16[256,8,256]{2,1,0:T(8,128)(2,1)S(1)}, u32[]{:S(2)}, u32[]{:S(2)}) async-start(bf16[256,8,256]{2,1,0:T(8,128)(2,1)} %x_ref.1), calls=%async_computation | async-start | bytes 2097152 | tf_op jit(solution)/shard_map/all_to_all | solution.py:518
  30.1 7.4 %copy-start.5 = (bf16[256,8,256]{2,1,0:T(8,128)(2,1)}, bf16[256,8,256]{2,1,0:T(8,128)(2,1)S(1)}, u32[]{:S(2)}) copy-start(bf16[256,8,256]{2,1,0:T(8,128)(2,1)S(1)} %all-to-all-done) | copy-start | bytes 3145732
  30.1 15.2 %all-to-all-start.1 = ((bf16[16,80,128]{2,1,0:T(8,128)(2,1)}), bf16[16,80,128]{2,1,0:T(8,128)(2,1)S(1)}, u32[]{:S(2)}, u32[]{:S(2)}) async-start(bf16[16,80,128]{2,1,0:T(8,128)(2,1)} %bitcast.20), calls=%async_computation.1 | async-start | bytes 655360 | tf_op jit(solution)/shard_map/all_to_all | solution.py:518
  37.4 39.9 %all-gather.2.cloned.1.call-start = ((), (), s32[]{:S(2)}) async-start(), calls=%async_computation.6 | async-start | bytes 2949120 | tf_op jit(solution)/shard_map/all_gather | solution.py:548
  45.3 0.7 copy-start.7
  46.0 5.0 %copy-start.13 = (s32[256]{0:T(256)S(1)}, s32[256]{0:T(256)}, u32[]{:S(2)}) copy-start(s32[256]{0:T(256)} %param.16) | copy-start | bytes 3076
  46.0 5.7 %copy-start.9 = (bf16[256,32]{0,1:T(8,128)(2,1)S(1)}, bf16[256,32]{0,1:T(8,128)(2,1)}, u32[]{:S(2)}) copy-start(bf16[256,32]{0,1:T(8,128)(2,1)} %param.25) | copy-start | bytes 49156
  46.0 23.9 %all-to-all-start.2 = ((bf16[8,3,2,16,8,128]{5,4,3,2,1,0:T(8,128)(2,1)}), bf16[8,3,2,16,8,128]{5,4,3,2,1,0:T(8,128)(2,1)S(1)}, u32[]{:S(2)}, u32[]{:S(2)}) async-start(bf16[8,3,2,16,8,128]{5,4,3,2,1,0:T(8,128)(2,1)} %get-tuple-element.29), calls=%async_computation.2 | async-start | bytes 3145728 | tf_op jit(solution)/shard_map/all_to_all | solution.py:518
  69.9 1.2 copy-start.6
  71.1 26.7 %all-to-all-start.3 = ((bf16[8,3,2,16,8,128]{5,4,3,2,1,0:T(8,128)(2,1)}), bf16[8,3,2,16,8,128]{5,4,3,2,1,0:T(8,128)(2,1)S(1)}, u32[]{:S(2)}, u32[]{:S(2)}) async-start(bf16[8,3,2,16,8,128]{5,4,3,2,1,0:T(8,128)(2,1)} %get-tuple-element.34), calls=%async_computation.3 | async-start | bytes 3145728 | tf_op jit(solution)/shard_map/all_to_all | solution.py:518
  97.9 1.2 copy-start.4
  102.9 20.5 %all-to-all-start.4 = ((bf16[8,1,4,8,128]{4,3,2,1,0:T(8,128)(2,1)}), bf16[8,1,4,8,128]{4,3,2,1,0:T(8,128)(2,1)S(1)}, u32[]{:S(2)}, u32[]{:S(2)}) async-start(bf16[8,1,4,8,128]{4,3,2,1,0:T(8,128)(2,1)} %slab_attention.1), calls=%async_computation.4 | async-start | bytes 131072 | tf_op jit(solution)/shard_map/all_to_all | solution.py:518
  123.3 0.6 copy-start.8
  127.2 34.2 %copy-start.10 = (bf16[256,32]{0,1:T(8,128)(2,1)S(1)}, bf16[256,32]{0,1:T(8,128)(2,1)}, u32[]{:S(2)}) copy-start(bf16[256,32]{0,1:T(8,128)(2,1)} %param.26) | copy-start | bytes 49156
  127.2 34.3 %copy-start = (bf16[256,256]{1,0:T(8,128)(2,1)S(1)}, bf16[256,256]{1,0:T(8,128)(2,1)}, u32[]{:S(2)}) copy-start(bf16[256,256]{1,0:T(8,128)(2,1)} %out_w_ref.3) | copy-start | bytes 393220
  159.5 7.1 %collective-permute-start = (bf16[16,8,2,8,128]{4,3,2,1,0:T(8,128)(2,1)S(1)}, bf16[16,8,2,8,128]{4,3,2,1,0:T(8,128)(2,1)S(1)}, u32[]{:S(2)}, u32[]{:S(2)}) collective-permute-start(bf16[16,8,2,8,128]{4,3,2,1,0:T(8,128)(2,1)S(1)} %slice.4.mine_ref), channel_id=1, source_target_pairs={{0,8},{8,0},{1,9},{9,1},{2,10},{10,2},{3,11},{11,3},{4,12},{12,4},... | collective-permute-start | bytes 1572872 | tf_op jit(solution)/shard_map/ppermute | solution.py:575
  161.5 1.6 copy-start.2
  163.1 3.5 %copy-start.1 = (s32[2]{0:T(128)S(1)}, s32[2]{0:T(128)}, u32[]{:S(2)}) copy-start(s32[2]{0:T(128)} %pad_add_fusion.at_ref) | copy-start | bytes 28
  163.1 3.5 %copy-start.3 = (bf16[1024,128]{1,0:T(8,128)(2,1)S(1)}, bf16[1024,128]{1,0:T(8,128)(2,1)}, u32[]{:S(2)}) copy-start(bf16[1024,128]{1,0:T(8,128)(2,1)} %product_ref.1) | copy-start | bytes 786436
Sparse Core Ops, SparseCore 0:
  46.1 24.8 all-gather.1
